TPU v7x, 32 devices: a whole 2x2x4 slice. The times are simulated.
32 devices in a mesh: dp: 8 (over z, x), tensor: 4 (over y, core).
Axes of the slice: x: 2, y: 2, z: 4, core: 2. Of those that a mesh axis runs over, the one named last changes fastest.
Arguments:
- tokens: bfloat16 [4096, 768], P(('dp', 'tensor')), may hold values from -6 to 6
- block_count: int32 [32], P('dp'), may hold values from 0 to 128, as said below
- block_first: int32 [32], P('dp'), may hold values from 0 to 1, as said below
- norm1_gain: bfloat16 [768], replicated, may hold values from 0.5 to 1.5
- w_qkv: bfloat16 [768, 3, 768], P('dp', None, 'tensor'), may hold values from -0.3125 to 0.3125
- w_out: bfloat16 [768, 768], P('tensor', 'dp'), may hold values from -0.875 to 0.875
- norm2_gain: bfloat16 [768], replicated, may hold values from 0.5 to 1.5
- w_in: bfloat16 [768, 2, 1152], P('dp', None, 'tensor'), may hold values from -0.21875 to 0.21875
- w_down: bfloat16 [1152, 768], P('tensor', 'dp'), may hold values from -0.375 to 0.375
- cotangent: bfloat16 [4096, 768], P(('dp', 'tensor')), may hold values from -6 to 6
Outputs:
- mixed: bfloat16 [4096, 768], P(('dp', 'tensor'))
- input_grad: bfloat16 [4096, 768], P(('dp', 'tensor'))
- grad_norm1: float32 [768], replicated
- grad_qkv: float32 [768, 3, 768], P('dp', None, 'tensor')
- grad_out: float32 [768, 768], P('tensor', 'dp')
- grad_norm2: float32 [768], replicated
- grad_in: float32 [768, 2, 1152], P('dp', None, 'tensor')
- grad_down: float32 [1152, 768], P('tensor', 'dp')
Inputs may be any that keep to these rules, and one draw needn't show every extreme that they name: `block_count`: A dp index's 4 blocks hold its sequences in order, each starting at a block's start, all its blocks full but the last; the blocks after a dp index's last sequence hold 0; every dp index uses its first block; on some dp index one sequence fills all 512 rows, on another only the first half of the blocks is used. `block_first`: 1 exactly on the first block of each sequence; the first block of every dp index is 1; unused blocks are 0.
All inputs are finite; a program needn't handle non-finite values.
Results may differ from a plain program's by a relative error of at most 0.023.
Values may be sent and summed in bfloat16 or wider, within the bound.
No kernel may reach another device: no remote copies, remote signals or barrier semaphores. Data moves between devices by JAX's collectives and lax.ppermute only.
A program may use at most 64 MiB of HBM per device.

v0:
```python
import jax
import jax.numpy as jnp
from jax import lax
from jax.sharding import PartitionSpec as P

HEAD_DIM = 64
WINDOW = 128


EPS = 1e-05
ROPE_BASE = 10000.0
NEG_FILL = -1e30


def normalize(values, gain):
    center = jnp.mean(values, axis=-1, keepdims=True)
    centred = values - center
    spread = jnp.mean(centred * centred, axis=-1, keepdims=True)
    return centred * lax.rsqrt(spread + EPS) * gain


def layout(count, first):
    blocks = count.shape[0]
    total_rows = blocks * WINDOW
    within = jnp.broadcast_to(jnp.arange(WINDOW, dtype=jnp.int32)[None, :], (blocks, WINDOW))
    usable = (within < count[:, None]).reshape(total_rows)
    seq_blocks = jnp.cumsum(first)
    start_block = lax.cummax(jnp.where(first > 0, jnp.arange(blocks, dtype=jnp.int32), 0), axis=0)
    seq_ids = jnp.broadcast_to(seq_blocks[:, None], (blocks, WINDOW)).reshape(total_rows)
    offsets = jnp.broadcast_to((start_block * WINDOW)[:, None], (blocks, WINDOW)).reshape(
        total_rows
    )
    places = jnp.arange(total_rows, dtype=jnp.int32) - offsets
    return (usable, seq_ids, places)


def rope_tables(places, head_dim):
    freqs = ROPE_BASE ** (-(jnp.arange(head_dim // 2, dtype=jnp.float32) * 2.0) / head_dim)
    angles = places.astype(jnp.float32)[:, None] * freqs[None, :]
    return (jnp.cos(angles)[:, None, :], jnp.sin(angles)[:, None, :])


def rotate(values, cosine, sine):
    middle = values.shape[-1] // 2
    first_half, second_half = (values[..., :middle], values[..., middle:])
    return jnp.concatenate(
        [first_half * cosine - second_half * sine, second_half * cosine + first_half * sine],
        axis=-1,
    )


def window_mask(start, qrows, usable_pad, seq_pad):
    half = WINDOW // 2
    span = qrows + 2 * half
    query_ok = lax.dynamic_slice_in_dim(usable_pad, start + half, qrows, 0)
    query_seq = lax.dynamic_slice_in_dim(seq_pad, start + half, qrows, 0)
    offset = (
        jnp.arange(qrows, dtype=jnp.int32)[:, None]
        + half
        - jnp.arange(span, dtype=jnp.int32)[None, :]
    )
    allowed = (
        (jnp.abs(offset) <= half)
        & (query_seq[:, None] == seq_pad[None, :])
        & query_ok[:, None]
        & usable_pad[None, :]
    )
    return (allowed, query_ok)


def padded_inputs(keys, values, usable, seq_ids):
    half = WINDOW // 2
    keys_pad = jnp.pad(keys, ((half, half), (0, 0), (0, 0)))
    values_pad = jnp.pad(values, ((half, half), (0, 0), (0, 0)))
    usable_pad = jnp.pad(usable, (half, half))
    seq_pad = jnp.pad(seq_ids, (half, half), constant_values=-1)
    return (keys_pad, values_pad, usable_pad, seq_pad)


def add_rows(whole, piece):
    return whole + piece


def attend_forward(query, keys, values, usable, seq_ids, trips):
    total_rows, local_heads, head_dim = query.shape
    qrows = min(512, total_rows)
    scale = head_dim ** (-0.5)
    keys_pad, values_pad, usable_pad, seq_pad = padded_inputs(keys, values, usable, seq_ids)

    def step(index, carry):
        start = index * qrows
        allowed, query_ok = window_mask(start, qrows, usable_pad, seq_pad)
        scores = (
            jnp.einsum("qhd,khd->hqk", query, keys_pad, preferred_element_type=jnp.float32) * scale
        )
        masked = jnp.where(allowed[None], scores, NEG_FILL)
        peak_rows = jnp.max(masked, axis=-1)
        raised = jnp.where(allowed[None], jnp.exp(masked - peak_rows[..., None]), 0.0)
        total_rows_sum = jnp.sum(raised, axis=-1) + (1.0 - query_ok.astype(jnp.float32))[None, :]
        probs = (raised / total_rows_sum[..., None]).astype(jnp.bfloat16)
        mixed_rows = jnp.einsum(
            "hqk,khd->qhd", probs, values_pad, preferred_element_type=jnp.float32
        )
        return (mixed_rows, peak_rows, total_rows_sum)

    start_carry = (
        jnp.zeros((total_rows, local_heads, head_dim), jnp.float32),
        jnp.zeros((local_heads, total_rows), jnp.float32),
        jnp.ones((local_heads, total_rows), jnp.float32),
    )
    return lax.fori_loop(0, trips, step, start_carry)


def attend_backward(query, keys, values, grad_heads, usable, seq_ids, peaks, totals, trips):
    total_rows, local_heads, head_dim = query.shape
    qrows = min(512, total_rows)
    half = WINDOW // 2
    scale = head_dim ** (-0.5)
    keys_pad, values_pad, usable_pad, seq_pad = padded_inputs(keys, values, usable, seq_ids)

    def step(index, carry):
        grad_query, grad_keys, grad_values = carry
        start = index * qrows
        allowed, query_ok = window_mask(start, qrows, usable_pad, seq_pad)
        scores = (
            jnp.einsum("qhd,khd->hqk", query, keys_pad, preferred_element_type=jnp.float32) * scale
        )
        masked = jnp.where(allowed[None], scores, NEG_FILL)
        probs = (
            jnp.where(allowed[None], jnp.exp(masked - peaks[..., None]), 0.0) / totals[..., None]
        )
        grad_probs = jnp.einsum(
            "qhd,khd->hqk", grad_heads, values_pad, preferred_element_type=jnp.float32
        )
        delta = jnp.sum(probs * grad_probs, axis=-1, keepdims=True)
        grad_scores = (probs * (grad_probs - delta)).astype(jnp.bfloat16)
        query_part = (
            jnp.einsum("hqk,khd->qhd", grad_scores, keys_pad, preferred_element_type=jnp.float32)
            * scale
        )
        key_part = (
            jnp.einsum("hqk,qhd->khd", grad_scores, query, preferred_element_type=jnp.float32)
            * scale
        )
        value_part = jnp.einsum(
            "hqk,qhd->khd",
            probs.astype(jnp.bfloat16),
            grad_heads,
            preferred_element_type=jnp.float32,
        )
        grad_query = query_part
        grad_keys = add_rows(grad_keys, key_part)
        grad_values = add_rows(grad_values, value_part)
        return (grad_query, grad_keys, grad_values)

    start_carry = (
        jnp.zeros((total_rows, local_heads, head_dim), jnp.float32),
        jnp.zeros((total_rows + 2 * half, local_heads, head_dim), jnp.float32),
        jnp.zeros((total_rows + 2 * half, local_heads, head_dim), jnp.float32),
    )
    grad_query, grad_keys, grad_values = lax.fori_loop(0, trips, step, start_carry)
    return (grad_query, grad_keys[half : half + total_rows], grad_values[half : half + total_rows])


def gelu_product(gate_pre, up_pre):
    return jax.nn.gelu(gate_pre, approximate=False) * up_pre


def local(
    tokens, block_count, block_first, norm1_gain, w_qkv, w_out, norm2_gain, w_in, w_down, cotangent
):
    model_width = tokens.shape[1]
    usable, seq_ids, places = layout(block_count, block_first)
    total_rows = usable.shape[0]
    head_width = w_qkv.shape[2]
    local_heads = head_width // HEAD_DIM
    unit_width = w_in.shape[2]
    qrows = min(512, total_rows)
    trips = total_rows // qrows
    qkv_full, out_full = (
        lax.all_gather(w_qkv, "dp", axis=0, tiled=True),
        lax.all_gather(w_out, "dp", axis=1, tiled=True),
    )
    gain_one = norm1_gain.astype(jnp.float32)
    gain_two = norm2_gain.astype(jnp.float32)
    inputs = tokens.astype(jnp.float32)
    normed_one = normalize(inputs, gain_one).astype(jnp.bfloat16)
    rows_one = lax.all_gather(normed_one, "tensor", axis=0, tiled=True)
    qkv_flat = qkv_full.reshape(model_width, 3 * head_width)
    raw = jnp.dot(rows_one, qkv_flat, preferred_element_type=jnp.float32).reshape(
        total_rows, 3, local_heads, HEAD_DIM
    )
    cosine, sine = rope_tables(places, HEAD_DIM)
    query = rotate(raw[:, 0], cosine, sine).astype(jnp.bfloat16)
    keys = rotate(raw[:, 1], cosine, sine).astype(jnp.bfloat16)
    values = raw[:, 2].astype(jnp.bfloat16)
    attended, peaks, totals = attend_forward(query, keys, values, usable, seq_ids, trips)
    heads_flat = attended.astype(jnp.bfloat16).reshape(total_rows, head_width)
    branch_one = lax.psum_scatter(
        jnp.dot(heads_flat, out_full, preferred_element_type=jnp.float32).astype(jnp.bfloat16),
        "tensor",
        scatter_dimension=0,
        tiled=True,
    ).astype(jnp.float32)
    residual = inputs + branch_one
    mid_full, down_full = (
        lax.all_gather(w_in, "dp", axis=0, tiled=True),
        lax.all_gather(w_down, "dp", axis=1, tiled=True),
    )
    normed_two = normalize(residual, gain_two).astype(jnp.bfloat16)
    rows_two = lax.all_gather(normed_two, "tensor", axis=0, tiled=True)
    mid_flat = mid_full.reshape(model_width, 2 * unit_width)
    both = jnp.dot(rows_two, mid_flat, preferred_element_type=jnp.float32).reshape(
        total_rows, 2, unit_width
    )
    gate_pre = both[:, 0]
    up_pre = both[:, 1]
    activated = gelu_product(gate_pre, up_pre).astype(jnp.bfloat16)
    branch_two = lax.psum_scatter(
        jnp.dot(activated, down_full, preferred_element_type=jnp.float32).astype(jnp.bfloat16),
        "tensor",
        scatter_dimension=0,
        tiled=True,
    ).astype(jnp.float32)
    mixed = (residual + branch_two).astype(jnp.bfloat16)
    grad_top = cotangent.astype(jnp.float32)
    grad_rows = lax.all_gather(cotangent, "tensor", axis=0, tiled=True)
    grad_act = jnp.dot(grad_rows, down_full.T, preferred_element_type=jnp.float32)
    grad_down = jnp.einsum("rf,rd->fd", activated, grad_rows, preferred_element_type=jnp.float32)
    _, gelu_pull = jax.vjp(gelu_product, gate_pre, up_pre)
    grad_gate, grad_up = gelu_pull(grad_act)
    grad_both = (
        jnp.stack([grad_gate, grad_up], axis=1)
        .astype(jnp.bfloat16)
        .reshape(total_rows, 2 * unit_width)
    )
    grad_normed_two = lax.psum_scatter(
        jnp.dot(grad_both, mid_flat.T, preferred_element_type=jnp.float32).astype(jnp.bfloat16),
        "tensor",
        scatter_dimension=0,
        tiled=True,
    ).astype(jnp.float32)
    grad_in = jnp.einsum(
        "rd,re->de", rows_two, grad_both, preferred_element_type=jnp.float32
    ).reshape(model_width, 2, unit_width)
    _, norm_pull_two = jax.vjp(normalize, residual, gain_two)
    grad_res_norm, grad_gain_two = norm_pull_two(grad_normed_two)
    grad_residual = grad_top + grad_res_norm
    grad_branch = grad_residual.astype(jnp.bfloat16)
    branch_rows = lax.all_gather(grad_branch, "tensor", axis=0, tiled=True)
    grad_heads = jnp.dot(branch_rows, out_full.T, preferred_element_type=jnp.float32).astype(
        jnp.bfloat16
    )
    grad_heads = grad_heads.reshape(total_rows, local_heads, HEAD_DIM)
    grad_out_local = jnp.einsum(
        "rh,rd->hd", heads_flat, branch_rows, preferred_element_type=jnp.float32
    )
    grad_query, grad_keys, grad_values = attend_backward(
        query, keys, values, grad_heads, usable, seq_ids, peaks, totals, trips
    )
    grad_raw = jnp.stack(
        [rotate(grad_query, cosine, -sine), rotate(grad_keys, cosine, -sine), grad_values], axis=1
    )
    grad_raw = grad_raw.astype(jnp.bfloat16).reshape(total_rows, 3 * head_width)
    grad_normed_one = lax.psum_scatter(
        jnp.dot(grad_raw, qkv_flat.T, preferred_element_type=jnp.float32).astype(jnp.bfloat16),
        "tensor",
        scatter_dimension=0,
        tiled=True,
    ).astype(jnp.float32)
    grad_qkv = jnp.einsum(
        "rd,re->de", rows_one, grad_raw, preferred_element_type=jnp.float32
    ).reshape(model_width, 3, head_width)
    _, norm_pull_one = jax.vjp(normalize, inputs, gain_one)
    grad_in_norm, grad_gain_one = norm_pull_one(grad_normed_one)
    input_grad = (grad_residual + grad_in_norm).astype(jnp.bfloat16)
    qkv_summed, out_summed, in_summed, down_summed = (
        lax.psum_scatter(grad_qkv, "dp", scatter_dimension=0, tiled=True),
        lax.psum_scatter(grad_out_local, "dp", scatter_dimension=1, tiled=True),
        lax.psum_scatter(grad_in, "dp", scatter_dimension=0, tiled=True),
        lax.psum_scatter(grad_down, "dp", scatter_dimension=1, tiled=True),
    )
    gain_sum_one, gain_sum_two = lax.psum((grad_gain_one, grad_gain_two), ("dp", "tensor"))
    return (
        mixed,
        input_grad,
        gain_sum_one,
        qkv_summed,
        out_summed,
        gain_sum_two,
        in_summed,
        down_summed,
    )


def solution(mesh):
    return jax.shard_map(
        local,
        mesh=mesh,
        in_specs=(
            P(("dp", "tensor"), None),
            P("dp"),
            P("dp"),
            P(),
            P("dp", None, "tensor"),
            P("tensor", "dp"),
            P(),
            P("dp", None, "tensor"),
            P("tensor", "dp"),
            P(("dp", "tensor"), None),
        ),
        out_specs=(
            P(("dp", "tensor"), None),
            P(("dp", "tensor"), None),
            P(),
            P("dp", None, "tensor"),
            P("tensor", "dp"),
            P(),
            P("dp", None, "tensor"),
            P("tensor", "dp"),
        ),
        check_vma=False,
    )
```

profile of v0, /device:TPU:0, one launch (start us, length us, event | category | flops | bytes accessed | tf_op | source)
XLA Modules:
  0.0 559.8 jit_solution(17782289549849140234)
XLA Ops:
  13.7 10.1 %all_gather.24 = bf16[512,768]{1,0:T(8,128)(2,1)S(1)} all-gather(bf16[128,768]{1,0:T(8,128)(2,1)S(1)} %fusion.53), channel_id=1, replica_groups=mesh['dp'=8,'tensor'=4] {'tensor'}, dimensions={0}, use_global_device_ids=true | all-gather | bytes 983040 | tf_op jit(solution)/shard_map/all_gather | solution.py:188
  23.8 38.0 %all_gather.25 = bf16[768,3,192]{2,1,0:T(4,128)(2,1)S(1)} all-gather(bf16[96,3,192]{2,1,0:T(4,128)(2,1)S(1)} %copy.28), channel_id=1, replica_groups=mesh['dp'=8,'tensor'=4] {'dp'}, dimensions={0}, use_global_device_ids=true | all-gather | bytes 995328 | tf_op jit(solution)/shard_map/all_gather | solution.py:181
  64.8 31.2 %all_gather.26 = bf16[192,768]{0,1:T(8,128)(2,1)S(1)} all-gather(bf16[192,96]{0,1:T(8,128)(2,1)S(1)} %copy.30), channel_id=1, replica_groups=mesh['dp'=8,'tensor'=4] {'dp'}, dimensions={1}, use_global_device_ids=true | all-gather | bytes 331776 | tf_op jit(solution)/shard_map/all_gather | solution.py:182
  97.8 3.8 fusion.95
  101.7 2.9 convolution_convert_fusion.4
  106.3 33.4 %all_gather.28 = bf16[768,2,288]{2,0,1:T(8,128)(2,1)S(1)} all-gather(bf16[96,2,288]{2,0,1:T(8,128)(2,1)S(1)} %copy.31), channel_id=1, replica_groups=mesh['dp'=8,'tensor'=4] {'dp'}, dimensions={0}, use_global_device_ids=true | all-gather | bytes 995328 | tf_op jit(solution)/shard_map/all_gather | solution.py:207
  142.0 31.4 %all_gather.29 = bf16[288,768]{0,1:T(8,128)(2,1)S(1)} all-gather(bf16[288,96]{0,1:T(8,128)(2,1)S(1)} %copy.33), channel_id=1, replica_groups=mesh['dp'=8,'tensor'=4] {'dp'}, dimensions={1}, use_global_device_ids=true | all-gather | bytes 497664 | tf_op jit(solution)/shard_map/all_gather | solution.py:208
  173.4 8.2 %all_gather.30 = bf16[512,768]{1,0:T(8,128)(2,1)S(1)} all-gather(bf16[128,768]{1,0:T(8,128)(2,1)S(1)} %copy-done.14), channel_id=1, replica_groups=mesh['dp'=8,'tensor'=4] {'tensor'}, dimensions={0}, use_global_device_ids=true | all-gather | bytes 983040 | tf_op jit(solution)/shard_map/all_gather | solution.py:227
  186.3 8.9 %all_gather.27 = bf16[512,768]{1,0:T(8,128)(2,1)S(1)} all-gather(bf16[128,768]{1,0:T(8,128)(2,1)S(1)} %multiply_convert_fusion.2), channel_id=1, replica_groups=mesh['dp'=8,'tensor'=4] {'tensor'}, dimensions={0}, use_global_device_ids=true | all-gather | bytes 983040 | tf_op jit(solution)/shard_map/all_gather | solution.py:211
  205.5 2.7 convolution_bitcast_fusion
  208.3 15.2 %reduce-scatter.17.cloned.1.call-done = bf16[128,768]{1,0:T(8,128)(2,1)} async-done(((bf16[512,768]{1,0:T(8,128)(2,1)}), bf16[128,768]{1,0:T(8,128)(2,1)}) %reduce-scatter.17.cloned.1.call-update) | async-done | bytes 196624 | tf_op jit(solution)/shard_map/reduce_scatter | solution.py:237
  225.3 24.0 %reduce-scatter.15.cloned.1.call-done = bf16[128,768]{1,0:T(8,128)(2,1)} async-done(((bf16[512,768]{1,0:T(8,128)(2,1)}), bf16[128,768]{1,0:T(8,128)(2,1)}) %reduce-scatter.15.cloned.1.call-update) | async-done | bytes 196624 | tf_op jit(solution)/shard_map/reduce_scatter | solution.py:219
  251.3 8.3 %all_gather.31 = bf16[512,768]{1,0:T(8,128)(2,1)S(1)} all-gather(bf16[128,768]{1,0:T(8,128)(2,1)S(1)} %fusion.64), channel_id=1, replica_groups=mesh['dp'=8,'tensor'=4] {'tensor'}, dimensions={0}, use_global_device_ids=true | all-gather | bytes 983040 | tf_op jit(solution)/shard_map/all_gather | solution.py:250
  261.5 3.2 multiply_reduce_fusion
  268.1 2.8 convolution_bitcast_fusion.2
  273.0 2.2 fusion.18
  275.3 2.2 fusion.16
  277.6 39.4 %reduce-scatter.27.cloned.1.call-done = f32[96,288]{1,0:T(8,128)} async-done(((f32[768,288]{1,0:T(8,128)}), f32[96,288]{1,0:T(8,128)}) %reduce-scatter.27.cloned.1.call-update) | async-done | bytes 110608
  318.7 63.3 %reduce-scatter.25.cloned.1.call-done = f32[96,192]{1,0:T(8,128)} async-done(((f32[768,192]{1,0:T(8,128)}), f32[96,192]{1,0:T(8,128)}) %reduce-scatter.25.cloned.1.call-update) | async-done | bytes 73744
  383.6 23.1 %reduce-scatter.19.cloned.1.call-done = bf16[128,768]{1,0:T(8,128)(2,1)} async-done(((bf16[512,768]{1,0:T(8,128)(2,1)}), bf16[128,768]{1,0:T(8,128)(2,1)}) %reduce-scatter.19.cloned.1.call-update) | async-done | bytes 196624 | tf_op jit(solution)/shard_map/reduce_scatter | solution.py:265
  409.1 40.9 %all-reduce.4 = (f32[768]{0:T(1024)}, f32[768]{0:T(1024)}) all-reduce(f32[768]{0:T(1024)S(1)} %get-tuple-element.99, f32[768]{0:T(1024)S(1)} %copy-done.40), channel_id=1, replica_groups=mesh['dp'=8,'tensor'=4] {'dp','tensor'}, use_global_device_ids=true, to_apply=%region_18.19 | all-reduce | flops 1536 | bytes 12288 | tf_op jit(solution)/shard_map/psum | solution.py:283
  451.8 28.6 %reduce-scatter.23.cloned.1.call-done = f32[96,2,288]{2,0,1:T(8,128)} async-done(((f32[768,2,288]{2,0,1:T(8,128)}), f32[96,2,288]{2,0,1:T(8,128)}) %reduce-scatter.23.cloned.1.call-update) | async-done | bytes 221200 | tf_op jit(solution)/shard_map/reduce_scatter | solution.py:280
  480.3 1.9 copy.36
  482.2 70.7 %reduce-scatter.21.cloned.1.call-done = f32[96,3,192]{2,0,1:T(8,128)} async-done(((f32[768,3,192]{2,0,1:T(8,128)}), f32[96,3,192]{2,0,1:T(8,128)}) %reduce-scatter.21.cloned.1.call-update) | async-done | bytes 221200 | tf_op jit(solution)/shard_map/reduce_scatter | solution.py:278
  (194 shorter events, 48.6 us)
Async XLA Ops:
  7.2 175.8 %reduce-scatter.13.cloned.1.call-start = ((), (), s32[]{:S(2)}) async-start(), calls=%async_computation.8 | async-start | bytes 983040 | tf_op jit(solution)/shard_map/reduce_scatter | solution.py:199
  10.9 51.8 %copy-start.50 = (f32[128]{0:T(128)}, f32[128]{0:T(128)S(1)}, u32[]{:S(2)}) copy-start(f32[128]{0:T(128)S(1)} %fusion.57) | copy-start | bytes 1540
  10.9 51.8 %copy-start.45 = (f32[128]{0:T(128)}, f32[128]{0:T(128)S(1)}, u32[]{:S(2)}) copy-start(f32[128]{0:T(128)S(1)} %fusion.77) | copy-start | bytes 1540
  104.6 35.1 %copy-start.20 = (bf16[3,64,512]{2,1,0:T(8,128)(2,1)}, bf16[3,64,512]{2,1,0:T(8,128)(2,1)S(1)}, u32[]{:S(2)}) copy-start(bf16[3,64,512]{2,1,0:T(8,128)(2,1)S(1)} %convolution_convert_fusion.4) | copy-start | bytes 589828
  106.1 117.4 %reduce-scatter.17.cloned.1.call-start = ((), (), s32[]{:S(2)}) async-start(), calls=%async_computation.10 | async-start | bytes 983040 | tf_op jit(solution)/shard_map/reduce_scatter | solution.py:237
  106.3 67.1 %copy-start.14 = (bf16[128,768]{1,0:T(8,128)(2,1)S(1)}, bf16[128,768]{1,0:T(8,128)(2,1)}, u32[]{:S(2)}) copy-start(bf16[128,768]{1,0:T(8,128)(2,1)} %param.19) | copy-start | bytes 589828
  142.0 40.9 %copy-start = (bf16[128,768]{1,0:T(8,128)(2,1)S(1)}, bf16[128,768]{1,0:T(8,128)(2,1)}, u32[]{:S(2)}) copy-start(bf16[128,768]{1,0:T(8,128)(2,1)} %param.10) | copy-start | bytes 589828
  201.7 47.6 %reduce-scatter.15.cloned.1.call-start = ((), (), s32[]{:S(2)}) async-start(), calls=%async_computation.9 | async-start | bytes 983040 | tf_op jit(solution)/shard_map/reduce_scatter | solution.py:219
  205.4 18.1 %copy-start.5 = (bf16[128,768]{1,0:T(8,128)(2,1)S(1)}, bf16[128,768]{1,0:T(8,128)(2,1)}, u32[]{:S(2)}) copy-start(bf16[128,768]{1,0:T(8,128)(2,1)} %reduce-scatter.13.cloned.1.call-done) | copy-start | bytes 589828
  205.4 18.1 %copy-start.44 = (f32[128]{0:T(128)S(1)}, f32[128]{0:T(128)}, u32[]{:S(2)}) copy-start(f32[128]{0:T(128)} %copy-done.43) | copy-start | bytes 1540
  205.4 18.1 %copy-start.48 = (f32[128]{0:T(128)S(1)}, f32[128]{0:T(128)}, u32[]{:S(2)}) copy-start(f32[128]{0:T(128)} %copy-done.47) | copy-start | bytes 1540
  205.5 19.8 %copy-start.53 = (f32[128]{0:T(128)S(1)}, f32[128]{0:T(128)}, u32[]{:S(2)}) copy-start(f32[128]{0:T(128)} %copy-done.52) | copy-start | bytes 1540
  205.5 111.5 %reduce-scatter.27.cloned.1.call-start = ((), (), s32[]{:S(2)}) async-start(), calls=%async_computation.15 | async-start | bytes 1327104
  208.2 43.0 %copy-start.15 = (bf16[128,768]{1,0:T(8,128)(2,1)S(1)}, bf16[128,768]{1,0:T(8,128)(2,1)}, u32[]{:S(2)}) copy-start(bf16[128,768]{1,0:T(8,128)(2,1)} %param.19) | copy-start | bytes 589828
  208.2 51.5 %copy-start.12 = (bf16[192,768]{0,1:T(8,128)(2,1)S(1)}, bf16[192,768]{0,1:T(8,128)(2,1)}, u32[]{:S(2)}) copy-start(bf16[192,768]{0,1:T(8,128)(2,1)} %copy-done.11) | copy-start | bytes 884740
  208.3 173.7 %reduce-scatter.25.cloned.1.call-start = ((), (), s32[]{:S(2)}) async-start(), calls=%async_computation.14 | async-start | bytes 884736
  225.3 34.8 %copy-start.21 = (bf16[3,64,512]{2,1,0:T(8,128)(2,1)S(1)}, bf16[3,64,512]{2,1,0:T(8,128)(2,1)}, u32[]{:S(2)}) copy-start(bf16[3,64,512]{2,1,0:T(8,128)(2,1)} %copy-done.20) | copy-start | bytes 589828
  267.1 139.5 %reduce-scatter.19.cloned.1.call-start = ((), (), s32[]{:S(2)}) async-start(), calls=%async_computation.11 | async-start | bytes 983040 | tf_op jit(solution)/shard_map/reduce_scatter | solution.py:265
  272.9 207.4 %reduce-scatter.23.cloned.1.call-start = ((), (), s32[]{:S(2)}) async-start(), calls=%async_computation.13 | async-start | bytes 2654208 | tf_op jit(solution)/shard_map/reduce_scatter | solution.py:280
  275.3 277.7 %reduce-scatter.21.cloned.1.call-start = ((), (), s32[]{:S(2)}) async-start(), calls=%async_computation.12 | async-start | bytes 2654208 | tf_op jit(solution)/shard_map/reduce_scatter | solution.py:278
  277.6 129.1 %copy-start.42 = (f32[128]{0:T(128)S(1)}, f32[128]{0:T(128)}, u32[]{:S(2)}) copy-start(f32[128]{0:T(128)} %copy-done.41) | copy-start | bytes 1540
  277.6 130.2 %copy-start.51 = (f32[128]{0:T(128)S(1)}, f32[128]{0:T(128)}, u32[]{:S(2)}) copy-start(f32[128]{0:T(128)} %copy-done.50) | copy-start | bytes 1540
  277.6 130.3 %copy-start.46 = (f32[128]{0:T(128)S(1)}, f32[128]{0:T(128)}, u32[]{:S(2)}) copy-start(f32[128]{0:T(128)} %copy-done.45) | copy-start | bytes 1540
  277.6 131.5 %copy-start.40 = (f32[768]{0:T(1024)S(1)}, f32[768]{0:T(1024)}, u32[]{:S(2)}) copy-start(f32[768]{0:T(1024)} %get-tuple-element.97) | copy-start | bytes 9220
  (39 other events, 104.3 us)
Sparse Core Ops, SparseCore 0:
  106.2 21.8 reduce-scatter.12
  201.9 21.5 reduce-scatter.16
  226.0 23.2 reduce-scatter.14
  252.9 64.0 reduce-scatter.26
  320.5 61.4 reduce-scatter.24
  384.4 22.2 reduce-scatter.18
  410.6 69.7 reduce-scatter.22
  484.8 68.1 reduce-scatter.20
where the time goes:
time: 561 us; the launch traced here: 560 us
  waiting for transfers between devices  264 us (47%)
  blocking collectives  210 us (37%)
  matrix products  33 us (6%)
  other arithmetic  22.6 us (4%)
  between operations  14.8 us (3%)
  local copies, waits for them, and re-layouts  14.2 us (3%)
    unnamed x10, waiting for transfers between devices  103 us
    reduce_scatter x1, waiting for transfers between devices, local(): lax.psum_scatter(grad_qkv, 'dp', scatter_dimension=0, tiled=True)  70.7 us
    psum x1, blocking collectives, local(): lax.psum((grad_gain_one, grad_gain_two), ('dp', 'tensor'))  40.9 us
    all_gather x1, blocking collectives, local(): lax.all_gather(w_qkv, 'dp', axis=0, tiled=True)  38 us
    all_gather x1, blocking collectives, local(): lax.all_gather(w_in, 'dp', axis=0, tiled=True)  33.4 us
    all_gather x1, blocking collectives, local(): lax.all_gather(w_down, 'dp', axis=1, tiled=True)  31.4 us
    all_gather x1, blocking collectives, local(): lax.all_gather(w_out, 'dp', axis=1, tiled=True)  31.2 us
    reduce_scatter x1, waiting for transfers between devices, local(): lax.psum_scatter(grad_in, 'dp', scatter_dimension=0, tiled=True)  28.6 us
  transfers between devices with their start and end apart: 8, of which 7 were waited for; matrix products, arithmetic and copies ran while one was open for 7% of the time, Pallas kernels for 0%

commit v1 on v0

v1 whole, which is shorter than its diff:
```python
import functools

import jax
import jax.numpy as jnp
import numpy as np
from jax import lax
from jax.experimental import pallas as pl
from jax.experimental.pallas import tpu as pltpu
from jax.sharding import PartitionSpec as P

HEAD_DIM = 64
WINDOW = 128
EPS = 1e-05
ROPE_BASE = 10000.0
NEG_FILL = -1e30
BF = jnp.bfloat16
F32 = jnp.float32

NN = (((1,), (0,)), ((), ()))
NT = (((1,), (1,)), ((), ()))
TN = (((0,), (0,)), ((), ()))


def dot(left, right, dims=NN):
    return lax.dot_general(left, right, dims, preferred_element_type=F32)


def call(kernel, outs, args, scalars=(), scratch=(), flops=0):
    size = sum(int(np.prod(a.shape)) * a.dtype.itemsize for a in list(args) + list(outs))
    return pl.pallas_call(
        kernel,
        out_shape=tuple(outs),
        in_specs=[pl.BlockSpec(memory_space=pltpu.SMEM)] * len(scalars)
        + [pl.BlockSpec(memory_space=pltpu.VMEM)] * len(args),
        out_specs=tuple(pl.BlockSpec(memory_space=pltpu.VMEM) for _ in outs),
        scratch_shapes=list(scratch),
        compiler_params=pltpu.CompilerParams(vmem_limit_bytes=48 * 1024 * 1024),
        cost_estimate=pl.CostEstimate(flops=flops, bytes_accessed=size, transcendentals=0),
    )(*scalars, *args)


def shape(*dims, dtype=BF):
    return jax.ShapeDtypeStruct(dims, dtype)


def rows_of(index, count=WINDOW):
    return pl.ds(pl.multiple_of(index * count, 16), count)


def normed(values):
    center = jnp.mean(values, axis=-1, keepdims=True)
    centred = values - center
    spread = jnp.mean(centred * centred, axis=-1, keepdims=True)
    scale = lax.rsqrt(spread + EPS)
    return centred * scale, scale


def norm_back(grad, gain, unit, scale):
    scaled = grad * gain
    first = jnp.mean(scaled, axis=-1, keepdims=True)
    second = jnp.mean(scaled * unit, axis=-1, keepdims=True)
    return scale * (scaled - first - unit * second)


def swap_halves(values):
    width = values.shape[1]
    lane = lax.broadcasted_iota(jnp.int32, values.shape, 1)
    return jnp.where(
        lane % HEAD_DIM < HEAD_DIM // 2,
        pltpu.roll(values, width - HEAD_DIM // 2, 1),
        pltpu.roll(values, HEAD_DIM // 2, 1),
    )


def head_lanes(shape_of, head):
    lane = lax.broadcasted_iota(jnp.int32, shape_of, 1)
    return (lane >= head * HEAD_DIM) & (lane < (head + 1) * HEAD_DIM)


def prepare_kernel(ids, first, pair, other, gain, freq, n1, cosine, sine):
    gain_row = gain[...].astype(F32)
    for i in range(4):
        source = pair if i < 2 else other
        unit, _ = normed(source[(i % 2) * WINDOW : (i % 2 + 1) * WINDOW, :].astype(F32))
        n1[rows_of(ids[i]), :] = (unit * gain_row).astype(BF)
    start = jnp.int32(0)
    lane = lax.broadcasted_iota(jnp.int32, (WINDOW, 128), 1)
    sign = jnp.where(lane % HEAD_DIM < HEAD_DIM // 2, -1.0, 1.0)
    for b in range(4):
        start = jnp.where(first[b] > 0, b, start)
        place = lax.broadcasted_iota(jnp.int32, (WINDOW, 128), 0) + (b - start) * WINDOW
        angle = place.astype(F32) * freq[...]
        cosine[b * WINDOW : (b + 1) * WINDOW, :] = jnp.cos(angle)
        sine[b * WINDOW : (b + 1) * WINDOW, :] = jnp.sin(angle) * sign


def put_pieces(ids, offsets, pieces, whole, rows):
    if offsets is None:
        whole[...] = pieces[0][...]
        return
    for offset, piece in zip(offsets, pieces):
        whole[rows_of(jnp.bitwise_xor(ids[4], offset), rows), :] = piece[...]


def attend_kernel(offsets, n_pieces, rows, ids, count, first, n1, cosine, sine, *rest):
    pieces = rest[:n_pieces]
    q_out, k_out, v_out, probs_out, att_out, whole = rest[n_pieces : n_pieces + 6]
    k_pad, v_pad = rest[n_pieces + 6 :]
    put_pieces(ids, offsets, pieces, whole, rows)
    half = WINDOW // 2
    width = q_out.shape[1]
    heads = width // HEAD_DIM
    total_rows = q_out.shape[0]
    blocks = total_rows // WINDOW
    for pad in (k_pad, v_pad):
        pad[0:half, :] = jnp.zeros((half, width), BF)
        pad[half + total_rows :, :] = jnp.zeros((half, width), BF)
    for b in range(blocks):
        rows_b = slice(b * WINDOW, (b + 1) * WINDOW)
        raw = dot(n1[rows_b, :], whole[...])
        c = jnp.concatenate([cosine[rows_b, :]] * 3, axis=1)
        s = jnp.concatenate([sine[rows_b, :]] * 3, axis=1)
        qk = raw[:, : 2 * width]
        turned = (qk * c + swap_halves(qk) * s).astype(BF)
        q_out[rows_b, :] = turned[:, :width]
        k_b = turned[:, width:]
        v_b = raw[:, 2 * width :].astype(BF)
        k_out[rows_b, :] = k_b
        v_out[rows_b, :] = v_b
        k_pad[half + b * WINDOW : half + (b + 1) * WINDOW, :] = k_b
        v_pad[half + b * WINDOW : half + (b + 1) * WINDOW, :] = v_b
    span = 2 * WINDOW
    column = lax.broadcasted_iota(jnp.int32, (WINDOW, span), 1)
    row = lax.broadcasted_iota(jnp.int32, (WINDOW, span), 0)
    near = jnp.abs(row + half - column) <= half
    for b in range(blocks):
        rows_b = slice(b * WINDOW, (b + 1) * WINDOW)
        span_b = slice(b * WINDOW, b * WINDOW + span)
        before = jnp.where(first[b] == 0, count[b - 1], 0) if b > 0 else 0
        after = jnp.where(first[b + 1] == 0, count[b + 1], 0) if b + 1 < blocks else 0
        limit = jnp.where(
            column < half,
            before - half,
            jnp.where(column < half + WINDOW, count[b] + half, after + half + WINDOW),
        )
        allowed = near & (column < limit) & (row < count[b])
        spare = (lax.broadcasted_iota(jnp.int32, (WINDOW, 1), 0) >= count[b]).astype(F32)
        q_b = q_out[rows_b, :]
        keys = k_pad[span_b, :]
        values = v_pad[span_b, :]
        mixed = jnp.zeros((WINDOW, width), F32)
        for h in range(heads):
            mine = head_lanes((WINDOW, width), h)
            scores = dot(jnp.where(mine, q_b, 0), keys, NT) * (HEAD_DIM**-0.5)
            masked = jnp.where(allowed, scores, NEG_FILL)
            peak = jnp.max(masked, axis=-1, keepdims=True)
            raised = jnp.where(allowed, jnp.exp(masked - peak), 0.0)
            total = jnp.sum(raised, axis=-1, keepdims=True) + spare
            probs = (raised * (1.0 / total)).astype(BF)
            probs_out[h, rows_b, :] = probs
            mixed = jnp.where(mine, dot(probs, values), mixed)
        att_out[rows_b, :] = mixed.astype(BF)


def collect_kernel(offsets, n_pieces, rows, widths, ids, *rest):
    pieces = rest[:n_pieces]
    in_w, out_w, down_w = rest[n_pieces:]
    units2, heads_w, units = widths
    for j, piece in enumerate(pieces):
        if offsets is None:
            at = slice(None)
        else:
            at = rows_of(jnp.bitwise_xor(ids[4], offsets[j]), rows)
        value = piece[...]
        in_w[at, :] = value[:, :units2]
        out_w[at, :] = value[:, units2 : units2 + heads_w]
        down_w[at, :] = value[:, units2 + heads_w :]


def project_kernel(ids, att, out_w, send, keep):
    for i in range(4):
        part = dot(att[rows_of(ids[i]), :], out_w[...], NT)
        at = slice((i % 2) * WINDOW, (i % 2 + 1) * WINDOW)
        if i < 2:
            keep[at, :] = part
        else:
            send[at, :] = part.astype(BF)


def middle_kernel(own, received, tokens, gain, h_out, n2_out):
    for i in range(2):
        at = slice(i * WINDOW, (i + 1) * WINDOW)
        back = slice((1 - i) * WINDOW, (2 - i) * WINDOW)
        branch = own[at, :].astype(F32) + received[back, :].astype(F32)
        h = tokens[at, :].astype(F32) + branch
        h_out[at, :] = h
        unit, _ = normed(h)
        n2_out[at, :] = (unit * gain[...].astype(F32)).astype(BF)


def units_kernel(n2, n2_far, gz, gz_far, in_w, down_w, send, keep, both_out, act_out):
    units = act_out.shape[1]
    gate_w, up_w = in_w[:, :units], in_w[:, units:]
    for i in (2, 3, 0, 1):
        at = slice((i % 2) * WINDOW, (i % 2 + 1) * WINDOW)
        rows_n = (n2 if i < 2 else n2_far)[at, :]
        rows_g = (gz if i < 2 else gz_far)[at, :]
        gate = dot(rows_n, gate_w)
        up = dot(rows_n, up_w)
        g_act = dot(rows_g, down_w[...])
        phi = 0.5 * (1.0 + lax.erf(gate * np.float32(np.sqrt(0.5))))
        gelu = gate * phi
        slope = phi + gate * (jnp.exp(-0.5 * gate * gate) * np.float32(1.0 / np.sqrt(2.0 * np.pi)))
        act_out[i * WINDOW : (i + 1) * WINDOW, :] = (gelu * up).astype(BF)
        g_both = jnp.concatenate([g_act * up * slope, g_act * gelu], axis=1).astype(BF)
        both_out[i * WINDOW : (i + 1) * WINDOW, :] = g_both
        part = dot(g_both, in_w[...], NT)
        if i < 2:
            keep[at, :] = part
        else:
            send[at, :] = part.astype(BF)


def emit_slots(ids, slots, rows, total, send, keep):
    for k in range(slots):
        near = jnp.bitwise_xor(ids[4], 2 * k)
        far = jnp.bitwise_xor(ids[4], 2 * k + 1)
        send[k] = total[rows_of(far, rows), :].astype(BF)
        keep[k] = total[rows_of(near, rows), :].astype(BF)


def unit_grads_kernel(
    slots, rows, ids, n2, n2_far, gz, gz_far, both, act, down_w, send, keep, b_send, b_keep, total
):
    pair = 2 * WINDOW
    units2 = both.shape[1]
    in_part = dot(n2[...], both[:pair, :], TN) + dot(n2_far[...], both[pair:, :], TN)
    total[:, :units2] = in_part
    down_part = dot(gz[...], act[:pair, :], TN) + dot(gz_far[...], act[pair:, :], TN)
    total[:, units2:] = down_part
    if slots:
        emit_slots(ids, slots, rows, total, send, keep)
    else:
        send[...] = total[...]
        keep[...] = jnp.zeros(keep.shape, BF)
    b_keep[...] = dot(act[:pair, :], down_w[...], NT)
    b_send[...] = dot(act[pair:, :], down_w[...], NT).astype(BF)


def residual_kernel(own, received, h, cot, gain, gh_out, gy_out, gain_out):
    gain_row = gain[...].astype(F32)
    for i in range(2):
        at = slice(i * WINDOW, (i + 1) * WINDOW)
        back = slice((1 - i) * WINDOW, (2 - i) * WINDOW)
        grad = own[at, :].astype(F32) + received[back, :].astype(F32)
        unit, scale = normed(h[at, :])
        gh = cot[at, :].astype(F32) + norm_back(grad, gain_row, unit, scale)
        gy_out[at, :] = gh.astype(BF)
        if i == 0:
            gh_out[...] = gh
            gain_out[...] = jnp.sum(grad * unit, axis=0, keepdims=True)


def attend_back_kernel(
    slots, rows, ids, gy, gy_far, out_w, att, q_in, k_in, v_in, probs_in, cosine, sine, n1, qkv_w, gain,
    g_send, g_keep, send, keep, gain_out,
    gy_all, k_pad, v_pad, gk_pad, gv_pad, gq_all, g_raw, total,
):
    half = WINDOW // 2
    total_rows, width = q_in.shape
    heads = width // HEAD_DIM
    blocks = total_rows // WINDOW
    span = 2 * WINDOW
    for i in range(4):
        source = gy if i < 2 else gy_far
        gy_all[rows_of(ids[i]), :] = source[(i % 2) * WINDOW : (i % 2 + 1) * WINDOW, :]
    for pad, source in ((k_pad, k_in), (v_pad, v_in)):
        pad[0:half, :] = jnp.zeros((half, width), BF)
        pad[half + total_rows :, :] = jnp.zeros((half, width), BF)
        pad[half : half + total_rows, :] = source[...]
    gk_pad[...] = jnp.zeros(gk_pad.shape, F32)
    gv_pad[...] = jnp.zeros(gv_pad.shape, F32)
    for b in range(blocks):
        rows_b = slice(b * WINDOW, (b + 1) * WINDOW)
        span_b = slice(b * WINDOW, b * WINDOW + span)
        g_att = dot(gy_all[rows_b, :], out_w[...]).astype(BF)
        q_b = q_in[rows_b, :]
        keys = k_pad[span_b, :]
        values = v_pad[span_b, :]
        gq = jnp.zeros((WINDOW, width), F32)
        gk = jnp.zeros((span, width), F32)
        gv = jnp.zeros((span, width), F32)
        for h in range(heads):
            mine = head_lanes((WINDOW, width), h)
            g_mine = jnp.where(mine, g_att, 0)
            probs = probs_in[h, rows_b, :]
            wide = probs.astype(F32)
            g_probs = dot(g_mine, values, NT)
            delta = jnp.sum(wide * g_probs, axis=-1, keepdims=True)
            g_scores = (wide * (g_probs - delta)).astype(BF)
            gq = jnp.where(mine, dot(g_scores, keys), gq)
            gk = gk + dot(g_scores, jnp.where(mine, q_b, 0), TN)
            gv = gv + dot(probs, g_mine, TN)
        gq_all[rows_b, :] = gq
        gk_pad[span_b, :] += gk
        gv_pad[span_b, :] += gv
    scale = HEAD_DIM**-0.5
    columns = 3 * width
    for b in range(blocks):
        rows_b = slice(b * WINDOW, (b + 1) * WINDOW)
        inner = slice(half + b * WINDOW, half + (b + 1) * WINDOW)
        c = jnp.concatenate([cosine[rows_b, :]] * 3, axis=1)
        s = jnp.concatenate([sine[rows_b, :]] * 3, axis=1)
        qk = jnp.concatenate([gq_all[rows_b, :], gk_pad[inner, :]], axis=1) * scale
        turned = qk * c - swap_halves(qk) * s
        g_raw[rows_b, : 2 * width] = turned.astype(BF)
        g_raw[rows_b, 2 * width :] = gv_pad[inner, :].astype(BF)
    total[:, :columns] = dot(n1[...], g_raw[...], TN)
    total[:, columns:] = dot(gy_all[...], att[...], TN)
    if slots:
        emit_slots(ids, slots, rows, total, send, keep)
    else:
        send[...] = total[...]
        keep[...] = jnp.zeros(keep.shape, BF)
    gain_sum = jnp.zeros(gain_out.shape, F32)
    for i in range(4):
        at = slice((i % 2) * WINDOW, (i % 2 + 1) * WINDOW)
        g_n1 = dot(g_raw[rows_of(ids[i]), :], qkv_w[...], NT)
        gain_sum += jnp.sum(g_n1 * n1[rows_of(ids[i]), :].astype(F32), axis=0, keepdims=True)
        if i < 2:
            g_keep[at, :] = g_n1
        else:
            g_send[at, :] = g_n1.astype(BF)
    gain_out[...] = gain_sum / gain[...].astype(F32)


def finish_kernel(
    g_keep, g_core, b_keep, b_core, received, h, tokens, gain, gh, mixed_out, grad_out
):
    gain_row = gain[...].astype(F32)
    grad = g_keep[:WINDOW, :] + g_core[:WINDOW, :].astype(F32) + received[:WINDOW, :].astype(F32)
    unit, scale = normed(tokens[:WINDOW, :].astype(F32))
    grad_out[...] = (gh[...] + norm_back(grad, gain_row, unit, scale)).astype(BF)
    branch = b_keep[:WINDOW, :] + b_core[:WINDOW, :].astype(F32) + received[WINDOW:, :].astype(F32)
    mixed_out[...] = (h[:WINDOW, :] + branch).astype(BF)


def swap(values, axis, bit, size):
    return lax.ppermute(values, axis, [(i, i ^ bit) for i in range(size)])


def local(
    tokens, block_count, block_first, norm1_gain, w_qkv, w_out, norm2_gain, w_in, w_down, cotangent
):
    n_dp = lax.axis_size("dp")
    width = tokens.shape[1]
    shard = width // n_dp
    head_width = w_qkv.shape[2]
    units = w_in.shape[2]
    heads = head_width // HEAD_DIM
    total_rows = block_count.shape[0] * WINDOW
    pair_rows = 2 * WINDOW
    slots = n_dp // 2 if shard % 16 == 0 and n_dp % 2 == 0 and n_dp <= 8 else 0
    place = lax.axis_index("tensor").astype(jnp.int32)
    ids = jnp.stack(
        [place, place ^ 2, place ^ 1, place ^ 3, lax.axis_index("dp").astype(jnp.int32)]
    )
    core = functools.partial(swap, axis="tensor", bit=1, size=4)
    across = functools.partial(swap, axis="tensor", bit=2, size=4)
    dp = functools.partial(swap, axis="dp", size=n_dp)

    def gather(value):
        if not slots:
            return (lax.all_gather(value, "dp", axis=0, tiled=True),), None
        near = [value] + [dp(value, bit=2 * k) for k in range(1, slots)]
        far = [dp(piece, bit=1) for piece in near]
        offsets = [2 * k for k in range(slots)] + [2 * k + 1 for k in range(slots)]
        return tuple(near + far), tuple(offsets)

    def reduce(send, keep):
        if not slots:
            return lax.psum_scatter(send, "dp", scatter_dimension=0, tiled=True)
        part = keep.astype(F32) + dp(send, bit=1).astype(F32)
        rounded = part.astype(BF)
        total = part[0]
        for k in range(1, slots):
            total = total + dp(rounded[k], bit=2 * k).astype(F32)
        return total

    def slot_shapes(columns):
        if not slots:
            return (shape(width, columns, dtype=F32), shape(16, 128))
        return (shape(slots, shard, columns), shape(slots, shard, columns))

    gain_one = norm1_gain.reshape(1, width)
    gain_two = norm2_gain.reshape(1, width)
    freqs = ROPE_BASE ** (-(np.arange(HEAD_DIM // 2, dtype=np.float32) * 2.0) / HEAD_DIM)
    freq = jnp.asarray(np.tile(freqs, 128 // (HEAD_DIM // 2))[None, :], F32)

    qkv_pieces, offsets = gather(w_qkv.reshape(shard, 3 * head_width))
    staged = jnp.stack([tokens, cotangent])
    pair = jnp.concatenate([staged, across(staged)], axis=1)
    other = core(pair)
    own_tokens, own_cot = pair[0], pair[1]
    far_tokens, far_cot = other[0], other[1]
    rest_pieces, _ = gather(
        jnp.concatenate([w_in.reshape(shard, 2 * units), w_out.T, w_down.T], axis=1)
    )

    n1, cosine, sine = call(
        prepare_kernel,
        (shape(total_rows, width), shape(total_rows, 128, dtype=F32), shape(total_rows, 128, dtype=F32)),
        (own_tokens, far_tokens, gain_one, freq),
        (ids, block_first),
    )
    flat = shape(total_rows, head_width)
    query, keys, values, probs, attended, qkv_w = call(
        functools.partial(attend_kernel, offsets, len(qkv_pieces), shard),
        (flat, flat, flat, shape(heads, total_rows, 2 * WINDOW), flat, shape(width, 3 * head_width)),
        (n1, cosine, sine) + qkv_pieces,
        (ids, block_count, block_first),
        [pltpu.VMEM((total_rows + WINDOW, head_width), BF)] * 2,
        flops=2 * total_rows * width * 3 * head_width,
    )
    in_w, out_w, down_w = call(
        functools.partial(
            collect_kernel, offsets, len(rest_pieces), shard, (2 * units, head_width, units)
        ),
        (shape(width, 2 * units), shape(width, head_width), shape(width, units)),
        rest_pieces,
        (ids,),
    )
    pair_f32 = shape(pair_rows, width, dtype=F32)
    pair_bf = shape(pair_rows, width)
    a_send, a_keep = call(
        project_kernel, (pair_bf, pair_f32), (attended, out_w), (ids,),
        flops=2 * total_rows * width * head_width,
    )
    a_sum = (a_keep + core(a_send).astype(F32)).astype(BF)
    h, n2 = call(middle_kernel, (pair_f32, pair_bf), (a_sum, across(a_sum), own_tokens, gain_two))
    n2_far = core(n2)
    u_send, u_keep, both, act = call(
        units_kernel,
        (pair_bf, pair_f32, shape(total_rows, 2 * units), shape(total_rows, units)),
        (n2, n2_far, own_cot, far_cot, in_w, down_w),
        flops=2 * total_rows * width * 5 * units,
    )
    u_sum = (u_keep + core(u_send).astype(F32)).astype(BF)
    u_got = across(u_sum)
    s_shapes = slot_shapes(3 * units)
    in_send, in_keep, b_send, b_keep = call(
        functools.partial(unit_grads_kernel, slots, shard),
        s_shapes + (pair_bf, pair_f32),
        (n2, n2_far, own_cot, far_cot, both, act, down_w),
        (ids,),
        [pltpu.VMEM((width, 3 * units), F32)],
        flops=2 * total_rows * width * 4 * units,
    )
    b_core = core(b_send)
    unit_grads = reduce(in_send, in_keep)
    gh, gy, gain_part_two = call(
        residual_kernel,
        (shape(WINDOW, width, dtype=F32), pair_bf, shape(1, width, dtype=F32)),
        (u_sum, u_got, h, own_cot, gain_two),
    )
    gy_far = core(gy)
    g_send, g_keep, att_send, att_keep, gain_part_one = call(
        functools.partial(attend_back_kernel, slots, shard),
        (pair_bf, pair_f32) + slot_shapes(4 * head_width) + (shape(1, width, dtype=F32),),
        (gy, gy_far, out_w, attended, query, keys, values, probs, cosine, sine, n1, qkv_w, gain_one),
        (ids,),
        [
            pltpu.VMEM((total_rows, width), BF),
            pltpu.VMEM((total_rows + WINDOW, head_width), BF),
            pltpu.VMEM((total_rows + WINDOW, head_width), BF),
            pltpu.VMEM((total_rows + WINDOW, head_width), F32),
            pltpu.VMEM((total_rows + WINDOW, head_width), F32),
            pltpu.VMEM((total_rows, head_width), F32),
            pltpu.VMEM((total_rows, 3 * head_width), BF),
            pltpu.VMEM((width, 4 * head_width), F32),
        ],
        flops=2 * total_rows * width * 8 * head_width,
    )
    att_grads = reduce(att_send, att_keep)
    g_core = core(g_send)
    back = jnp.concatenate(
        [
            (g_keep[WINDOW:] + g_core[WINDOW:].astype(F32)).astype(BF),
            (b_keep[WINDOW:] + b_core[WINDOW:].astype(F32)).astype(BF),
        ],
        axis=0,
    )
    mixed, input_grad = call(
        finish_kernel,
        (shape(WINDOW, width), shape(WINDOW, width)),
        (g_keep, g_core, b_keep, b_core, across(back), h, own_tokens, gain_one, gh),
    )
    gains = jnp.concatenate([gain_part_one, gain_part_two], axis=0)
    if slots:
        gains = gains + core(gains)
        gains = gains + across(gains)
        gains = gains + dp(gains, bit=1)
        total = gains
        for k in range(1, slots):
            total = total + dp(gains, bit=2 * k)
        gains = total
    else:
        gains = lax.psum(gains, ("dp", "tensor"))
    columns = 3 * head_width
    return (
        mixed,
        input_grad,
        gains[0],
        att_grads[:, :columns].reshape(shard, 3, head_width),
        att_grads[:, columns:].T,
        gains[1],
        unit_grads[:, : 2 * units].reshape(shard, 2, units),
        unit_grads[:, 2 * units :].T,
    )


def solution(mesh):
    return jax.shard_map(
        local,
        mesh=mesh,
        in_specs=(
            P(("dp", "tensor"), None),
            P("dp"),
            P("dp"),
            P(),
            P("dp", None, "tensor"),
            P("tensor", "dp"),
            P(),
            P("dp", None, "tensor"),
            P("tensor", "dp"),
            P(("dp", "tensor"), None),
        ),
        out_specs=(
            P(("dp", "tensor"), None),
            P(("dp", "tensor"), None),
            P(),
            P("dp", None, "tensor"),
            P("tensor", "dp"),
            P(),
            P("dp", None, "tensor"),
            P("tensor", "dp"),
        ),
        check_vma=False,
    )
```

time: 561 us -> 193 us (0.34)
  blocking collectives: 210 us -> 0 us
  waiting for transfers between devices: 264 us -> 87.7 us
  starting transfers between devices: 0.51 us -> 55.8 us
  matrix products: 33 us -> 0 us
  Pallas kernels: 0 us -> 27.7 us
  other arithmetic: 22.6 us -> 6.34 us
  between operations: 14.8 us -> 1.08 us
    all_gather x8 -> x0, blocking collectives: 169 us -> none  [the longest x1 38 us: local(): lax.all_gather(w_qkv, 'dp', axis=0, tiled=True)]
    reduce_scatter x6 -> x0, waiting for transfers between devices: 162 us -> none  [the longest x1 70.7 us: local(): lax.psum_scatter(grad_qkv, 'dp', scatter_dimension=0, tiled=True)]
    unnamed x10 -> x0, waiting for transfers between devices: 103 us -> none
    ppermute x0 -> x39, waiting for transfers between devices: none -> 87.7 us  [swap(): return lax.ppermute(values, axis, [(i, i ^ bit) for i in range(size)])]
    ppermute x0 -> x39, starting transfers between devices: none -> 55.8 us  [swap(): return lax.ppermute(values, axis, [(i, i ^ bit) for i in range(size)])]
    psum x1 -> x0, blocking collectives: 40.9 us -> none  [local(): lax.psum((grad_gain_one, grad_gain_two), ('dp', 'tensor'))]
    pallas_call x0 -> x10, Pallas kernels: none -> 27.7 us  [call(): pl.pallas_call(kernel, out_shape=tuple(outs), in_specs=[pl.BlockSpec(memo...]
    dot_general x15 -> x0, matrix products: 25.2 us -> none  [the longest x1 3.24 us: step(): jnp.einsum('qhd,khd->hqk', grad_heads, values_pad, preferred_element_type...]
  transfers between devices with their start and end apart: 8 -> 39, of which waited for: 7 -> 24; matrix products, arithmetic and copies ran while one was open for 7% -> 8% of each run, Pallas kernels for 0% -> 8%
where the time goes in v1:
time: 193 us
  waiting for transfers between devices  87.7 us (45%)
  starting transfers between devices  55.8 us (29%)
  Pallas kernels  27.7 us (14%)
  local copies, waits for them, and re-layouts  14 us (7%)
  other arithmetic  6.34 us (3%)
    ppermute x39, waiting for transfers between devices, swap(): return lax.ppermute(values, axis, [(i, i ^ bit) for i in range(size)])  87.7 us
    ppermute x39, starting transfers between devices, swap(): return lax.ppermute(values, axis, [(i, i ^ bit) for i in range(size)])  55.8 us
    pallas_call x10, Pallas kernels, call(): pl.pallas_call(kernel, out_shape=tuple(outs), in_specs=[pl.BlockSpec(memo...  27.7 us
    unnamed x38, local copies, waits for them, and re-layouts  7.27 us
  transfers between devices with their start and end apart: 39, of which 24 were waited for; matrix products, arithmetic and copies ran while one was open for 8% of the time, Pallas kernels for 8%

profile of v1, /device:TPU:0, one launch (start us, length us, event | category | flops | bytes accessed | tf_op | source)
XLA Modules:
  0.0 192.7 jit_solution(8860044644279870964)
XLA Ops:
  1.8 3.0 %collective-permute-start = (bf16[2,128,768]{2,1,0:T(8,128)(2,1)S(1)}, bf16[2,128,768]{2,1,0:T(8,128)(2,1)S(1)}, u32[]{:S(2)}, u32[]{:S(2)}) collective-permute-start(bf16[2,128,768]{2,1,0:T(8,128)(2,1)S(1)} %pad_maximum_fusion.1), channel_id=1, source_target_pairs={{0,2},{1,3},{2,0},{3,1},{4,6},{5,7},{6,4},{7,5},{8,10},{9,11},{10,... | collective-permute-start | bytes 1179656 | tf_op jit(solution)/shard_map/ppermute | solution.py:349
  4.8 9.1 %collective-permute-done = bf16[2,128,768]{2,1,0:T(8,128)(2,1)S(1)} collective-permute-done((bf16[2,128,768]{2,1,0:T(8,128)(2,1)S(1)}, bf16[2,128,768]{2,1,0:T(8,128)(2,1)S(1)}, u32[]{:S(2)}, u32[]{:S(2)}) %collective-permute-start) | collective-permute-done | bytes 393248 | tf_op jit(solution)/shard_map/ppermute | solution.py:349
  15.4 3.9 %collective-permute-start.4 = (bf16[96,576]{1,0:T(8,128)(2,1)S(1)}, bf16[96,576]{1,0:T(8,128)(2,1)S(1)}, u32[]{:S(2)}, u32[]{:S(2)}) collective-permute-start(bf16[96,576]{1,0:T(8,128)(2,1)S(1)} %copy.30.rest_0_), channel_id=1, source_target_pairs={{0,24},{4,28},{8,16},{12,20},{16,8},{20,12},{24,0},{28,4},{1,25},{... | collective-permute-start | bytes 331784 | tf_op jit(solution)/shard_map/ppermute | solution.py:349
  23.6 14.6 %collective-permute-start.9 = (bf16[96,1056]{1,0:T(8,128)(2,1)S(1)}, bf16[96,1056]{1,0:T(8,128)(2,1)S(1)}, u32[]{:S(2)}, u32[]{:S(2)}) collective-permute-start(bf16[96,1056]{1,0:T(8,128)(2,1)S(1)} %concatenate.13.rest_0_), channel_id=1, source_target_pairs={{0,8},{4,12},{8,0},{12,4},{16,24},{20,28},{24,16},{28,20},{1,9},{5... | collective-permute-start | bytes 608264 | tf_op jit(solution)/shard_map/ppermute | solution.py:349
  40.3 11.6 %collective-permute-done.2.rest_1_ = bf16[96,576]{1,0:T(8,128)(2,1)S(1)} collective-permute-done((bf16[96,576]{1,0:T(8,128)(2,1)S(1)}, bf16[96,576]{1,0:T(8,128)(2,1)S(1)}, u32[]{:S(2)}, u32[]{:S(2)}) %collective-permute-start.2) | collective-permute-done | bytes 110624 | tf_op jit(solution)/shard_map/ppermute | solution.py:349
  56.1 4.1 %collective-permute-done.12.rest_4_ = bf16[96,1056]{1,0:T(8,128)(2,1)S(1)} collective-permute-done((bf16[96,1056]{1,0:T(8,128)(2,1)S(1)}, bf16[96,1056]{1,0:T(8,128)(2,1)S(1)}, u32[]{:S(2)}, u32[]{:S(2)}) %collective-permute-start.12) | collective-permute-done | bytes 202784 | tf_op jit(solution)/shard_map/ppermute | solution.py:349
  61.7 3.2 %collective-permute-done.15.rest_7_ = bf16[96,1056]{1,0:T(8,128)(2,1)S(1)} collective-permute-done((bf16[96,1056]{1,0:T(8,128)(2,1)S(1)}, bf16[96,1056]{1,0:T(8,128)(2,1)S(1)}, u32[]{:S(2)}, u32[]{:S(2)}) %collective-permute-start.15) | collective-permute-done | bytes 202784 | tf_op jit(solution)/shard_map/ppermute | solution.py:349
  66.5 3.2 %collective-permute-done.14.rest_6_ = bf16[96,1056]{1,0:T(8,128)(2,1)S(1)} collective-permute-done((bf16[96,1056]{1,0:T(8,128)(2,1)S(1)}, bf16[96,1056]{1,0:T(8,128)(2,1)S(1)}, u32[]{:S(2)}, u32[]{:S(2)}) %collective-permute-start.14) | collective-permute-done | bytes 202784 | tf_op jit(solution)/shard_map/ppermute | solution.py:349
  71.2 3.2 %collective-permute-done.13.rest_5_ = bf16[96,1056]{1,0:T(8,128)(2,1)S(1)} collective-permute-done((bf16[96,1056]{1,0:T(8,128)(2,1)S(1)}, bf16[96,1056]{1,0:T(8,128)(2,1)S(1)}, u32[]{:S(2)}, u32[]{:S(2)}) %collective-permute-start.13) | collective-permute-done | bytes 202784 | tf_op jit(solution)/shard_map/ppermute | solution.py:349
  80.0 2.4 %collective-permute-done.7.rest_6_ = bf16[96,576]{1,0:T(8,128)(2,1)S(1)} collective-permute-done((bf16[96,576]{1,0:T(8,128)(2,1)S(1)}, bf16[96,576]{1,0:T(8,128)(2,1)S(1)}, u32[]{:S(2)}, u32[]{:S(2)}) %collective-permute-start.7) | collective-permute-done | bytes 110624 | tf_op jit(solution)/shard_map/ppermute | solution.py:349
  84.0 6.1 %shard_map.171 = (bf16[512,192]{1,0:T(8,128)(2,1)S(1)}, bf16[512,192]{1,0:T(8,128)(2,1)S(1)}, bf16[512,192]{1,0:T(8,128)(2,1)S(1)}, bf16[3,512,256]{2,1,0:T(8,12...) custom-call(s32[5]{0:T(128)S(1)} %stack.32.ids, s32[4]{0:T(128)S(1)} %copy-done.6, ...), custom_call_target="tpu_custom_call" | custom-call | flops 452984832 | bytes 4653056 | tf_op jit(solution)/shard_map/pallas_call | solution.py:30
  95.8 9.6 %collective-permute-done.17.received = bf16[256,768]{1,0:T(8,128)(2,1)S(1)} collective-permute-done((bf16[256,768]{1,0:T(8,128)(2,1)S(1)}, bf16[256,768]{1,0:T(8,128)(2,1)S(1)}, u32[]{:S(2)}, u32[]{:S(2)}) %collective-permute-start.17) | collective-permute-done | bytes 393248 | tf_op jit(solution)/shard_map/ppermute | solution.py:349
  107.6 3.0 %shard_map.175 = (bf16[256,768]{1,0:T(8,128)(2,1)S(1)}, f32[256,768]{1,0:T(8,128)S(1)}, bf16[512,576]{1,0:T(8,128)(2,1)S(1)}, bf16[512,288]{1,0:T(8,128)(2,1)S(1)}) custom-call(bf16[256,768]{1,0:T(8,128)(2,1)S(1)} %get-tuple-element.49.n2, bf16[256,768]{1,0:T(8,128)(2,1)S(1)} %collective-permute-done.18.n2_far, ...), custom_call_target="tpu_custom_call" | custom-call | flops 1132462080 | bytes 4964352 | tf_op jit(solution)/shard_map/pallas_call | solution.py:30
  114.1 2.5 %shard_map.178 = (bf16[4,96,864]{2,1,0:T(8,128)(2,1)S(1)}, bf16[4,96,864]{2,1,0:T(8,128)(2,1)S(1)}, bf16[256,768]{1,0:T(8,128)(2,1)S(1)}, f32[256,768]{1,0:T(8,128)S(1)}) custom-call(s32[5]{0:T(128)S(1)} %stack.32.ids, bf16[256,768]{1,0:T(8,128)(2,1)S(1)} %get-tuple-element.49.n2, bf16[256,768]{1,0:T(8,128)(2,1)S(1)} %collective-permute-done.18.n2_far, ...), custom_call_target="tpu_custom_call" | custom-call | flops 905969664 | bytes 5406720 | tf_op jit(solution)/shard_map/pallas_call | solution.py:30
  118.2 5.5 %collective-permute-done.20.received = bf16[256,768]{1,0:T(8,128)(2,1)S(1)} collective-permute-done((bf16[256,768]{1,0:T(8,128)(2,1)S(1)}, bf16[256,768]{1,0:T(8,128)(2,1)S(1)}, u32[]{:S(2)}, u32[]{:S(2)}) %collective-permute-start.20) | collective-permute-done | bytes 393248 | tf_op jit(solution)/shard_map/ppermute | solution.py:349
  126.1 9.0 %shard_map.177 = (bf16[256,768]{1,0:T(8,128)(2,1)S(1)}, f32[256,768]{1,0:T(8,128)S(1)}, bf16[4,96,768]{2,1,0:T(8,128)(2,1)}, bf16[4,96,768]{2,1,0:T(8,128)(2,1)S(1)}, f32[1,768]{1,0:T(1,128)S(1)}) custom-call(s32[5]{0:T(128)S(1)} %stack.32.ids, bf16[256,768]{1,0:T(8,128)(2,1)S(1)} %get-tuple-element.55.gy, ...), custom_call_target="tpu_custom_call" | custom-call | flops 1207959552 | bytes 7213568 | tf_op jit(solution)/shard_map/pallas_call | solution.py:30
  138.1 2.5 %collective-permute-start.38 = (bf16[96,864]{1,0:T(8,128)(2,1)S(1)}, bf16[96,864]{1,0:T(8,128)(2,1)S(1)}, u32[]{:S(2)}, u32[]{:S(2)}) collective-permute-start(bf16[96,864]{1,0:T(8,128)(2,1)S(1)} %get-tuple-element.103), channel_id=1, source_target_pairs={{0,24},{4,28},{8,16},{12,20},{16,8},{20,12},{24,0},{28,4},{1,25},{... | collective-permute-start | bytes 497672 | tf_op jit(solution)/shard_map/ppermute | solution.py:349
  144.7 4.8 %collective-permute-done.38 = bf16[96,864]{1,0:T(8,128)(2,1)S(1)} collective-permute-done((bf16[96,864]{1,0:T(8,128)(2,1)S(1)}, bf16[96,864]{1,0:T(8,128)(2,1)S(1)}, u32[]{:S(2)}, u32[]{:S(2)}) %collective-permute-start.38) | collective-permute-done | bytes 165920 | tf_op jit(solution)/shard_map/ppermute | solution.py:349
  149.6 6.9 %collective-permute-done.37 = bf16[96,864]{1,0:T(8,128)(2,1)S(1)} collective-permute-done((bf16[96,864]{1,0:T(8,128)(2,1)S(1)}, bf16[96,864]{1,0:T(8,128)(2,1)S(1)}, u32[]{:S(2)}, u32[]{:S(2)}) %collective-permute-start.37) | collective-permute-done | bytes 165920 | tf_op jit(solution)/shard_map/ppermute | solution.py:349
  156.6 2.5 %collective-permute-start.30 = (f32[2,768]{1,0:T(2,128)S(1)}, f32[2,768]{1,0:T(2,128)}, u32[]{:S(2)}, u32[]{:S(2)}) collective-permute-start(f32[2,768]{1,0:T(2,128)S(1)} %add.60), channel_id=1, source_target_pairs={{0,24},{4,28},{8,16},{12,20},{16,8},{20,12},{24,0},{28,4},{1,25},{... | collective-permute-start | bytes 18440 | tf_op jit(solution)/shard_map/ppermute | solution.py:349
  167.7 2.5 %collective-permute-start.34 = (bf16[96,768]{1,0:T(8,128)(2,1)S(1)}, bf16[96,768]{1,0:T(8,128)(2,1)S(1)}, u32[]{:S(2)}, u32[]{:S(2)}) collective-permute-start(bf16[96,768]{1,0:T(8,128)(2,1)S(1)} %get-tuple-element.106), channel_id=1, source_target_pairs={{0,24},{4,28},{8,16},{12,20},{16,8},{20,12},{24,0},{28,4},{1,25},{... | collective-permute-start | bytes 442376 | tf_op jit(solution)/shard_map/ppermute | solution.py:349
  173.6 3.9 %collective-permute-done.34 = bf16[96,768]{1,0:T(8,128)(2,1)S(1)} collective-permute-done((bf16[96,768]{1,0:T(8,128)(2,1)S(1)}, bf16[96,768]{1,0:T(8,128)(2,1)S(1)}, u32[]{:S(2)}, u32[]{:S(2)}) %collective-permute-start.34) | collective-permute-done | bytes 147488 | tf_op jit(solution)/shard_map/ppermute | solution.py:349
  177.5 5.2 %collective-permute-done.33 = bf16[96,768]{1,0:T(8,128)(2,1)S(1)} collective-permute-done((bf16[96,768]{1,0:T(8,128)(2,1)S(1)}, bf16[96,768]{1,0:T(8,128)(2,1)S(1)}, u32[]{:S(2)}, u32[]{:S(2)}) %collective-permute-start.33) | collective-permute-done | bytes 147488 | tf_op jit(solution)/shard_map/ppermute | solution.py:349
  190.5 2.2 %shard_map.179 = (bf16[128,768]{1,0:T(8,128)(2,1)}, bf16[128,768]{1,0:T(8,128)(2,1)}) custom-call(f32[256,768]{1,0:T(8,128)S(1)} %get-tuple-element.61.g_keep, bf16[256,768]{1,0:T(8,128)(2,1)S(1)} %collective-permute-done.22.g_core, f32[256,768]{1,0:T(8,128)S(1)} %get-tuple-element.65.b_keep, bf16[256,768]{1,0:T(8,128)(2,1)S(1)} %collective-permute-done.23.b_core, ...), custom_call_target="tpu_custom_call" | custom-call | bytes 4720128 | tf_op jit(solution)/shard_map/pallas_call | solution.py:30
  (135 shorter events, 66.8 us)
Async XLA Ops:
  1.8 12.1 %collective-permute-start = (bf16[2,128,768]{2,1,0:T(8,128)(2,1)S(1)}, bf16[2,128,768]{2,1,0:T(8,128)(2,1)S(1)}, u32[]{:S(2)}, u32[]{:S(2)}) collective-permute-start(bf16[2,128,768]{2,1,0:T(8,128)(2,1)S(1)} %pad_maximum_fusion.1), channel_id=1, source_target_pairs={{0,2},{1,3},{2,0},{3,1},{4,6},{5,7},{6,4},{7,5},{8,10},{9,11},{10,... | collective-permute-start | bytes 1179656 | tf_op jit(solution)/shard_map/ppermute | solution.py:349
  15.0 61.7 %collective-permute-start.1 = (bf16[2,256,768]{2,1,0:T(8,128)(2,1)S(1)}, bf16[2,256,768]{2,1,0:T(8,128)(2,1)}, u32[]{:S(2)}, u32[]{:S(2)}) collective-permute-start(bf16[2,256,768]{2,1,0:T(8,128)(2,1)S(1)} %pad_maximum_fusion), channel_id=1, source_target_pairs={{0,1},{1,0},{2,3},{3,2},{4,5},{5,4},{6,7},{7,6},{8,9},{9,8},{10,11... | collective-permute-start | bytes 2359304 | tf_op jit(solution)/shard_map/ppermute | solution.py:349
  19.3 20.9 %collective-permute-start.3 = (bf16[96,576]{1,0:T(8,128)(2,1)S(1)}, bf16[96,576]{1,0:T(8,128)(2,1)S(1)}, u32[]{:S(2)}, u32[]{:S(2)}) collective-permute-start(bf16[96,576]{1,0:T(8,128)(2,1)S(1)} %copy.30.rest_0_), channel_id=1, source_target_pairs={{0,16},{4,20},{8,24},{12,28},{16,0},{20,4},{24,8},{28,12},{1,17},{... | collective-permute-start | bytes 331784 | tf_op jit(solution)/shard_map/ppermute | solution.py:349
  19.8 33.6 %collective-permute-start.11 = (bf16[96,1056]{1,0:T(8,128)(2,1)S(1)}, bf16[96,1056]{1,0:T(8,128)(2,1)S(1)}, u32[]{:S(2)}, u32[]{:S(2)}) collective-permute-start(bf16[96,1056]{1,0:T(8,128)(2,1)S(1)} %concatenate.13.rest_0_), channel_id=1, source_target_pairs={{0,24},{4,28},{8,16},{12,20},{16,8},{20,12},{24,0},{28,4},{1,25},{... | collective-permute-start | bytes 608264 | tf_op jit(solution)/shard_map/ppermute | solution.py:349
  21.8 32.2 %collective-permute-start.10 = (bf16[96,1056]{1,0:T(8,128)(2,1)S(1)}, bf16[96,1056]{1,0:T(8,128)(2,1)S(1)}, u32[]{:S(2)}, u32[]{:S(2)}) collective-permute-start(bf16[96,1056]{1,0:T(8,128)(2,1)S(1)} %concatenate.13.rest_0_), channel_id=1, source_target_pairs={{0,16},{4,20},{8,24},{12,28},{16,0},{20,4},{24,8},{28,12},{1,17},{... | collective-permute-start | bytes 608264 | tf_op jit(solution)/shard_map/ppermute | solution.py:349
  23.6 31.9 %collective-permute-start.9 = (bf16[96,1056]{1,0:T(8,128)(2,1)S(1)}, bf16[96,1056]{1,0:T(8,128)(2,1)S(1)}, u32[]{:S(2)}, u32[]{:S(2)}) collective-permute-start(bf16[96,1056]{1,0:T(8,128)(2,1)S(1)} %concatenate.13.rest_0_), channel_id=1, source_target_pairs={{0,8},{4,12},{8,0},{12,4},{16,24},{20,28},{24,16},{28,20},{1,9},{5... | collective-permute-start | bytes 608264 | tf_op jit(solution)/shard_map/ppermute | solution.py:349
  40.2 11.7 %collective-permute-start.2 = (bf16[96,576]{1,0:T(8,128)(2,1)S(1)}, bf16[96,576]{1,0:T(8,128)(2,1)S(1)}, u32[]{:S(2)}, u32[]{:S(2)}) collective-permute-start(bf16[96,576]{1,0:T(8,128)(2,1)S(1)} %copy.30.rest_0_), channel_id=1, source_target_pairs={{0,8},{4,12},{8,0},{12,4},{16,24},{20,28},{24,16},{28,20},{1,9},{5... | collective-permute-start | bytes 331784 | tf_op jit(solution)/shard_map/ppermute | solution.py:349
  53.4 11.5 %collective-permute-start.15 = (bf16[96,1056]{1,0:T(8,128)(2,1)S(1)}, bf16[96,1056]{1,0:T(8,128)(2,1)S(1)}, u32[]{:S(2)}, u32[]{:S(2)}) collective-permute-start(bf16[96,1056]{1,0:T(8,128)(2,1)S(1)} %collective-permute-done.11.rest_3_), channel_id=1, source_target_pairs={{0,4},{4,0},{8,12},{12,8},{16,20},{20,16},{24,28},{28,24},{1,5},{5... | collective-permute-start | bytes 608264 | tf_op jit(solution)/shard_map/ppermute | solution.py:349
  54.0 15.7 %collective-permute-start.14 = (bf16[96,1056]{1,0:T(8,128)(2,1)S(1)}, bf16[96,1056]{1,0:T(8,128)(2,1)S(1)}, u32[]{:S(2)}, u32[]{:S(2)}) collective-permute-start(bf16[96,1056]{1,0:T(8,128)(2,1)S(1)} %collective-permute-done.10.rest_2_), channel_id=1, source_target_pairs={{0,4},{4,0},{8,12},{12,8},{16,20},{20,16},{24,28},{28,24},{1,5},{5... | collective-permute-start | bytes 608264 | tf_op jit(solution)/shard_map/ppermute | solution.py:349
  55.5 19.0 %collective-permute-start.13 = (bf16[96,1056]{1,0:T(8,128)(2,1)S(1)}, bf16[96,1056]{1,0:T(8,128)(2,1)S(1)}, u32[]{:S(2)}, u32[]{:S(2)}) collective-permute-start(bf16[96,1056]{1,0:T(8,128)(2,1)S(1)} %collective-permute-done.9.rest_1_), channel_id=1, source_target_pairs={{0,4},{4,0},{8,12},{12,8},{16,20},{20,16},{24,28},{28,24},{1,5},{5... | collective-permute-start | bytes 608264 | tf_op jit(solution)/shard_map/ppermute | solution.py:349
  60.2 19.7 %collective-permute-start.5 = (bf16[96,576]{1,0:T(8,128)(2,1)S(1)}, bf16[96,576]{1,0:T(8,128)(2,1)S(1)}, u32[]{:S(2)}, u32[]{:S(2)}) collective-permute-start(bf16[96,576]{1,0:T(8,128)(2,1)S(1)} %copy.30.rest_0_), channel_id=1, source_target_pairs={{0,4},{4,0},{8,12},{12,8},{16,20},{20,16},{24,28},{28,24},{1,5},{5... | collective-permute-start | bytes 331784 | tf_op jit(solution)/shard_map/ppermute | solution.py:349
  65.0 15.0 %collective-permute-start.8 = (bf16[96,576]{1,0:T(8,128)(2,1)S(1)}, bf16[96,576]{1,0:T(8,128)(2,1)S(1)}, u32[]{:S(2)}, u32[]{:S(2)}) collective-permute-start(bf16[96,576]{1,0:T(8,128)(2,1)S(1)} %collective-permute-done.4.rest_3_), channel_id=1, source_target_pairs={{0,4},{4,0},{8,12},{12,8},{16,20},{20,16},{24,28},{28,24},{1,5},{5... | collective-permute-start | bytes 331784 | tf_op jit(solution)/shard_map/ppermute | solution.py:349
  69.7 12.6 %collective-permute-start.7 = (bf16[96,576]{1,0:T(8,128)(2,1)S(1)}, bf16[96,576]{1,0:T(8,128)(2,1)S(1)}, u32[]{:S(2)}, u32[]{:S(2)}) collective-permute-start(bf16[96,576]{1,0:T(8,128)(2,1)S(1)} %collective-permute-done.3.rest_2_), channel_id=1, source_target_pairs={{0,4},{4,0},{8,12},{12,8},{16,20},{20,16},{24,28},{28,24},{1,5},{5... | collective-permute-start | bytes 331784 | tf_op jit(solution)/shard_map/ppermute | solution.py:349
  74.4 9.6 %collective-permute-start.6 = (bf16[96,576]{1,0:T(8,128)(2,1)S(1)}, bf16[96,576]{1,0:T(8,128)(2,1)S(1)}, u32[]{:S(2)}, u32[]{:S(2)}) collective-permute-start(bf16[96,576]{1,0:T(8,128)(2,1)S(1)} %collective-permute-done.2.rest_1_), channel_id=1, source_target_pairs={{0,4},{4,0},{8,12},{12,8},{16,20},{20,16},{24,28},{28,24},{1,5},{5... | collective-permute-start | bytes 331784 | tf_op jit(solution)/shard_map/ppermute | solution.py:349
  94.2 11.2 %collective-permute-start.17 = (bf16[256,768]{1,0:T(8,128)(2,1)S(1)}, bf16[256,768]{1,0:T(8,128)(2,1)S(1)}, u32[]{:S(2)}, u32[]{:S(2)}) collective-permute-start(bf16[256,768]{1,0:T(8,128)(2,1)S(1)} %add_convert_fusion.1.own), channel_id=1, source_target_pairs={{0,2},{1,3},{2,0},{3,1},{4,6},{5,7},{6,4},{7,5},{8,10},{9,11},{10,... | collective-permute-start | bytes 1179656 | tf_op jit(solution)/shard_map/ppermute | solution.py:349
  112.5 11.2 %collective-permute-start.20 = (bf16[256,768]{1,0:T(8,128)(2,1)S(1)}, bf16[256,768]{1,0:T(8,128)(2,1)S(1)}, u32[]{:S(2)}, u32[]{:S(2)}) collective-permute-start(bf16[256,768]{1,0:T(8,128)(2,1)S(1)} %add_convert_fusion.own), channel_id=1, source_target_pairs={{0,2},{1,3},{2,0},{3,1},{4,6},{5,7},{6,4},{7,5},{8,10},{9,11},{10,... | collective-permute-start | bytes 1179656 | tf_op jit(solution)/shard_map/ppermute | solution.py:349
  116.6 18.7 %collective-permute-start.35 = (bf16[4,96,864]{2,1,0:T(8,128)(2,1)S(1)}, bf16[4,96,864]{2,1,0:T(8,128)(2,1)S(1)}, u32[]{:S(2)}, u32[]{:S(2)}) collective-permute-start(bf16[4,96,864]{2,1,0:T(8,128)(2,1)S(1)} %get-tuple-element.75), channel_id=1, source_target_pairs={{0,4},{4,0},{8,12},{12,8},{16,20},{20,16},{24,28},{28,24},{1,5},{5... | collective-permute-start | bytes 1990664 | tf_op jit(solution)/shard_map/ppermute | solution.py:349
  138.1 11.4 %collective-permute-start.38 = (bf16[96,864]{1,0:T(8,128)(2,1)S(1)}, bf16[96,864]{1,0:T(8,128)(2,1)S(1)}, u32[]{:S(2)}, u32[]{:S(2)}) collective-permute-start(bf16[96,864]{1,0:T(8,128)(2,1)S(1)} %get-tuple-element.103), channel_id=1, source_target_pairs={{0,24},{4,28},{8,16},{12,20},{16,8},{20,12},{24,0},{28,4},{1,25},{... | collective-permute-start | bytes 497672 | tf_op jit(solution)/shard_map/ppermute | solution.py:349
  140.7 15.9 %collective-permute-start.37 = (bf16[96,864]{1,0:T(8,128)(2,1)S(1)}, bf16[96,864]{1,0:T(8,128)(2,1)S(1)}, u32[]{:S(2)}, u32[]{:S(2)}) collective-permute-start(bf16[96,864]{1,0:T(8,128)(2,1)S(1)} %get-tuple-element.104), channel_id=1, source_target_pairs={{0,16},{4,20},{8,24},{12,28},{16,0},{20,4},{24,8},{28,12},{1,17},{... | collective-permute-start | bytes 497672 | tf_op jit(solution)/shard_map/ppermute | solution.py:349
  141.6 23.6 %collective-permute-start.31 = (bf16[4,96,768]{2,1,0:T(8,128)(2,1)}, bf16[4,96,768]{2,1,0:T(8,128)(2,1)}, u32[]{:S(2)}, u32[]{:S(2)}) collective-permute-start(bf16[4,96,768]{2,1,0:T(8,128)(2,1)} %get-tuple-element.73), channel_id=1, source_target_pairs={{0,4},{4,0},{8,12},{12,8},{16,20},{20,16},{24,28},{28,24},{1,5},{5... | collective-permute-start | bytes 1769480 | tf_op jit(solution)/shard_map/ppermute | solution.py:349
  143.1 13.5 %collective-permute-start.27 = (f32[2,768]{1,0:T(2,128)S(1)}, f32[2,768]{1,0:T(2,128)S(1)}, u32[]{:S(2)}, u32[]{:S(2)}) collective-permute-start(f32[2,768]{1,0:T(2,128)S(1)} %fusion.9), channel_id=1, source_target_pairs={{0,4},{4,0},{8,12},{12,8},{16,20},{20,16},{24,28},{28,24},{1,5},{5... | collective-permute-start | bytes 18440 | tf_op jit(solution)/shard_map/ppermute | solution.py:349
  167.7 9.9 %collective-permute-start.34 = (bf16[96,768]{1,0:T(8,128)(2,1)S(1)}, bf16[96,768]{1,0:T(8,128)(2,1)S(1)}, u32[]{:S(2)}, u32[]{:S(2)}) collective-permute-start(bf16[96,768]{1,0:T(8,128)(2,1)S(1)} %get-tuple-element.106), channel_id=1, source_target_pairs={{0,24},{4,28},{8,16},{12,20},{16,8},{20,12},{24,0},{28,4},{1,25},{... | collective-permute-start | bytes 442376 | tf_op jit(solution)/shard_map/ppermute | solution.py:349
  170.1 12.6 %collective-permute-start.33 = (bf16[96,768]{1,0:T(8,128)(2,1)S(1)}, bf16[96,768]{1,0:T(8,128)(2,1)S(1)}, u32[]{:S(2)}, u32[]{:S(2)}) collective-permute-start(bf16[96,768]{1,0:T(8,128)(2,1)S(1)} %get-tuple-element.107), channel_id=1, source_target_pairs={{0,16},{4,20},{8,24},{12,28},{16,0},{20,4},{24,8},{28,12},{1,17},{... | collective-permute-start | bytes 442376 | tf_op jit(solution)/shard_map/ppermute | solution.py:349
  171.0 18.5 %collective-permute-start.24 = (bf16[256,768]{1,0:T(8,128)(2,1)}, bf16[256,768]{1,0:T(8,128)(2,1)}, u32[]{:S(2)}, u32[]{:S(2)}) collective-permute-start(bf16[256,768]{1,0:T(8,128)(2,1)} %pad_maximum_fusion.2), channel_id=1, source_target_pairs={{0,2},{1,3},{2,0},{3,1},{4,6},{5,7},{6,4},{7,5},{8,10},{9,11},{10,... | collective-permute-start | bytes 1179656 | tf_op jit(solution)/shard_map/ppermute | solution.py:349
  (31 other events, 261.4 us)

commit v2 on v1

--- a/solution.py
+++ b/solution.py
@@ -77,11 +77,10 @@
     return (lane >= head * HEAD_DIM) & (lane < (head + 1) * HEAD_DIM)
 
 
-def prepare_kernel(ids, first, pair, other, gain, freq, n1, cosine, sine):
+def prepare_kernel(ids, first, t0, t1, t2, t3, gain, freq, n1, cosine, sine):
     gain_row = gain[...].astype(F32)
-    for i in range(4):
-        source = pair if i < 2 else other
-        unit, _ = normed(source[(i % 2) * WINDOW : (i % 2 + 1) * WINDOW, :].astype(F32))
+    for i, source in enumerate((t0, t1, t2, t3)):
+        unit, _ = normed(source[...].astype(F32))
         n1[rows_of(ids[i]), :] = (unit * gain_row).astype(BF)
     start = jnp.int32(0)
     lane = lax.broadcasted_iota(jnp.int32, (WINDOW, 128), 1)
@@ -162,10 +161,9 @@
         att_out[rows_b, :] = mixed.astype(BF)
 
 
-def collect_kernel(offsets, n_pieces, rows, widths, ids, *rest):
+def collect_kernel(offsets, n_pieces, rows, units2, ids, *rest):
     pieces = rest[:n_pieces]
-    in_w, out_w, down_w = rest[n_pieces:]
-    units2, heads_w, units = widths
+    in_w, down_w = rest[n_pieces:]
     for j, piece in enumerate(pieces):
         if offsets is None:
             at = slice(None)
@@ -173,11 +171,13 @@
             at = rows_of(jnp.bitwise_xor(ids[4], offsets[j]), rows)
         value = piece[...]
         in_w[at, :] = value[:, :units2]
-        out_w[at, :] = value[:, units2 : units2 + heads_w]
-        down_w[at, :] = value[:, units2 + heads_w :]
-
-
-def project_kernel(ids, att, out_w, send, keep):
+        down_w[at, :] = value[:, units2:]
+
+
+def project_kernel(offsets, n_pieces, rows, ids, att, *rest):
+    pieces = rest[:n_pieces]
+    send, keep, out_w = rest[n_pieces:]
+    put_pieces(ids, offsets, pieces, out_w, rows)
     for i in range(4):
         part = dot(att[rows_of(ids[i]), :], out_w[...], NT)
         at = slice((i % 2) * WINDOW, (i % 2 + 1) * WINDOW)
@@ -187,24 +187,24 @@
             send[at, :] = part.astype(BF)
 
 
-def middle_kernel(own, received, tokens, gain, h_out, n2_out):
-    for i in range(2):
+def middle_kernel(own, received, t0, t1, gain, h_out, n2_out):
+    for i, tokens in enumerate((t0, t1)):
         at = slice(i * WINDOW, (i + 1) * WINDOW)
         back = slice((1 - i) * WINDOW, (2 - i) * WINDOW)
         branch = own[at, :].astype(F32) + received[back, :].astype(F32)
-        h = tokens[at, :].astype(F32) + branch
+        h = tokens[...].astype(F32) + branch
         h_out[at, :] = h
         unit, _ = normed(h)
         n2_out[at, :] = (unit * gain[...].astype(F32)).astype(BF)
 
 
-def units_kernel(n2, n2_far, gz, gz_far, in_w, down_w, send, keep, both_out, act_out):
+def units_kernel(n2, n2_far, c0, c1, c2, c3, in_w, down_w, send, keep, both_out, act_out):
     units = act_out.shape[1]
     gate_w, up_w = in_w[:, :units], in_w[:, units:]
     for i in (2, 3, 0, 1):
         at = slice((i % 2) * WINDOW, (i % 2 + 1) * WINDOW)
         rows_n = (n2 if i < 2 else n2_far)[at, :]
-        rows_g = (gz if i < 2 else gz_far)[at, :]
+        rows_g = (c0, c1, c2, c3)[i][...]
         gate = dot(rows_n, gate_w)
         up = dot(rows_n, up_w)
         g_act = dot(rows_g, down_w[...])
@@ -230,13 +230,14 @@
 
 
 def unit_grads_kernel(
-    slots, rows, ids, n2, n2_far, gz, gz_far, both, act, down_w, send, keep, b_send, b_keep, total
+    slots, rows, ids, n2, n2_far, c0, c1, c2, c3, both, act, down_w, send, keep, b_send, b_keep, total
 ):
     pair = 2 * WINDOW
     units2 = both.shape[1]
     in_part = dot(n2[...], both[:pair, :], TN) + dot(n2_far[...], both[pair:, :], TN)
     total[:, :units2] = in_part
-    down_part = dot(gz[...], act[:pair, :], TN) + dot(gz_far[...], act[pair:, :], TN)
+    gz = jnp.concatenate([c0[...], c1[...], c2[...], c3[...]], axis=0)
+    down_part = dot(gz, act[...], TN)
     total[:, units2:] = down_part
     if slots:
         emit_slots(ids, slots, rows, total, send, keep)
@@ -247,14 +248,14 @@
     b_send[...] = dot(act[pair:, :], down_w[...], NT).astype(BF)
 
 
-def residual_kernel(own, received, h, cot, gain, gh_out, gy_out, gain_out):
+def residual_kernel(own, received, h, c0, c1, gain, gh_out, gy_out, gain_out):
     gain_row = gain[...].astype(F32)
-    for i in range(2):
+    for i, cot in enumerate((c0, c1)):
         at = slice(i * WINDOW, (i + 1) * WINDOW)
         back = slice((1 - i) * WINDOW, (2 - i) * WINDOW)
         grad = own[at, :].astype(F32) + received[back, :].astype(F32)
         unit, scale = normed(h[at, :])
-        gh = cot[at, :].astype(F32) + norm_back(grad, gain_row, unit, scale)
+        gh = cot[...].astype(F32) + norm_back(grad, gain_row, unit, scale)
         gy_out[at, :] = gh.astype(BF)
         if i == 0:
             gh_out[...] = gh
@@ -262,9 +263,9 @@
 
 
 def attend_back_kernel(
-    slots, rows, ids, gy, gy_far, out_w, att, q_in, k_in, v_in, probs_in, cosine, sine, n1, qkv_w, gain,
-    g_send, g_keep, send, keep, gain_out,
-    gy_all, k_pad, v_pad, gk_pad, gv_pad, gq_all, g_raw, total,
+    ids, gy, gy_far, out_w, q_in, k_in, v_in, probs_in, cosine, sine,
+    g_raw,
+    g_att_all, k_pad, v_pad, gk_pad, gv_pad, gq_all,
 ):
     half = WINDOW // 2
     total_rows, width = q_in.shape
@@ -273,7 +274,8 @@
     span = 2 * WINDOW
     for i in range(4):
         source = gy if i < 2 else gy_far
-        gy_all[rows_of(ids[i]), :] = source[(i % 2) * WINDOW : (i % 2 + 1) * WINDOW, :]
+        part = dot(source[(i % 2) * WINDOW : (i % 2 + 1) * WINDOW, :], out_w[...])
+        g_att_all[rows_of(ids[i]), :] = part.astype(BF)
     for pad, source in ((k_pad, k_in), (v_pad, v_in)):
         pad[0:half, :] = jnp.zeros((half, width), BF)
         pad[half + total_rows :, :] = jnp.zeros((half, width), BF)
@@ -283,7 +285,7 @@
     for b in range(blocks):
         rows_b = slice(b * WINDOW, (b + 1) * WINDOW)
         span_b = slice(b * WINDOW, b * WINDOW + span)
-        g_att = dot(gy_all[rows_b, :], out_w[...]).astype(BF)
+        g_att = g_att_all[rows_b, :]
         q_b = q_in[rows_b, :]
         keys = k_pad[span_b, :]
         values = v_pad[span_b, :]
@@ -305,7 +307,6 @@
         gk_pad[span_b, :] += gk
         gv_pad[span_b, :] += gv
     scale = HEAD_DIM**-0.5
-    columns = 3 * width
     for b in range(blocks):
         rows_b = slice(b * WINDOW, (b + 1) * WINDOW)
         inner = slice(half + b * WINDOW, half + (b + 1) * WINDOW)
@@ -315,15 +316,24 @@
         turned = qk * c - swap_halves(qk) * s
         g_raw[rows_b, : 2 * width] = turned.astype(BF)
         g_raw[rows_b, 2 * width :] = gv_pad[inner, :].astype(BF)
+
+
+def attend_grads_kernel(slots, rows, ids, n1, g_raw, gy, gy_far, att, send, keep, total):
+    columns = g_raw.shape[1]
     total[:, :columns] = dot(n1[...], g_raw[...], TN)
-    total[:, columns:] = dot(gy_all[...], att[...], TN)
+    near = jnp.concatenate([att[rows_of(ids[i]), :] for i in (0, 1)], axis=0)
+    far = jnp.concatenate([att[rows_of(ids[i]), :] for i in (2, 3)], axis=0)
+    total[:, columns:] = dot(gy[...], near, TN) + dot(gy_far[...], far, TN)
     if slots:
         emit_slots(ids, slots, rows, total, send, keep)
     else:
         send[...] = total[...]
         keep[...] = jnp.zeros(keep.shape, BF)
-    gain_sum = jnp.zeros(gain_out.shape, F32)
-    for i in range(4):
+
+
+def first_back_kernel(ids, g_raw, qkv_w, n1, gain, gain_two, g_send, g_keep, gains):
+    gain_sum = jnp.zeros(gain_two.shape, F32)
+    for i in (2, 3, 0, 1):
         at = slice((i % 2) * WINDOW, (i % 2 + 1) * WINDOW)
         g_n1 = dot(g_raw[rows_of(ids[i]), :], qkv_w[...], NT)
         gain_sum += jnp.sum(g_n1 * n1[rows_of(ids[i]), :].astype(F32), axis=0, keepdims=True)
@@ -331,7 +341,25 @@
             g_keep[at, :] = g_n1
         else:
             g_send[at, :] = g_n1.astype(BF)
-    gain_out[...] = gain_sum / gain[...].astype(F32)
+    gains[0:1, :] = gain_sum / gain[...].astype(F32)
+    gains[1:2, :] = gain_two[...]
+
+
+def merge_kernel(keep, got, first, *others):
+    first[...] = keep[0].astype(F32) + got[0].astype(F32)
+    for k, other in enumerate(others):
+        other[...] = (keep[k + 1].astype(F32) + got[k + 1].astype(F32)).astype(BF)
+
+
+def deliver_kernel(first, *rest):
+    wide, turned = rest[-2:]
+    total = first[...]
+    for part in rest[:-2]:
+        total = total + part[...].astype(F32)
+    _, count, width = wide.shape
+    for j in range(count):
+        wide[:, j, :] = total[:, j * width : (j + 1) * width]
+    turned[...] = total[:, count * width :].T
 
 
 def finish_kernel(
@@ -339,7 +367,7 @@
 ):
     gain_row = gain[...].astype(F32)
     grad = g_keep[:WINDOW, :] + g_core[:WINDOW, :].astype(F32) + received[:WINDOW, :].astype(F32)
-    unit, scale = normed(tokens[:WINDOW, :].astype(F32))
+    unit, scale = normed(tokens[...].astype(F32))
     grad_out[...] = (gh[...] + norm_back(grad, gain_row, unit, scale)).astype(BF)
     branch = b_keep[:WINDOW, :] + b_core[:WINDOW, :].astype(F32) + received[WINDOW:, :].astype(F32)
     mixed_out[...] = (h[:WINDOW, :] + branch).astype(BF)
@@ -369,23 +397,38 @@
     across = functools.partial(swap, axis="tensor", bit=2, size=4)
     dp = functools.partial(swap, axis="dp", size=n_dp)
 
-    def gather(value):
+    def along(value):
         if not slots:
-            return (lax.all_gather(value, "dp", axis=0, tiled=True),), None
-        near = [value] + [dp(value, bit=2 * k) for k in range(1, slots)]
-        far = [dp(piece, bit=1) for piece in near]
-        offsets = [2 * k for k in range(slots)] + [2 * k + 1 for k in range(slots)]
-        return tuple(near + far), tuple(offsets)
-
-    def reduce(send, keep):
+            return [lax.all_gather(value, "dp", axis=0, tiled=True)]
+        return [dp(value, bit=2 * k) for k in range(1, slots)]
+
+    def aside(pieces):
         if not slots:
-            return lax.psum_scatter(send, "dp", scatter_dimension=0, tiled=True)
-        part = keep.astype(F32) + dp(send, bit=1).astype(F32)
-        rounded = part.astype(BF)
-        total = part[0]
-        for k in range(1, slots):
-            total = total + dp(rounded[k], bit=2 * k).astype(F32)
-        return total
+            return []
+        return list(dp(jnp.stack(pieces), bit=1))
+
+    def picked(own, near, far):
+        return (own, *near, *far) if slots else tuple(near)
+
+    def merge(keep, got):
+        _, rows, columns = keep.shape
+        return call(
+            merge_kernel,
+            (shape(rows, columns, dtype=F32),) + (shape(rows, columns),) * (slots - 1),
+            (keep, got),
+        )
+
+    def deliver(parts, count):
+        columns = parts[0].shape[1]
+        each = columns // (count + 1)
+        if not slots:
+            total = parts[0]
+            return total[:, : count * each].reshape(shard, count, each), total[:, count * each :].T
+        return call(
+            deliver_kernel,
+            (shape(shard, count, each, dtype=F32), shape(each, shard, dtype=F32)),
+            parts,
+        )
 
     def slot_shapes(columns):
         if not slots:
@@ -397,22 +440,32 @@
     freqs = ROPE_BASE ** (-(np.arange(HEAD_DIM // 2, dtype=np.float32) * 2.0) / HEAD_DIM)
     freq = jnp.asarray(np.tile(freqs, 128 // (HEAD_DIM // 2))[None, :], F32)
 
-    qkv_pieces, offsets = gather(w_qkv.reshape(shard, 3 * head_width))
-    staged = jnp.stack([tokens, cotangent])
-    pair = jnp.concatenate([staged, across(staged)], axis=1)
-    other = core(pair)
-    own_tokens, own_cot = pair[0], pair[1]
-    far_tokens, far_cot = other[0], other[1]
-    rest_pieces, _ = gather(
-        jnp.concatenate([w_in.reshape(shard, 2 * units), w_out.T, w_down.T], axis=1)
-    )
-
+    offsets = tuple(range(0, n_dp, 2)) + tuple(range(1, n_dp, 2)) if slots else None
+    pin = lax.optimization_barrier
+
+    qkv_own = w_qkv.reshape(shard, 3 * head_width)
+    qkv_near = along(qkv_own)
+    token_blocks = [tokens, across(tokens), core(tokens)]
+    token_blocks.append(core(token_blocks[1]))
     n1, cosine, sine = call(
         prepare_kernel,
         (shape(total_rows, width), shape(total_rows, 128, dtype=F32), shape(total_rows, 128, dtype=F32)),
-        (own_tokens, far_tokens, gain_one, freq),
+        tuple(token_blocks) + (gain_one, freq),
         (ids, block_first),
     )
+    out_own = w_out.T
+    unit_own = jnp.concatenate([w_in.reshape(shard, 2 * units), w_down.T], axis=1)
+    qkv_near, n1, out_own, unit_own, cot = pin((qkv_near, n1, out_own, unit_own, cotangent))
+    qkv_far = aside([qkv_own] + qkv_near)
+    out_near = along(out_own)
+    unit_near = along(unit_own)
+    cot_blocks = [cotangent, across(cot), core(cot)]
+    cot_blocks.append(core(cot_blocks[1]))
+    cot_blocks = tuple(cot_blocks)
+    qkv_pieces = picked(qkv_own, qkv_near, qkv_far)
+    out_near, _ = pin((out_near, qkv_far))
+    out_far = aside([out_own] + out_near)
+    out_pieces = picked(out_own, out_near, out_far)
     flat = shape(total_rows, head_width)
     query, keys, values, probs, attended, qkv_w = call(
         functools.partial(attend_kernel, offsets, len(qkv_pieces), shard),
@@ -422,27 +475,35 @@
         [pltpu.VMEM((total_rows + WINDOW, head_width), BF)] * 2,
         flops=2 * total_rows * width * 3 * head_width,
     )
-    in_w, out_w, down_w = call(
-        functools.partial(
-            collect_kernel, offsets, len(rest_pieces), shard, (2 * units, head_width, units)
-        ),
-        (shape(width, 2 * units), shape(width, head_width), shape(width, units)),
-        rest_pieces,
+    attended, unit_near, out_pieces = pin((attended, unit_near, out_pieces))
+    unit_far = aside([unit_own] + unit_near)
+    unit_pieces = picked(unit_own, unit_near, unit_far)
+    in_w, down_w = call(
+        functools.partial(collect_kernel, offsets, len(unit_pieces), shard, 2 * units),
+        (shape(width, 2 * units), shape(width, units)),
+        unit_pieces,
         (ids,),
     )
     pair_f32 = shape(pair_rows, width, dtype=F32)
     pair_bf = shape(pair_rows, width)
-    a_send, a_keep = call(
-        project_kernel, (pair_bf, pair_f32), (attended, out_w), (ids,),
+    a_send, a_keep, out_w = call(
+        functools.partial(project_kernel, offsets, len(out_pieces), shard),
+        (pair_bf, pair_f32, shape(width, head_width)),
+        (attended,) + out_pieces,
+        (ids,),
         flops=2 * total_rows * width * head_width,
     )
     a_sum = (a_keep + core(a_send).astype(F32)).astype(BF)
-    h, n2 = call(middle_kernel, (pair_f32, pair_bf), (a_sum, across(a_sum), own_tokens, gain_two))
+    h, n2 = call(
+        middle_kernel,
+        (pair_f32, pair_bf),
+        (a_sum, across(a_sum), token_blocks[0], token_blocks[1], gain_two),
+    )
     n2_far = core(n2)
     u_send, u_keep, both, act = call(
         units_kernel,
         (pair_bf, pair_f32, shape(total_rows, 2 * units), shape(total_rows, units)),
-        (n2, n2_far, own_cot, far_cot, in_w, down_w),
+        (n2, n2_far) + cot_blocks + (in_w, down_w),
         flops=2 * total_rows * width * 5 * units,
     )
     u_sum = (u_keep + core(u_send).astype(F32)).astype(BF)
@@ -451,37 +512,50 @@
     in_send, in_keep, b_send, b_keep = call(
         functools.partial(unit_grads_kernel, slots, shard),
         s_shapes + (pair_bf, pair_f32),
-        (n2, n2_far, own_cot, far_cot, both, act, down_w),
+        (n2, n2_far) + cot_blocks + (both, act, down_w),
         (ids,),
         [pltpu.VMEM((width, 3 * units), F32)],
         flops=2 * total_rows * width * 4 * units,
     )
     b_core = core(b_send)
-    unit_grads = reduce(in_send, in_keep)
+    if slots:
+        in_parts = merge(in_keep, dp(in_send, bit=1))
     gh, gy, gain_part_two = call(
         residual_kernel,
         (shape(WINDOW, width, dtype=F32), pair_bf, shape(1, width, dtype=F32)),
-        (u_sum, u_got, h, own_cot, gain_two),
+        (u_sum, u_got, h, cot_blocks[0], cot_blocks[1], gain_two),
     )
     gy_far = core(gy)
-    g_send, g_keep, att_send, att_keep, gain_part_one = call(
-        functools.partial(attend_back_kernel, slots, shard),
-        (pair_bf, pair_f32) + slot_shapes(4 * head_width) + (shape(1, width, dtype=F32),),
-        (gy, gy_far, out_w, attended, query, keys, values, probs, cosine, sine, n1, qkv_w, gain_one),
+    (g_raw,) = call(
+        attend_back_kernel,
+        (shape(total_rows, 3 * head_width),),
+        (gy, gy_far, out_w, query, keys, values, probs, cosine, sine),
         (ids,),
         [
-            pltpu.VMEM((total_rows, width), BF),
+            pltpu.VMEM((total_rows, head_width), BF),
             pltpu.VMEM((total_rows + WINDOW, head_width), BF),
             pltpu.VMEM((total_rows + WINDOW, head_width), BF),
             pltpu.VMEM((total_rows + WINDOW, head_width), F32),
             pltpu.VMEM((total_rows + WINDOW, head_width), F32),
             pltpu.VMEM((total_rows, head_width), F32),
-            pltpu.VMEM((total_rows, 3 * head_width), BF),
-            pltpu.VMEM((width, 4 * head_width), F32),
         ],
-        flops=2 * total_rows * width * 8 * head_width,
-    )
-    att_grads = reduce(att_send, att_keep)
+        flops=2 * total_rows * width * 3 * head_width,
+    )
+    att_send, att_keep = call(
+        functools.partial(attend_grads_kernel, slots, shard),
+        slot_shapes(4 * head_width),
+        (n1, g_raw, gy, gy_far, attended),
+        (ids,),
+        [pltpu.VMEM((width, 4 * head_width), F32)],
+        flops=2 * total_rows * width * 4 * head_width,
+    )
+    g_send, g_keep, gains = call(
+        first_back_kernel,
+        (pair_bf, pair_f32, shape(2, width, dtype=F32)),
+        (g_raw, qkv_w, n1, gain_one, gain_part_two),
+        (ids,),
+        flops=2 * total_rows * width * 3 * head_width,
+    )
     g_core = core(g_send)
     back = jnp.concatenate(
         [
@@ -493,30 +567,29 @@
     mixed, input_grad = call(
         finish_kernel,
         (shape(WINDOW, width), shape(WINDOW, width)),
-        (g_keep, g_core, b_keep, b_core, across(back), h, own_tokens, gain_one, gh),
-    )
-    gains = jnp.concatenate([gain_part_one, gain_part_two], axis=0)
+        (g_keep, g_core, b_keep, b_core, across(back), h, tokens, gain_one, gh),
+    )
     if slots:
+        att_got = dp(att_send, bit=1)
+        in_parts = (in_parts[0], *(dp(in_parts[k], bit=2 * k) for k in range(1, slots)))
         gains = gains + core(gains)
         gains = gains + across(gains)
         gains = gains + dp(gains, bit=1)
-        total = gains
-        for k in range(1, slots):
-            total = total + dp(gains, bit=2 * k)
-        gains = total
+        att_got, gains, in_parts = pin((att_got, gains, in_parts))
+        att_parts = merge(att_keep, att_got)
+        att_parts = (att_parts[0], *(dp(att_parts[k], bit=2 * k) for k in range(1, slots)))
+        for part in [dp(gains, bit=2 * k) for k in range(1, slots)]:
+            gains = gains + part
     else:
         gains = lax.psum(gains, ("dp", "tensor"))
-    columns = 3 * head_width
-    return (
-        mixed,
-        input_grad,
-        gains[0],
-        att_grads[:, :columns].reshape(shard, 3, head_width),
-        att_grads[:, columns:].T,
-        gains[1],
-        unit_grads[:, : 2 * units].reshape(shard, 2, units),
-        unit_grads[:, 2 * units :].T,
-    )
+        in_parts = (lax.psum_scatter(in_send, "dp", scatter_dimension=0, tiled=True),)
+        att_parts = (lax.psum_scatter(att_send, "dp", scatter_dimension=0, tiled=True),)
+    in_grad, down_grad = deliver(in_parts, 2)
+    att_parts, mixed, input_grad, in_grad, down_grad = pin(
+        (att_parts, mixed, input_grad, in_grad, down_grad)
+    )
+    qkv_grad, out_grad = deliver(att_parts, 3)
+    return (mixed, input_grad, gains[0], qkv_grad, out_grad, gains[1], in_grad, down_grad)
 
 
 def solution(mesh):

time: 193 us -> 152 us (0.79)
  waiting for transfers between devices: 87.7 us -> 70.4 us
  local copies, waits for them, and re-layouts: 14 us -> 4.72 us
  starting transfers between devices: 55.8 us -> 46.8 us
  other arithmetic: 6.34 us -> 0.66 us
    ppermute x39 -> x41, waiting for transfers between devices: 87.7 us -> 70.4 us  [swap(): return lax.ppermute(values, axis, [(i, i ^ bit) for i in range(size)])]
    ppermute x39 -> x41, starting transfers between devices: 55.8 us -> 46.8 us  [swap(): return lax.ppermute(values, axis, [(i, i ^ bit) for i in range(size)])]
    unnamed x38 -> x24, local copies, waits for them, and re-layouts: 7.27 us -> 3.45 us
    slice x3 -> x0, local copies, waits for them, and re-layouts: 2.54 us -> none  [the longest x2 2.52 us: local(): att_grads[:, :columns].reshape(shard, 3, head_width)]
    pallas_call x10 -> x16, Pallas kernels: 27.7 us -> 28.6 us  [call(): pl.pallas_call(kernel, out_shape=tuple(outs), in_specs=[pl.BlockSpec(memo...]
  transfers between devices with their start and end apart: 39 -> 41, of which waited for: 24 -> 14; matrix products, arithmetic and copies ran while one was open for 8% -> 2% of each run, Pallas kernels for 8% -> 15%
where the time goes in v2:
time: 152 us
  waiting for transfers between devices  70.4 us (46%)
  starting transfers between devices  46.8 us (31%)
  Pallas kernels  28.6 us (19%)
  local copies, waits for them, and re-layouts  4.72 us (3%)
    ppermute x41, waiting for transfers between devices, swap(): return lax.ppermute(values, axis, [(i, i ^ bit) for i in range(size)])  70.4 us
    ppermute x41, starting transfers between devices, swap(): return lax.ppermute(values, axis, [(i, i ^ bit) for i in range(size)])  46.8 us
    pallas_call x16, Pallas kernels, call(): pl.pallas_call(kernel, out_shape=tuple(outs), in_specs=[pl.BlockSpec(memo...  28.6 us
    unnamed x24, local copies, waits for them, and re-layouts  3.45 us
  transfers between devices with their start and end apart: 41, of which 14 were waited for; matrix products, arithmetic and copies ran while one was open for 2% of the time, Pallas kernels for 15%

profile of v2, /device:TPU:0, one launch (start us, length us, event | category | flops | bytes accessed | tf_op | source)
XLA Modules:
  0.0 152.2 jit_solution(16232315243626475749)
XLA Ops:
  0.6 3.0 %collective-permute-start.3 = (bf16[128,768]{1,0:T(8,128)(2,1)}, bf16[128,768]{1,0:T(8,128)(2,1)S(1)}, u32[]{:S(2)}, u32[]{:S(2)}) collective-permute-start(bf16[128,768]{1,0:T(8,128)(2,1)} %tokens.1), channel_id=1, source_target_pairs={{0,2},{1,3},{2,0},{3,1},{4,6},{5,7},{6,4},{7,5},{8,10},{9,11},{10,... | collective-permute-start | bytes 589832 | tf_op jit(solution)/shard_map/ppermute | solution.py:377
  3.7 5.1 %collective-permute-done.3.t1 = bf16[128,768]{1,0:T(8,128)(2,1)S(1)} collective-permute-done((bf16[128,768]{1,0:T(8,128)(2,1)}, bf16[128,768]{1,0:T(8,128)(2,1)S(1)}, u32[]{:S(2)}, u32[]{:S(2)}) %collective-permute-start.3) | collective-permute-done | bytes 196640 | tf_op jit(solution)/shard_map/ppermute | solution.py:377
  11.9 2.6 %collective-permute-start.1 = (bf16[96,576]{1,0:T(8,128)(2,1)S(1)}, bf16[96,576]{1,0:T(8,128)(2,1)S(1)}, u32[]{:S(2)}, u32[]{:S(2)}) collective-permute-start(bf16[96,576]{1,0:T(8,128)(2,1)S(1)} %copy.25.rest_0_), channel_id=1, source_target_pairs={{0,16},{4,20},{8,24},{12,28},{16,0},{20,4},{24,8},{28,12},{1,17},{... | collective-permute-start | bytes 331784 | tf_op jit(solution)/shard_map/ppermute | solution.py:377
  16.0 2.0 %shard_map.170 = (bf16[512,768]{1,0:T(8,128)(2,1)S(1)}, f32[512,128]{1,0:T(8,128)S(1)}, f32[512,128]{1,0:T(8,128)S(1)}) custom-call(s32[5]{0:T(128)S(1)} %stack.65.ids, s32[4]{0:T(128)S(1)} %copy-done.2, bf16[128,768]{1,0:T(8,128)(2,1)S(1)} %copy-done, bf16[128,768]{1,0:T(8,128)(2,1)S(1)} %collective-permute-done.3.t1, ...), custom_call_target="tpu_custom_call" | custom-call | bytes 2099200 | tf_op jit(solution)/shard_map/pallas_call | solution.py:30
  18.0 6.2 %collective-permute-done.1.rest_2_ = bf16[96,576]{1,0:T(8,128)(2,1)S(1)} collective-permute-done((bf16[96,576]{1,0:T(8,128)(2,1)S(1)}, bf16[96,576]{1,0:T(8,128)(2,1)S(1)}, u32[]{:S(2)}, u32[]{:S(2)}) %collective-permute-start.1) | collective-permute-done | bytes 110624 | tf_op jit(solution)/shard_map/ppermute | solution.py:377
  25.9 2.5 %collective-permute-start.10 = (bf16[96,192]{1,0:T(8,128)(2,1)S(1)}, bf16[96,192]{1,0:T(8,128)(2,1)S(1)}, u32[]{:S(2)}, u32[]{:S(2)}) collective-permute-start(bf16[96,192]{1,0:T(8,128)(2,1)S(1)} %bitcast.51), channel_id=1, source_target_pairs={{0,8},{4,12},{8,0},{12,4},{16,24},{20,28},{24,16},{28,20},{1,9},{5... | collective-permute-start | bytes 110600 | tf_op jit(solution)/shard_map/ppermute | solution.py:377
  30.9 5.5 %collective-permute-done.6 = bf16[4,96,576]{2,1,0:T(8,128)(2,1)S(1)} collective-permute-done((bf16[4,96,576]{2,1,0:T(8,128)(2,1)S(1)}, bf16[4,96,576]{2,1,0:T(8,128)(2,1)S(1)}, u32[]{:S(2)}, u32[]{:S(2)}) %collective-permute-start.6) | collective-permute-done | bytes 442400 | tf_op jit(solution)/shard_map/ppermute | solution.py:377
  38.1 3.0 %collective-permute-start.7 = (bf16[96,864]{1,0:T(8,128)(2,1)S(1)}, bf16[96,864]{1,0:T(8,128)(2,1)S(1)}, u32[]{:S(2)}, u32[]{:S(2)}) collective-permute-start(bf16[96,864]{1,0:T(8,128)(2,1)S(1)} %pad_maximum_fusion.4.rest_0_), channel_id=1, source_target_pairs={{0,8},{4,12},{8,0},{12,4},{16,24},{20,28},{24,16},{28,20},{1,9},{5... | collective-permute-start | bytes 497672 | tf_op jit(solution)/shard_map/ppermute | solution.py:377
  44.3 6.1 %shard_map.171 = (bf16[512,192]{1,0:T(8,128)(2,1)S(1)}, bf16[512,192]{1,0:T(8,128)(2,1)S(1)}, bf16[512,192]{1,0:T(8,128)(2,1)S(1)}, bf16[3,512,256]{2,1,0:T(8,12...) custom-call(s32[5]{0:T(128)S(1)} %stack.65.ids, s32[4]{0:T(128)S(1)} %copy-done.3, ...), custom_call_target="tpu_custom_call" | custom-call | flops 452984832 | bytes 4653056 | tf_op jit(solution)/shard_map/pallas_call | solution.py:30
  50.4 5.0 %collective-permute-done.8.rest_2_ = bf16[96,864]{1,0:T(8,128)(2,1)S(1)} collective-permute-done((bf16[96,864]{1,0:T(8,128)(2,1)S(1)}, bf16[96,864]{1,0:T(8,128)(2,1)S(1)}, u32[]{:S(2)}, u32[]{:S(2)}) %collective-permute-start.8) | collective-permute-done | bytes 165920 | tf_op jit(solution)/shard_map/ppermute | solution.py:377
  61.0 9.7 %collective-permute-done.15.received = bf16[256,768]{1,0:T(8,128)(2,1)S(1)} collective-permute-done((bf16[256,768]{1,0:T(8,128)(2,1)S(1)}, bf16[256,768]{1,0:T(8,128)(2,1)S(1)}, u32[]{:S(2)}, u32[]{:S(2)}) %collective-permute-start.15) | collective-permute-done | bytes 393248 | tf_op jit(solution)/shard_map/ppermute | solution.py:377
  71.6 2.5 %collective-permute-done.17.c1 = bf16[128,768]{1,0:T(8,128)(2,1)S(1)} collective-permute-done((bf16[128,768]{1,0:T(8,128)(2,1)S(1)}, bf16[128,768]{1,0:T(8,128)(2,1)S(1)}, u32[]{:S(2)}, u32[]{:S(2)}) %collective-permute-start.17) | collective-permute-done | bytes 196640 | tf_op jit(solution)/shard_map/ppermute | solution.py:377
  75.8 3.1 %shard_map.175 = (bf16[256,768]{1,0:T(8,128)(2,1)S(1)}, f32[256,768]{1,0:T(8,128)S(1)}, bf16[512,576]{1,0:T(8,128)(2,1)S(1)}, bf16[512,288]{1,0:T(8,128)(2,1)S(1)}) custom-call(bf16[256,768]{1,0:T(8,128)(2,1)S(1)} %get-tuple-element.114.n2, bf16[256,768]{1,0:T(8,128)(2,1)S(1)} %collective-permute-done.16.n2_far, bf16[128,768]{1,0:T(8,128)(2,1)S(1)} %copy-done.1, ...), custom_call_target="tpu_custom_call" | custom-call | flops 1132462080 | bytes 4964352 | tf_op jit(solution)/shard_map/pallas_call | solution.py:30
  82.3 9.6 %collective-permute-done.22.received = bf16[256,768]{1,0:T(8,128)(2,1)S(1)} collective-permute-done((bf16[256,768]{1,0:T(8,128)(2,1)S(1)}, bf16[256,768]{1,0:T(8,128)(2,1)S(1)}, u32[]{:S(2)}, u32[]{:S(2)}) %collective-permute-start.22) | collective-permute-done | bytes 393248 | tf_op jit(solution)/shard_map/ppermute | solution.py:377
  92.8 2.4 %shard_map.180 = (bf16[4,96,864]{2,1,0:T(8,128)(2,1)S(1)}, bf16[4,96,864]{2,1,0:T(8,128)(2,1)S(1)}, bf16[256,768]{1,0:T(8,128)(2,1)S(1)}, f32[256,768]{1,0:T(8,128)S(1)}) custom-call(s32[5]{0:T(128)S(1)} %stack.65.ids, bf16[256,768]{1,0:T(8,128)(2,1)S(1)} %get-tuple-element.114.n2, bf16[256,768]{1,0:T(8,128)(2,1)S(1)} %collective-permute-done.16.n2_far, ...), custom_call_target="tpu_custom_call" | custom-call | flops 905969664 | bytes 5406720 | tf_op jit(solution)/shard_map/pallas_call | solution.py:30
  96.0 4.9 %shard_map.177.g_raw = bf16[512,576]{1,0:T(8,128)(2,1)S(1)} custom-call(s32[5]{0:T(128)S(1)} %stack.65.ids, bf16[256,768]{1,0:T(8,128)(2,1)S(1)} %get-tuple-element.124.gy, bf16[256,768]{1,0:T(8,128)(2,1)S(1)} %collective-permute-done.23.gy_far, bf16[768,192]{1,0:T(8,128)(2,1)S(1)} %get-tuple-element.125.out_w, ...), custom_call_target="tpu_custom_call" | custom-call | flops 452984832 | bytes 3571712 | tf_op jit(solution)/shard_map/pallas_call | solution.py:30
  100.9 1.9 %shard_map.179 = (bf16[256,768]{1,0:T(8,128)(2,1)S(1)}, f32[256,768]{1,0:T(8,128)S(1)}, f32[2,768]{1,0:T(2,128)S(1)}) custom-call(s32[5]{0:T(128)S(1)} %stack.65.ids, bf16[512,576]{1,0:T(8,128)(2,1)S(1)} %shard_map.177.g_raw, bf16[768,576]{1,0:T(8,128)(2,1)S(1)} %get-tuple-element.132.qkv_w, bf16[512,768]{1,0:T(8,128)(2,1)S(1)} %get-tuple-element.91.n1, ...), custom_call_target="tpu_custom_call" | custom-call | flops 452984832 | bytes 3451392 | tf_op jit(solution)/shard_map/pallas_call | solution.py:30
  108.3 5.1 %collective-permute-done.28.got = bf16[4,96,864]{2,1,0:T(8,128)(2,1)S(1)} collective-permute-done((bf16[4,96,864]{2,1,0:T(8,128)(2,1)S(1)}, bf16[4,96,864]{2,1,0:T(8,128)(2,1)S(1)}, u32[]{:S(2)}, u32[]{:S(2)}) %collective-permute-start.28) | collective-permute-done | bytes 663584 | tf_op jit(solution)/shard_map/ppermute | solution.py:377
  113.6 2.5 %collective-permute-start.29 = (bf16[96,864]{1,0:T(8,128)(2,1)S(1)}, bf16[96,864]{1,0:T(8,128)(2,1)S(1)}, u32[]{:S(2)}, u32[]{:S(2)}) collective-permute-start(bf16[96,864]{1,0:T(8,128)(2,1)S(1)} %get-tuple-element.140), channel_id=1, source_target_pairs={{0,8},{4,12},{8,0},{12,4},{16,24},{20,28},{24,16},{28,20},{1,9},{5... | collective-permute-start | bytes 497672 | tf_op jit(solution)/shard_map/ppermute | solution.py:377
  119.2 6.6 %collective-permute-done.27 = f32[2,768]{1,0:T(2,128)S(1)} collective-permute-done((f32[2,768]{1,0:T(2,128)S(1)}, f32[2,768]{1,0:T(2,128)S(1)}, u32[]{:S(2)}, u32[]{:S(2)}) %collective-permute-start.27) | collective-permute-done | bytes 6176 | tf_op jit(solution)/shard_map/ppermute | solution.py:377
  127.3 4.2 %collective-permute-done.30.rest_1_ = bf16[96,864]{1,0:T(8,128)(2,1)S(1)} collective-permute-done((bf16[96,864]{1,0:T(8,128)(2,1)S(1)}, bf16[96,864]{1,0:T(8,128)(2,1)S(1)}, u32[]{:S(2)}, u32[]{:S(2)}) %collective-permute-start.30) | collective-permute-done | bytes 165920 | tf_op jit(solution)/shard_map/ppermute | solution.py:377
  131.5 2.0 %collective-permute-start.40 = (f32[2,768]{1,0:T(2,128)S(1)}, f32[2,768]{1,0:T(2,128)S(1)}, u32[]{:S(2)}, u32[]{:S(2)}) collective-permute-start(f32[2,768]{1,0:T(2,128)S(1)} %add.34), channel_id=1, source_target_pairs={{0,24},{4,28},{8,16},{12,20},{16,8},{20,12},{24,0},{28,4},{1,25},{... | collective-permute-start | bytes 18440 | tf_op jit(solution)/shard_map/ppermute | solution.py:377
  133.5 2.0 %collective-permute-start.39 = (f32[2,768]{1,0:T(2,128)S(1)}, f32[2,768]{1,0:T(2,128)S(1)}, u32[]{:S(2)}, u32[]{:S(2)}) collective-permute-start(f32[2,768]{1,0:T(2,128)S(1)} %add.34), channel_id=1, source_target_pairs={{0,16},{4,20},{8,24},{12,28},{16,0},{20,4},{24,8},{28,12},{1,17},{... | collective-permute-start | bytes 18440 | tf_op jit(solution)/shard_map/ppermute | solution.py:377
  143.3 7.2 %collective-permute-done.33.rest_1_ = bf16[96,768]{1,0:T(8,128)(2,1)S(1)} collective-permute-done((bf16[96,768]{1,0:T(8,128)(2,1)S(1)}, bf16[96,768]{1,0:T(8,128)(2,1)S(1)}, u32[]{:S(2)}, u32[]{:S(2)}) %collective-permute-start.33) | collective-permute-done | bytes 147488 | tf_op jit(solution)/shard_map/ppermute | solution.py:377
  (121 shorter events, 46.5 us)
Async XLA Ops:
  3.7 11.6 %collective-permute-start.4 = (bf16[128,768]{1,0:T(8,128)(2,1)}, bf16[128,768]{1,0:T(8,128)(2,1)S(1)}, u32[]{:S(2)}, u32[]{:S(2)}) collective-permute-start(bf16[128,768]{1,0:T(8,128)(2,1)} %tokens.1), channel_id=1, source_target_pairs={{0,1},{1,0},{2,3},{3,2},{4,5},{5,4},{6,7},{7,6},{8,9},{9,8},{10,11... | collective-permute-start | bytes 589832 | tf_op jit(solution)/shard_map/ppermute | solution.py:377
  11.9 12.4 %collective-permute-start.1 = (bf16[96,576]{1,0:T(8,128)(2,1)S(1)}, bf16[96,576]{1,0:T(8,128)(2,1)S(1)}, u32[]{:S(2)}, u32[]{:S(2)}) collective-permute-start(bf16[96,576]{1,0:T(8,128)(2,1)S(1)} %copy.25.rest_0_), channel_id=1, source_target_pairs={{0,16},{4,20},{8,24},{12,28},{16,0},{20,4},{24,8},{28,12},{1,17},{... | collective-permute-start | bytes 331784 | tf_op jit(solution)/shard_map/ppermute | solution.py:377
  14.5 9.8 %collective-permute-start.2 = (bf16[96,576]{1,0:T(8,128)(2,1)S(1)}, bf16[96,576]{1,0:T(8,128)(2,1)S(1)}, u32[]{:S(2)}, u32[]{:S(2)}) collective-permute-start(bf16[96,576]{1,0:T(8,128)(2,1)S(1)} %copy.25.rest_0_), channel_id=1, source_target_pairs={{0,24},{4,28},{8,16},{12,20},{16,8},{20,12},{24,0},{28,4},{1,25},{... | collective-permute-start | bytes 331784 | tf_op jit(solution)/shard_map/ppermute | solution.py:377
  24.4 12.0 %collective-permute-start.6 = (bf16[4,96,576]{2,1,0:T(8,128)(2,1)S(1)}, bf16[4,96,576]{2,1,0:T(8,128)(2,1)S(1)}, u32[]{:S(2)}, u32[]{:S(2)}) collective-permute-start(bf16[4,96,576]{2,1,0:T(8,128)(2,1)S(1)} %pad_maximum_fusion.1), channel_id=1, source_target_pairs={{0,4},{4,0},{8,12},{12,8},{16,20},{20,16},{24,28},{28,24},{1,5},{5... | collective-permute-start | bytes 1327112 | tf_op jit(solution)/shard_map/ppermute | solution.py:377
  25.9 10.5 %collective-permute-start.10 = (bf16[96,192]{1,0:T(8,128)(2,1)S(1)}, bf16[96,192]{1,0:T(8,128)(2,1)S(1)}, u32[]{:S(2)}, u32[]{:S(2)}) collective-permute-start(bf16[96,192]{1,0:T(8,128)(2,1)S(1)} %bitcast.51), channel_id=1, source_target_pairs={{0,8},{4,12},{8,0},{12,4},{16,24},{20,28},{24,16},{28,20},{1,9},{5... | collective-permute-start | bytes 110600 | tf_op jit(solution)/shard_map/ppermute | solution.py:377
  36.6 13.8 %collective-permute-start.13 = (bf16[4,96,192]{2,1,0:T(8,128)(2,1)S(1)}, bf16[4,96,192]{2,1,0:T(8,128)(2,1)S(1)}, u32[]{:S(2)}, u32[]{:S(2)}) collective-permute-start(bf16[4,96,192]{2,1,0:T(8,128)(2,1)S(1)} %pad_maximum_fusion.3), channel_id=1, source_target_pairs={{0,4},{4,0},{8,12},{12,8},{16,20},{20,16},{24,28},{28,24},{1,5},{5... | collective-permute-start | bytes 442376 | tf_op jit(solution)/shard_map/ppermute | solution.py:377
  38.1 12.3 %collective-permute-start.7 = (bf16[96,864]{1,0:T(8,128)(2,1)S(1)}, bf16[96,864]{1,0:T(8,128)(2,1)S(1)}, u32[]{:S(2)}, u32[]{:S(2)}) collective-permute-start(bf16[96,864]{1,0:T(8,128)(2,1)S(1)} %pad_maximum_fusion.4.rest_0_), channel_id=1, source_target_pairs={{0,8},{4,12},{8,0},{12,4},{16,24},{20,28},{24,16},{28,20},{1,9},{5... | collective-permute-start | bytes 497672 | tf_op jit(solution)/shard_map/ppermute | solution.py:377
  41.2 14.3 %collective-permute-start.8 = (bf16[96,864]{1,0:T(8,128)(2,1)S(1)}, bf16[96,864]{1,0:T(8,128)(2,1)S(1)}, u32[]{:S(2)}, u32[]{:S(2)}) collective-permute-start(bf16[96,864]{1,0:T(8,128)(2,1)S(1)} %pad_maximum_fusion.4.rest_0_), channel_id=1, source_target_pairs={{0,16},{4,20},{8,24},{12,28},{16,0},{20,4},{24,8},{28,12},{1,17},{... | collective-permute-start | bytes 497672 | tf_op jit(solution)/shard_map/ppermute | solution.py:377
  42.2 13.3 %collective-permute-start.9 = (bf16[96,864]{1,0:T(8,128)(2,1)S(1)}, bf16[96,864]{1,0:T(8,128)(2,1)S(1)}, u32[]{:S(2)}, u32[]{:S(2)}) collective-permute-start(bf16[96,864]{1,0:T(8,128)(2,1)S(1)} %pad_maximum_fusion.4.rest_0_), channel_id=1, source_target_pairs={{0,24},{4,28},{8,16},{12,20},{16,8},{20,12},{24,0},{28,4},{1,25},{... | collective-permute-start | bytes 497672 | tf_op jit(solution)/shard_map/ppermute | solution.py:377
  56.9 17.9 %collective-permute-start.20 = (bf16[4,96,864]{2,1,0:T(8,128)(2,1)S(1)}, bf16[4,96,864]{2,1,0:T(8,128)(2,1)S(1)}, u32[]{:S(2)}, u32[]{:S(2)}) collective-permute-start(bf16[4,96,864]{2,1,0:T(8,128)(2,1)S(1)} %pad_maximum_fusion), channel_id=1, source_target_pairs={{0,4},{4,0},{8,12},{12,8},{16,20},{20,16},{24,28},{28,24},{1,5},{5... | collective-permute-start | bytes 1990664 | tf_op jit(solution)/shard_map/ppermute | solution.py:377
  58.6 12.0 %collective-permute-start.15 = (bf16[256,768]{1,0:T(8,128)(2,1)S(1)}, bf16[256,768]{1,0:T(8,128)(2,1)S(1)}, u32[]{:S(2)}, u32[]{:S(2)}) collective-permute-start(bf16[256,768]{1,0:T(8,128)(2,1)S(1)} %add_convert_fusion.1.own), channel_id=1, source_target_pairs={{0,2},{1,3},{2,0},{3,1},{4,6},{5,7},{6,4},{7,5},{8,10},{9,11},{10,... | collective-permute-start | bytes 1179656 | tf_op jit(solution)/shard_map/ppermute | solution.py:377
  60.2 13.8 %collective-permute-start.17 = (bf16[128,768]{1,0:T(8,128)(2,1)S(1)}, bf16[128,768]{1,0:T(8,128)(2,1)S(1)}, u32[]{:S(2)}, u32[]{:S(2)}) collective-permute-start(bf16[128,768]{1,0:T(8,128)(2,1)S(1)} %copy-done.1), channel_id=1, source_target_pairs={{0,2},{1,3},{2,0},{3,1},{4,6},{5,7},{6,4},{7,5},{8,10},{9,11},{10,... | collective-permute-start | bytes 589832 | tf_op jit(solution)/shard_map/ppermute | solution.py:377
  80.7 11.2 %collective-permute-start.22 = (bf16[256,768]{1,0:T(8,128)(2,1)S(1)}, bf16[256,768]{1,0:T(8,128)(2,1)S(1)}, u32[]{:S(2)}, u32[]{:S(2)}) collective-permute-start(bf16[256,768]{1,0:T(8,128)(2,1)S(1)} %add_convert_fusion.own), channel_id=1, source_target_pairs={{0,2},{1,3},{2,0},{3,1},{4,6},{5,7},{6,4},{7,5},{8,10},{9,11},{10,... | collective-permute-start | bytes 1179656 | tf_op jit(solution)/shard_map/ppermute | solution.py:377
  95.1 18.3 %collective-permute-start.28 = (bf16[4,96,864]{2,1,0:T(8,128)(2,1)S(1)}, bf16[4,96,864]{2,1,0:T(8,128)(2,1)S(1)}, u32[]{:S(2)}, u32[]{:S(2)}) collective-permute-start(bf16[4,96,864]{2,1,0:T(8,128)(2,1)S(1)} %get-tuple-element.138), channel_id=1, source_target_pairs={{0,4},{4,0},{8,12},{12,8},{16,20},{20,16},{24,28},{28,24},{1,5},{5... | collective-permute-start | bytes 1990664 | tf_op jit(solution)/shard_map/ppermute | solution.py:377
  95.7 12.5 %collective-permute-start.36 = (bf16[256,768]{1,0:T(8,128)(2,1)S(1)}, bf16[256,768]{1,0:T(8,128)(2,1)S(1)}, u32[]{:S(2)}, u32[]{:S(2)}) collective-permute-start(bf16[256,768]{1,0:T(8,128)(2,1)S(1)} %get-tuple-element.151), channel_id=1, source_target_pairs={{0,1},{1,0},{2,3},{3,2},{4,5},{5,4},{6,7},{7,6},{8,9},{9,8},{10,11... | collective-permute-start | bytes 1179656 | tf_op jit(solution)/shard_map/ppermute | solution.py:377
  102.8 15.8 %collective-permute-start.35 = (bf16[256,768]{1,0:T(8,128)(2,1)S(1)}, bf16[256,768]{1,0:T(8,128)(2,1)S(1)}, u32[]{:S(2)}, u32[]{:S(2)}) collective-permute-start(bf16[256,768]{1,0:T(8,128)(2,1)S(1)} %get-tuple-element.149), channel_id=1, source_target_pairs={{0,1},{1,0},{2,3},{3,2},{4,5},{5,4},{6,7},{7,6},{8,9},{9,8},{10,11... | collective-permute-start | bytes 1179656 | tf_op jit(solution)/shard_map/ppermute | solution.py:377
  105.1 26.4 %collective-permute-start.24 = (bf16[4,96,768]{2,1,0:T(8,128)(2,1)S(1)}, bf16[4,96,768]{2,1,0:T(8,128)(2,1)S(1)}, u32[]{:S(2)}, u32[]{:S(2)}) collective-permute-start(bf16[4,96,768]{2,1,0:T(8,128)(2,1)S(1)} %get-tuple-element.131), channel_id=1, source_target_pairs={{0,4},{4,0},{8,12},{12,8},{16,20},{20,16},{24,28},{28,24},{1,5},{5... | collective-permute-start | bytes 1769480 | tf_op jit(solution)/shard_map/ppermute | solution.py:377
  106.7 10.5 %collective-permute-start.26 = (f32[2,768]{1,0:T(2,128)S(1)}, f32[2,768]{1,0:T(2,128)S(1)}, u32[]{:S(2)}, u32[]{:S(2)}) collective-permute-start(f32[2,768]{1,0:T(2,128)S(1)} %add.32), channel_id=1, source_target_pairs={{0,2},{1,3},{2,0},{3,1},{4,6},{5,7},{6,4},{7,5},{8,10},{9,11},{10,... | collective-permute-start | bytes 18440 | tf_op jit(solution)/shard_map/ppermute | solution.py:377
  113.6 13.7 %collective-permute-start.29 = (bf16[96,864]{1,0:T(8,128)(2,1)S(1)}, bf16[96,864]{1,0:T(8,128)(2,1)S(1)}, u32[]{:S(2)}, u32[]{:S(2)}) collective-permute-start(bf16[96,864]{1,0:T(8,128)(2,1)S(1)} %get-tuple-element.140), channel_id=1, source_target_pairs={{0,8},{4,12},{8,0},{12,4},{16,24},{20,28},{24,16},{28,20},{1,9},{5... | collective-permute-start | bytes 497672 | tf_op jit(solution)/shard_map/ppermute | solution.py:377
  116.1 15.5 %collective-permute-start.30 = (bf16[96,864]{1,0:T(8,128)(2,1)S(1)}, bf16[96,864]{1,0:T(8,128)(2,1)S(1)}, u32[]{:S(2)}, u32[]{:S(2)}) collective-permute-start(bf16[96,864]{1,0:T(8,128)(2,1)S(1)} %get-tuple-element.141), channel_id=1, source_target_pairs={{0,16},{4,20},{8,24},{12,28},{16,0},{20,4},{24,8},{28,12},{1,17},{... | collective-permute-start | bytes 497672 | tf_op jit(solution)/shard_map/ppermute | solution.py:377
  117.2 14.4 %collective-permute-start.31 = (bf16[96,864]{1,0:T(8,128)(2,1)S(1)}, bf16[96,864]{1,0:T(8,128)(2,1)S(1)}, u32[]{:S(2)}, u32[]{:S(2)}) collective-permute-start(bf16[96,864]{1,0:T(8,128)(2,1)S(1)} %get-tuple-element.142), channel_id=1, source_target_pairs={{0,24},{4,28},{8,16},{12,20},{16,8},{20,12},{24,0},{28,4},{1,25},{... | collective-permute-start | bytes 497672 | tf_op jit(solution)/shard_map/ppermute | solution.py:377
  125.8 16.3 %collective-permute-start.37 = (bf16[256,768]{1,0:T(8,128)(2,1)S(1)}, bf16[256,768]{1,0:T(8,128)(2,1)S(1)}, u32[]{:S(2)}, u32[]{:S(2)}) collective-permute-start(bf16[256,768]{1,0:T(8,128)(2,1)S(1)} %pad_maximum_fusion.2), channel_id=1, source_target_pairs={{0,2},{1,3},{2,0},{3,1},{4,6},{5,7},{6,4},{7,5},{8,10},{9,11},{10,... | collective-permute-start | bytes 1179656 | tf_op jit(solution)/shard_map/ppermute | solution.py:377
  138.7 11.8 %collective-permute-start.33 = (bf16[96,768]{1,0:T(8,128)(2,1)S(1)}, bf16[96,768]{1,0:T(8,128)(2,1)S(1)}, u32[]{:S(2)}, u32[]{:S(2)}) collective-permute-start(bf16[96,768]{1,0:T(8,128)(2,1)S(1)} %get-tuple-element.146), channel_id=1, source_target_pairs={{0,16},{4,20},{8,24},{12,28},{16,0},{20,4},{24,8},{28,12},{1,17},{... | collective-permute-start | bytes 442376 | tf_op jit(solution)/shard_map/ppermute | solution.py:377
  139.7 10.9 %collective-permute-start.34 = (bf16[96,768]{1,0:T(8,128)(2,1)S(1)}, bf16[96,768]{1,0:T(8,128)(2,1)S(1)}, u32[]{:S(2)}, u32[]{:S(2)}) collective-permute-start(bf16[96,768]{1,0:T(8,128)(2,1)S(1)} %get-tuple-element.147), channel_id=1, source_target_pairs={{0,24},{4,28},{8,16},{12,20},{16,8},{20,12},{24,0},{28,4},{1,25},{... | collective-permute-start | bytes 442376 | tf_op jit(solution)/shard_map/ppermute | solution.py:377
  (27 other events, 119.3 us)

commit v3 on v2

--- a/solution.py
+++ b/solution.py
@@ -35,7 +35,7 @@
         out_specs=tuple(pl.BlockSpec(memory_space=pltpu.VMEM) for _ in outs),
         scratch_shapes=list(scratch),
         compiler_params=pltpu.CompilerParams(vmem_limit_bytes=48 * 1024 * 1024),
-        cost_estimate=pl.CostEstimate(flops=flops, bytes_accessed=size, transcendentals=0),
+        cost_estimate=pl.CostEstimate(flops=1, bytes_accessed=1, transcendentals=0),
     )(*scalars, *args)
 
 
@@ -75,6 +75,11 @@
 def head_lanes(shape_of, head):
     lane = lax.broadcasted_iota(jnp.int32, shape_of, 1)
     return (lane >= head * HEAD_DIM) & (lane < (head + 1) * HEAD_DIM)
+
+
+def pack_kernel(wide, tall, packed):
+    parts = [wide[j] for j in range(wide.shape[0])]
+    packed[...] = jnp.concatenate(parts + [tall[...].T], axis=1)
 
 
 def prepare_kernel(ids, first, t0, t1, t2, t3, gain, freq, n1, cosine, sine):
@@ -93,19 +98,23 @@
         sine[b * WINDOW : (b + 1) * WINDOW, :] = jnp.sin(angle) * sign
 
 
-def put_pieces(ids, offsets, pieces, whole, rows):
-    if offsets is None:
-        whole[...] = pieces[0][...]
-        return
-    for offset, piece in zip(offsets, pieces):
-        whole[rows_of(jnp.bitwise_xor(ids[4], offset), rows), :] = piece[...]
+def put_pieces(ids, offsets, pieces, left, right, rows):
+    cut = left.shape[1]
+    for j, piece in enumerate(pieces):
+        if offsets is None:
+            at = slice(None)
+        else:
+            at = rows_of(jnp.bitwise_xor(ids[4], offsets[j]), rows)
+        value = piece[...]
+        left[at, :] = value[:, :cut]
+        right[at, :] = value[:, cut:]
 
 
 def attend_kernel(offsets, n_pieces, rows, ids, count, first, n1, cosine, sine, *rest):
     pieces = rest[:n_pieces]
-    q_out, k_out, v_out, probs_out, att_out, whole = rest[n_pieces : n_pieces + 6]
-    k_pad, v_pad = rest[n_pieces + 6 :]
-    put_pieces(ids, offsets, pieces, whole, rows)
+    q_out, k_out, v_out, probs_out, att_out, whole, out_w = rest[n_pieces : n_pieces + 7]
+    k_pad, v_pad = rest[n_pieces + 7 :]
+    put_pieces(ids, offsets, pieces, whole, out_w, rows)
     half = WINDOW // 2
     width = q_out.shape[1]
     heads = width // HEAD_DIM
@@ -161,23 +170,11 @@
         att_out[rows_b, :] = mixed.astype(BF)
 
 
-def collect_kernel(offsets, n_pieces, rows, units2, ids, *rest):
-    pieces = rest[:n_pieces]
-    in_w, down_w = rest[n_pieces:]
-    for j, piece in enumerate(pieces):
-        if offsets is None:
-            at = slice(None)
-        else:
-            at = rows_of(jnp.bitwise_xor(ids[4], offsets[j]), rows)
-        value = piece[...]
-        in_w[at, :] = value[:, :units2]
-        down_w[at, :] = value[:, units2:]
-
-
-def project_kernel(offsets, n_pieces, rows, ids, att, *rest):
-    pieces = rest[:n_pieces]
-    send, keep, out_w = rest[n_pieces:]
-    put_pieces(ids, offsets, pieces, out_w, rows)
+def collect_kernel(offsets, n_pieces, rows, ids, *rest):
+    put_pieces(ids, offsets, rest[:n_pieces], rest[n_pieces], rest[n_pieces + 1], rows)
+
+
+def project_kernel(ids, att, out_w, send, keep):
     for i in range(4):
         part = dot(att[rows_of(ids[i]), :], out_w[...], NT)
         at = slice((i % 2) * WINDOW, (i % 2 + 1) * WINDOW)
@@ -351,14 +348,43 @@
         other[...] = (keep[k + 1].astype(F32) + got[k + 1].astype(F32)).astype(BF)
 
 
-def deliver_kernel(first, *rest):
+EXTRA = 8
+
+
+def merge_gains_kernel(keep, got, gains, gains_got, first, *others):
+    rows, columns = keep.shape[1:]
+    first[:rows, :] = keep[0].astype(F32) + got[0].astype(F32)
+    total = gains[...] + gains_got[...]
+    high = total.astype(BF).astype(F32)
+    low = (total - high).astype(BF).astype(F32)
+    first[rows:, :] = jnp.concatenate([total, jnp.zeros((EXTRA - 2, columns), F32)], axis=0)
+    coded = jnp.concatenate([high, low, jnp.zeros((EXTRA - 4, columns), F32)], axis=0).astype(BF)
+    for k, other in enumerate(others):
+        other[:rows, :] = (keep[k + 1].astype(F32) + got[k + 1].astype(F32)).astype(BF)
+        other[rows:, :] = coded
+
+
+def deliver_kernel(with_gains, first, *rest):
+    if with_gains:
+        rows = first.shape[0] - EXTRA
+        parts = rest[:-4]
+        gains = first[rows : rows + 2, :]
+        for part in parts:
+            coded = part[rows:, :].astype(F32)
+            gains = gains + coded[0:2, :] + coded[2:4, :]
+        rest[-4][...] = gains[0:1, :]
+        rest[-3][...] = gains[1:2, :]
+        total = first[:rows, :]
+        for part in parts:
+            total = total + part[:rows, :].astype(F32)
+    else:
+        total = first[...]
+        for part in rest[:-2]:
+            total = total + part[...].astype(F32)
     wide, turned = rest[-2:]
-    total = first[...]
-    for part in rest[:-2]:
-        total = total + part[...].astype(F32)
-    _, count, width = wide.shape
+    count, _, width = wide.shape
     for j in range(count):
-        wide[:, j, :] = total[:, j * width : (j + 1) * width]
+        wide[j] = total[:, j * width : (j + 1) * width]
     turned[...] = total[:, count * width :].T
 
 
@@ -410,25 +436,28 @@
     def picked(own, near, far):
         return (own, *near, *far) if slots else tuple(near)
 
-    def merge(keep, got):
+    def merge(keep, got, gains=()):
         _, rows, columns = keep.shape
+        rows += EXTRA if gains else 0
         return call(
-            merge_kernel,
+            merge_gains_kernel if gains else merge_kernel,
             (shape(rows, columns, dtype=F32),) + (shape(rows, columns),) * (slots - 1),
-            (keep, got),
+            (keep, got, *gains),
         )
 
-    def deliver(parts, count):
+    def deliver(parts, count, with_gains=False):
         columns = parts[0].shape[1]
         each = columns // (count + 1)
         if not slots:
             total = parts[0]
             return total[:, : count * each].reshape(shard, count, each), total[:, count * each :].T
-        return call(
-            deliver_kernel,
-            (shape(shard, count, each, dtype=F32), shape(each, shard, dtype=F32)),
+        *gains, wide, tall = call(
+            functools.partial(deliver_kernel, with_gains),
+            ((shape(1, columns, dtype=F32),) * 2 if with_gains else ())
+            + (shape(count, shard, each, dtype=F32), shape(each, shard, dtype=F32)),
             parts,
         )
+        return *(gain.reshape(columns) for gain in gains), jnp.transpose(wide, (1, 0, 2)), tall
 
     def slot_shapes(columns):
         if not slots:
@@ -443,53 +472,61 @@
     offsets = tuple(range(0, n_dp, 2)) + tuple(range(1, n_dp, 2)) if slots else None
     pin = lax.optimization_barrier
 
-    qkv_own = w_qkv.reshape(shard, 3 * head_width)
-    qkv_near = along(qkv_own)
-    token_blocks = [tokens, across(tokens), core(tokens)]
-    token_blocks.append(core(token_blocks[1]))
+    def pack(wide, tall):
+        count, _, each = wide.shape
+        if not slots:
+            return jnp.concatenate([*wide, tall.T], axis=1)
+        return call(pack_kernel, (shape(shard, count * each + tall.shape[0]),), (wide, tall))[0]
+
+    qkv_own = pack(jnp.transpose(w_qkv, (1, 0, 2)), w_out)
+    qkv_near, tokens_across = pin((along(qkv_own), across(tokens)))
+    token_blocks = (tokens, tokens_across, core(tokens), core(tokens_across))
+    qkv_far = aside([qkv_own] + qkv_near)
     n1, cosine, sine = call(
         prepare_kernel,
         (shape(total_rows, width), shape(total_rows, 128, dtype=F32), shape(total_rows, 128, dtype=F32)),
-        tuple(token_blocks) + (gain_one, freq),
+        token_blocks + (gain_one, freq),
         (ids, block_first),
     )
-    out_own = w_out.T
-    unit_own = jnp.concatenate([w_in.reshape(shard, 2 * units), w_down.T], axis=1)
-    qkv_near, n1, out_own, unit_own, cot = pin((qkv_near, n1, out_own, unit_own, cotangent))
-    qkv_far = aside([qkv_own] + qkv_near)
-    out_near = along(out_own)
+    unit_own = pack(jnp.transpose(w_in, (1, 0, 2)), w_down)
+    unit_own, cot, _ = pin((unit_own, cotangent, qkv_near))
     unit_near = along(unit_own)
-    cot_blocks = [cotangent, across(cot), core(cot)]
-    cot_blocks.append(core(cot_blocks[1]))
-    cot_blocks = tuple(cot_blocks)
+    cot_across = across(cot)
+    qkv_far, n1, cot_across = pin((qkv_far, n1, cot_across))
+    cot_blocks = (cotangent, cot_across, core(cot), core(cot_across))
     qkv_pieces = picked(qkv_own, qkv_near, qkv_far)
-    out_near, _ = pin((out_near, qkv_far))
-    out_far = aside([out_own] + out_near)
-    out_pieces = picked(out_own, out_near, out_far)
     flat = shape(total_rows, head_width)
-    query, keys, values, probs, attended, qkv_w = call(
+    query, keys, values, probs, attended, qkv_w, out_w = call(
         functools.partial(attend_kernel, offsets, len(qkv_pieces), shard),
-        (flat, flat, flat, shape(heads, total_rows, 2 * WINDOW), flat, shape(width, 3 * head_width)),
+        (
+            flat,
+            flat,
+            flat,
+            shape(heads, total_rows, 2 * WINDOW),
+            flat,
+            shape(width, 3 * head_width),
+            shape(width, head_width),
+        ),
         (n1, cosine, sine) + qkv_pieces,
         (ids, block_count, block_first),
         [pltpu.VMEM((total_rows + WINDOW, head_width), BF)] * 2,
         flops=2 * total_rows * width * 3 * head_width,
     )
-    attended, unit_near, out_pieces = pin((attended, unit_near, out_pieces))
+    attended, unit_near = pin((attended, unit_near))
     unit_far = aside([unit_own] + unit_near)
     unit_pieces = picked(unit_own, unit_near, unit_far)
     in_w, down_w = call(
-        functools.partial(collect_kernel, offsets, len(unit_pieces), shard, 2 * units),
+        functools.partial(collect_kernel, offsets, len(unit_pieces), shard),
         (shape(width, 2 * units), shape(width, units)),
         unit_pieces,
         (ids,),
     )
     pair_f32 = shape(pair_rows, width, dtype=F32)
     pair_bf = shape(pair_rows, width)
-    a_send, a_keep, out_w = call(
-        functools.partial(project_kernel, offsets, len(out_pieces), shard),
-        (pair_bf, pair_f32, shape(width, head_width)),
-        (attended,) + out_pieces,
+    a_send, a_keep = call(
+        project_kernel,
+        (pair_bf, pair_f32),
+        (attended, out_w),
         (ids,),
         flops=2 * total_rows * width * head_width,
     )
@@ -518,8 +555,7 @@
         flops=2 * total_rows * width * 4 * units,
     )
     b_core = core(b_send)
-    if slots:
-        in_parts = merge(in_keep, dp(in_send, bit=1))
+    u_got, in_keep = pin((u_got, in_keep))
     gh, gy, gain_part_two = call(
         residual_kernel,
         (shape(WINDOW, width, dtype=F32), pair_bf, shape(1, width, dtype=F32)),
@@ -541,6 +577,9 @@
         ],
         flops=2 * total_rows * width * 3 * head_width,
     )
+    if slots:
+        g_raw, in_got = pin((g_raw, dp(in_send, bit=1)))
+        in_parts = merge(in_keep, in_got)
     att_send, att_keep = call(
         functools.partial(attend_grads_kernel, slots, shard),
         slot_shapes(4 * head_width),
@@ -549,6 +588,7 @@
         [pltpu.VMEM((width, 4 * head_width), F32)],
         flops=2 * total_rows * width * 4 * head_width,
     )
+    g_raw, att_keep = pin((g_raw, att_keep))
     g_send, g_keep, gains = call(
         first_back_kernel,
         (pair_bf, pair_f32, shape(2, width, dtype=F32)),
@@ -557,6 +597,9 @@
         flops=2 * total_rows * width * 3 * head_width,
     )
     g_core = core(g_send)
+    if slots:
+        gains = gains + core(gains)
+        gains, g_core, b_core = pin((gains + across(gains), g_core, b_core))
     back = jnp.concatenate(
         [
             (g_keep[WINDOW:] + g_core[WINDOW:].astype(F32)).astype(BF),
@@ -570,16 +613,10 @@
         (g_keep, g_core, b_keep, b_core, across(back), h, tokens, gain_one, gh),
     )
     if slots:
-        att_got = dp(att_send, bit=1)
         in_parts = (in_parts[0], *(dp(in_parts[k], bit=2 * k) for k in range(1, slots)))
-        gains = gains + core(gains)
-        gains = gains + across(gains)
-        gains = gains + dp(gains, bit=1)
-        att_got, gains, in_parts = pin((att_got, gains, in_parts))
-        att_parts = merge(att_keep, att_got)
+        att_got, gains_got, in_parts = pin((dp(att_send, bit=1), dp(gains, bit=1), in_parts))
+        att_parts = merge(att_keep, att_got, (gains, gains_got))
         att_parts = (att_parts[0], *(dp(att_parts[k], bit=2 * k) for k in range(1, slots)))
-        for part in [dp(gains, bit=2 * k) for k in range(1, slots)]:
-            gains = gains + part
     else:
         gains = lax.psum(gains, ("dp", "tensor"))
         in_parts = (lax.psum_scatter(in_send, "dp", scatter_dimension=0, tiled=True),)
@@ -588,7 +625,10 @@
     att_parts, mixed, input_grad, in_grad, down_grad = pin(
         (att_parts, mixed, input_grad, in_grad, down_grad)
     )
-    qkv_grad, out_grad = deliver(att_parts, 3)
+    if slots:
+        *gains, qkv_grad, out_grad = deliver(att_parts, 3, True)
+    else:
+        qkv_grad, out_grad = deliver(att_parts, 3)
     return (mixed, input_grad, gains[0], qkv_grad, out_grad, gains[1], in_grad, down_grad)
 
 

time: 152 us -> 134 us (0.88)
  starting transfers between devices: 46.8 us -> 36.3 us
  waiting for transfers between devices: 70.4 us -> 61.7 us
    ppermute x41 -> x34, starting transfers between devices: 46.8 us -> 36.3 us  [swap(): return lax.ppermute(values, axis, [(i, i ^ bit) for i in range(size)])]
    ppermute x41 -> x34, waiting for transfers between devices: 70.4 us -> 61.7 us  [swap(): return lax.ppermute(values, axis, [(i, i ^ bit) for i in range(size)])]
    pallas_call x16 -> x18, Pallas kernels: 28.6 us -> 28.8 us  [call(): pl.pallas_call(kernel, out_shape=tuple(outs), in_specs=[pl.BlockSpec(memo...]
  transfers between devices with their start and end apart: 41 -> 34, of which waited for: 14 -> 15; matrix products, arithmetic and copies ran while one was open for 2% -> 0% of each run, Pallas kernels for 15% -> 18%
where the time goes in v3:
time: 134 us
  waiting for transfers between devices  61.7 us (46%)
  starting transfers between devices  36.3 us (27%)
  Pallas kernels  28.8 us (21%)
  local copies, waits for them, and re-layouts  4.23 us (3%)
  other arithmetic  1.7 us (1%)
    ppermute x34, waiting for transfers between devices, swap(): return lax.ppermute(values, axis, [(i, i ^ bit) for i in range(size)])  61.7 us
    ppermute x34, starting transfers between devices, swap(): return lax.ppermute(values, axis, [(i, i ^ bit) for i in range(size)])  36.3 us
    pallas_call x18, Pallas kernels, call(): pl.pallas_call(kernel, out_shape=tuple(outs), in_specs=[pl.BlockSpec(memo...  28.8 us
    unnamed x24, local copies, waits for them, and re-layouts  4.04 us
  transfers between devices with their start and end apart: 34, of which 15 were waited for; matrix products, arithmetic and copies ran while one was open for 0% of the time, Pallas kernels for 18%

profile of v3, /device:TPU:0, one launch (start us, length us, event | category | flops | bytes accessed | tf_op | source)
XLA Modules:
  0.0 133.7 jit_solution(13228161903658620092)
XLA Ops:
  0.6 3.0 %collective-permute-start.3 = (bf16[128,768]{1,0:T(8,128)(2,1)}, bf16[128,768]{1,0:T(8,128)(2,1)S(1)}, u32[]{:S(2)}, u32[]{:S(2)}) collective-permute-start(bf16[128,768]{1,0:T(8,128)(2,1)} %tokens.1), channel_id=1, source_target_pairs={{0,2},{1,3},{2,0},{3,1},{4,6},{5,7},{6,4},{7,5},{8,10},{9,11},{10,... | collective-permute-start | bytes 589832 | tf_op jit(solution)/shard_map/ppermute | solution.py:403
  5.5 3.7 %collective-permute-start.2 = (bf16[96,768]{1,0:T(8,128)(2,1)S(1)}, bf16[96,768]{1,0:T(8,128)(2,1)S(1)}, u32[]{:S(2)}, u32[]{:S(2)}) collective-permute-start(bf16[96,768]{1,0:T(8,128)(2,1)S(1)} %shard_map.170.rest_0_), channel_id=1, source_target_pairs={{0,24},{4,28},{8,16},{12,20},{16,8},{20,12},{24,0},{28,4},{1,25},{... | collective-permute-start | bytes 442376 | tf_op jit(solution)/shard_map/ppermute | solution.py:403
  10.0 4.2 %collective-permute-done.2.rest_3_ = bf16[96,768]{1,0:T(8,128)(2,1)S(1)} collective-permute-done((bf16[96,768]{1,0:T(8,128)(2,1)S(1)}, bf16[96,768]{1,0:T(8,128)(2,1)S(1)}, u32[]{:S(2)}, u32[]{:S(2)}) %collective-permute-start.2) | collective-permute-done | bytes 147488 | tf_op jit(solution)/shard_map/ppermute | solution.py:403
  14.2 7.2 %collective-permute-done.1.rest_2_ = bf16[96,768]{1,0:T(8,128)(2,1)S(1)} collective-permute-done((bf16[96,768]{1,0:T(8,128)(2,1)S(1)}, bf16[96,768]{1,0:T(8,128)(2,1)S(1)}, u32[]{:S(2)}, u32[]{:S(2)}) %collective-permute-start.1) | collective-permute-done | bytes 147488 | tf_op jit(solution)/shard_map/ppermute | solution.py:403
  24.6 2.5 %collective-permute-start.10 = (bf16[96,864]{1,0:T(8,128)(2,1)S(1)}, bf16[96,864]{1,0:T(8,128)(2,1)S(1)}, u32[]{:S(2)}, u32[]{:S(2)}) collective-permute-start(bf16[96,864]{1,0:T(8,128)(2,1)S(1)} %shard_map.172.rest_0_), channel_id=1, source_target_pairs={{0,24},{4,28},{8,16},{12,20},{16,8},{20,12},{24,0},{28,4},{1,25},{... | collective-permute-start | bytes 497672 | tf_op jit(solution)/shard_map/ppermute | solution.py:403
  27.1 1.9 %collective-permute-start.8 = (bf16[96,864]{1,0:T(8,128)(2,1)S(1)}, bf16[96,864]{1,0:T(8,128)(2,1)S(1)}, u32[]{:S(2)}, u32[]{:S(2)}) collective-permute-start(bf16[96,864]{1,0:T(8,128)(2,1)S(1)} %shard_map.172.rest_0_), channel_id=1, source_target_pairs={{0,8},{4,12},{8,0},{12,4},{16,24},{20,28},{24,16},{28,20},{1,9},{5... | collective-permute-start | bytes 497672 | tf_op jit(solution)/shard_map/ppermute | solution.py:403
  29.5 2.0 %shard_map.171 = (bf16[512,768]{1,0:T(8,128)(2,1)S(1)}, f32[512,128]{1,0:T(8,128)S(1)}, f32[512,128]{1,0:T(8,128)S(1)}) custom-call(s32[5]{0:T(128)S(1)} %stack.53.ids, s32[4]{0:T(128)S(1)} %copy-done.5, bf16[128,768]{1,0:T(8,128)(2,1)S(1)} %copy-done, bf16[128,768]{1,0:T(8,128)(2,1)S(1)} %collective-permute-done.3.t1, ...), custom_call_target="tpu_custom_call" | custom-call | flops 1 | bytes 1 | tf_op jit(solution)/shard_map/pallas_call | solution.py:30
  31.5 4.4 %collective-permute-done.4 = bf16[4,96,768]{2,1,0:T(8,128)(2,1)S(1)} collective-permute-done((bf16[4,96,768]{2,1,0:T(8,128)(2,1)S(1)}, bf16[4,96,768]{2,1,0:T(8,128)(2,1)S(1)}, u32[]{:S(2)}, u32[]{:S(2)}) %collective-permute-start.4) | collective-permute-done | bytes 589856 | tf_op jit(solution)/shard_map/ppermute | solution.py:403
  36.6 6.1 %shard_map.173 = (bf16[512,192]{1,0:T(8,128)(2,1)S(1)}, bf16[512,192]{1,0:T(8,128)(2,1)S(1)}, bf16[512,192]{1,0:T(8,128)(2,1)S(1)}, bf16[3,512,256]{2,1,0:T(8,12...) custom-call(s32[5]{0:T(128)S(1)} %stack.53.ids, ...), custom_call_target="tpu_custom_call" | custom-call | flops 1 | bytes 1 | tf_op jit(solution)/shard_map/pallas_call | solution.py:30
  46.5 10.7 %collective-permute-done.12.received = bf16[256,768]{1,0:T(8,128)(2,1)S(1)} collective-permute-done((bf16[256,768]{1,0:T(8,128)(2,1)S(1)}, bf16[256,768]{1,0:T(8,128)(2,1)S(1)}, u32[]{:S(2)}, u32[]{:S(2)}) %collective-permute-start.12) | collective-permute-done | bytes 393248 | tf_op jit(solution)/shard_map/ppermute | solution.py:403
  58.1 3.9 %collective-permute-done.16 = bf16[4,96,864]{2,1,0:T(8,128)(2,1)S(1)} collective-permute-done((bf16[4,96,864]{2,1,0:T(8,128)(2,1)S(1)}, bf16[4,96,864]{2,1,0:T(8,128)(2,1)S(1)}, u32[]{:S(2)}, u32[]{:S(2)}) %collective-permute-start.16) | collective-permute-done | bytes 663584 | tf_op jit(solution)/shard_map/ppermute | solution.py:403
  63.0 3.0 %shard_map.177 = (bf16[256,768]{1,0:T(8,128)(2,1)S(1)}, f32[256,768]{1,0:T(8,128)S(1)}, bf16[512,576]{1,0:T(8,128)(2,1)S(1)}, bf16[512,288]{1,0:T(8,128)(2,1)S(1)}) custom-call(bf16[256,768]{1,0:T(8,128)(2,1)S(1)} %get-tuple-element.114.n2, bf16[256,768]{1,0:T(8,128)(2,1)S(1)} %collective-permute-done.13.n2_far, bf16[128,768]{1,0:T(8,128)(2,1)S(1)} %copy-done.1, ...), custom_call_target="tpu_custom_call" | custom-call | flops 1 | bytes 1 | tf_op jit(solution)/shard_map/pallas_call | solution.py:30
  68.5 2.5 %shard_map.178 = (bf16[4,96,864]{2,1,0:T(8,128)(2,1)S(1)}, bf16[4,96,864]{2,1,0:T(8,128)(2,1)S(1)}, bf16[256,768]{1,0:T(8,128)(2,1)S(1)}, f32[256,768]{1,0:T(8,128)S(1)}) custom-call(s32[5]{0:T(128)S(1)} %stack.53.ids, bf16[256,768]{1,0:T(8,128)(2,1)S(1)} %get-tuple-element.114.n2, bf16[256,768]{1,0:T(8,128)(2,1)S(1)} %collective-permute-done.13.n2_far, ...), custom_call_target="tpu_custom_call" | custom-call | flops 1 | bytes 1 | tf_op jit(solution)/shard_map/pallas_call | solution.py:30
  72.6 6.5 %collective-permute-done.18.received = bf16[256,768]{1,0:T(8,128)(2,1)S(1)} collective-permute-done((bf16[256,768]{1,0:T(8,128)(2,1)S(1)}, bf16[256,768]{1,0:T(8,128)(2,1)S(1)}, u32[]{:S(2)}, u32[]{:S(2)}) %collective-permute-start.18) | collective-permute-done | bytes 393248 | tf_op jit(solution)/shard_map/ppermute | solution.py:403
  81.6 4.9 %shard_map.180.g_raw = bf16[512,576]{1,0:T(8,128)(2,1)S(1)} custom-call(s32[5]{0:T(128)S(1)} %stack.53.ids, bf16[256,768]{1,0:T(8,128)(2,1)S(1)} %get-tuple-element.128.gy, bf16[256,768]{1,0:T(8,128)(2,1)S(1)} %collective-permute-done.19.gy_far, bf16[768,192]{1,0:T(8,128)(2,1)S(1)} %get-tuple-element.111.out_w, ...), custom_call_target="tpu_custom_call" | custom-call | flops 1 | bytes 1 | tf_op jit(solution)/shard_map/pallas_call | solution.py:30
  86.5 1.9 %collective-permute-done.20.got = bf16[4,96,864]{2,1,0:T(8,128)(2,1)S(1)} collective-permute-done((bf16[4,96,864]{2,1,0:T(8,128)(2,1)S(1)}, bf16[4,96,864]{2,1,0:T(8,128)(2,1)S(1)}, u32[]{:S(2)}, u32[]{:S(2)}) %collective-permute-start.20) | collective-permute-done | bytes 663584 | tf_op jit(solution)/shard_map/ppermute | solution.py:403
  90.1 1.9 %shard_map.182 = (bf16[256,768]{1,0:T(8,128)(2,1)S(1)}, f32[256,768]{1,0:T(8,128)S(1)}, f32[2,768]{1,0:T(2,128)S(1)}) custom-call(s32[5]{0:T(128)S(1)} %stack.53.ids, bf16[512,576]{1,0:T(8,128)(2,1)S(1)} %shard_map.180.g_raw, bf16[768,576]{1,0:T(8,128)(2,1)S(1)} %get-tuple-element.139.qkv_w, bf16[512,768]{1,0:T(8,128)(2,1)S(1)} %get-tuple-element.101.n1, ...), custom_call_target="tpu_custom_call" | custom-call | flops 1 | bytes 1 | tf_op jit(solution)/shard_map/pallas_call | solution.py:30
  99.4 2.6 %collective-permute-start.28 = (bf16[96,864]{1,0:T(8,128)(2,1)S(1)}, bf16[96,864]{1,0:T(8,128)(2,1)S(1)}, u32[]{:S(2)}, u32[]{:S(2)}) collective-permute-start(bf16[96,864]{1,0:T(8,128)(2,1)S(1)} %get-tuple-element.149), channel_id=1, source_target_pairs={{0,16},{4,20},{8,24},{12,28},{16,0},{20,4},{24,8},{28,12},{1,17},{... | collective-permute-start | bytes 497672 | tf_op jit(solution)/shard_map/ppermute | solution.py:403
  102.0 1.8 %collective-permute-start.29 = (bf16[96,864]{1,0:T(8,128)(2,1)S(1)}, bf16[96,864]{1,0:T(8,128)(2,1)S(1)}, u32[]{:S(2)}, u32[]{:S(2)}) collective-permute-start(bf16[96,864]{1,0:T(8,128)(2,1)S(1)} %get-tuple-element.150), channel_id=1, source_target_pairs={{0,24},{4,28},{8,16},{12,20},{16,8},{20,12},{24,0},{28,4},{1,25},{... | collective-permute-start | bytes 497672 | tf_op jit(solution)/shard_map/ppermute | solution.py:403
  103.8 3.7 %collective-permute-done.27.rest_0_ = bf16[96,864]{1,0:T(8,128)(2,1)S(1)} collective-permute-done((bf16[96,864]{1,0:T(8,128)(2,1)S(1)}, bf16[96,864]{1,0:T(8,128)(2,1)S(1)}, u32[]{:S(2)}, u32[]{:S(2)}) %collective-permute-start.27) | collective-permute-done | bytes 165920 | tf_op jit(solution)/shard_map/ppermute | solution.py:403
  109.0 5.4 %collective-permute-done.28.rest_1_ = bf16[96,864]{1,0:T(8,128)(2,1)S(1)} collective-permute-done((bf16[96,864]{1,0:T(8,128)(2,1)S(1)}, bf16[96,864]{1,0:T(8,128)(2,1)S(1)}, u32[]{:S(2)}, u32[]{:S(2)}) %collective-permute-start.28) | collective-permute-done | bytes 165920 | tf_op jit(solution)/shard_map/ppermute | solution.py:403
  114.5 2.7 %collective-permute-start.30 = (bf16[104,768]{1,0:T(8,128)(2,1)S(1)}, bf16[104,768]{1,0:T(8,128)(2,1)S(1)}, u32[]{:S(2)}, u32[]{:S(2)}) collective-permute-start(bf16[104,768]{1,0:T(8,128)(2,1)S(1)} %get-tuple-element.154), channel_id=1, source_target_pairs={{0,8},{4,12},{8,0},{12,4},{16,24},{20,28},{24,16},{28,20},{1,9},{5... | collective-permute-start | bytes 479240 | tf_op jit(solution)/shard_map/ppermute | solution.py:403
  117.9 1.8 %collective-permute-start.32 = (bf16[104,768]{1,0:T(8,128)(2,1)S(1)}, bf16[104,768]{1,0:T(8,128)(2,1)S(1)}, u32[]{:S(2)}, u32[]{:S(2)}) collective-permute-start(bf16[104,768]{1,0:T(8,128)(2,1)S(1)} %get-tuple-element.156), channel_id=1, source_target_pairs={{0,24},{4,28},{8,16},{12,20},{16,8},{20,12},{24,0},{28,4},{1,25},{... | collective-permute-start | bytes 479240 | tf_op jit(solution)/shard_map/ppermute | solution.py:403
  122.1 8.6 %collective-permute-done.31.rest_1_ = bf16[104,768]{1,0:T(8,128)(2,1)S(1)} collective-permute-done((bf16[104,768]{1,0:T(8,128)(2,1)S(1)}, bf16[104,768]{1,0:T(8,128)(2,1)S(1)}, u32[]{:S(2)}, u32[]{:S(2)}) %collective-permute-start.31) | collective-permute-done | bytes 159776 | tf_op jit(solution)/shard_map/ppermute | solution.py:403
  (101 shorter events, 35.6 us)
Async XLA Ops:
  0.6 20.8 %collective-permute-start.3 = (bf16[128,768]{1,0:T(8,128)(2,1)}, bf16[128,768]{1,0:T(8,128)(2,1)S(1)}, u32[]{:S(2)}, u32[]{:S(2)}) collective-permute-start(bf16[128,768]{1,0:T(8,128)(2,1)} %tokens.1), channel_id=1, source_target_pairs={{0,2},{1,3},{2,0},{3,1},{4,6},{5,7},{6,4},{7,5},{8,10},{9,11},{10,... | collective-permute-start | bytes 589832 | tf_op jit(solution)/shard_map/ppermute | solution.py:403
  5.5 8.7 %collective-permute-start.2 = (bf16[96,768]{1,0:T(8,128)(2,1)S(1)}, bf16[96,768]{1,0:T(8,128)(2,1)S(1)}, u32[]{:S(2)}, u32[]{:S(2)}) collective-permute-start(bf16[96,768]{1,0:T(8,128)(2,1)S(1)} %shard_map.170.rest_0_), channel_id=1, source_target_pairs={{0,24},{4,28},{8,16},{12,20},{16,8},{20,12},{24,0},{28,4},{1,25},{... | collective-permute-start | bytes 442376 | tf_op jit(solution)/shard_map/ppermute | solution.py:403
  9.2 12.2 %collective-permute-start.1 = (bf16[96,768]{1,0:T(8,128)(2,1)S(1)}, bf16[96,768]{1,0:T(8,128)(2,1)S(1)}, u32[]{:S(2)}, u32[]{:S(2)}) collective-permute-start(bf16[96,768]{1,0:T(8,128)(2,1)S(1)} %shard_map.170.rest_0_), channel_id=1, source_target_pairs={{0,16},{4,20},{8,24},{12,28},{16,0},{20,4},{24,8},{28,12},{1,17},{... | collective-permute-start | bytes 442376 | tf_op jit(solution)/shard_map/ppermute | solution.py:403
  9.2 12.2 %collective-permute-start = (bf16[96,768]{1,0:T(8,128)(2,1)S(1)}, bf16[96,768]{1,0:T(8,128)(2,1)S(1)}, u32[]{:S(2)}, u32[]{:S(2)}) collective-permute-start(bf16[96,768]{1,0:T(8,128)(2,1)S(1)} %shard_map.170.rest_0_), channel_id=1, source_target_pairs={{0,8},{4,12},{8,0},{12,4},{16,24},{20,28},{24,16},{28,20},{1,9},{5... | collective-permute-start | bytes 442376 | tf_op jit(solution)/shard_map/ppermute | solution.py:403
  21.5 14.4 %collective-permute-start.4 = (bf16[4,96,768]{2,1,0:T(8,128)(2,1)S(1)}, bf16[4,96,768]{2,1,0:T(8,128)(2,1)S(1)}, u32[]{:S(2)}, u32[]{:S(2)}) collective-permute-start(bf16[4,96,768]{2,1,0:T(8,128)(2,1)S(1)} %pad_maximum_fusion.1), channel_id=1, source_target_pairs={{0,4},{4,0},{8,12},{12,8},{16,20},{20,16},{24,28},{28,24},{1,5},{5... | collective-permute-start | bytes 1769480 | tf_op jit(solution)/shard_map/ppermute | solution.py:403
  23.1 5.9 %collective-permute-start.6 = (bf16[128,768]{1,0:T(8,128)(2,1)S(1)}, bf16[128,768]{1,0:T(8,128)(2,1)S(1)}, u32[]{:S(2)}, u32[]{:S(2)}) collective-permute-start(bf16[128,768]{1,0:T(8,128)(2,1)S(1)} %collective-permute-done.3.t1), channel_id=1, source_target_pairs={{0,1},{1,0},{2,3},{3,2},{4,5},{5,4},{6,7},{7,6},{8,9},{9,8},{10,11... | collective-permute-start | bytes 589832 | tf_op jit(solution)/shard_map/ppermute | solution.py:403
  24.6 18.2 %collective-permute-start.10 = (bf16[96,864]{1,0:T(8,128)(2,1)S(1)}, bf16[96,864]{1,0:T(8,128)(2,1)S(1)}, u32[]{:S(2)}, u32[]{:S(2)}) collective-permute-start(bf16[96,864]{1,0:T(8,128)(2,1)S(1)} %shard_map.172.rest_0_), channel_id=1, source_target_pairs={{0,24},{4,28},{8,16},{12,20},{16,8},{20,12},{24,0},{28,4},{1,25},{... | collective-permute-start | bytes 497672 | tf_op jit(solution)/shard_map/ppermute | solution.py:403
  27.1 15.7 %collective-permute-start.9 = (bf16[96,864]{1,0:T(8,128)(2,1)S(1)}, bf16[96,864]{1,0:T(8,128)(2,1)S(1)}, u32[]{:S(2)}, u32[]{:S(2)}) collective-permute-start(bf16[96,864]{1,0:T(8,128)(2,1)S(1)} %shard_map.172.rest_0_), channel_id=1, source_target_pairs={{0,16},{4,20},{8,24},{12,28},{16,0},{20,4},{24,8},{28,12},{1,17},{... | collective-permute-start | bytes 497672 | tf_op jit(solution)/shard_map/ppermute | solution.py:403
  27.1 15.7 %collective-permute-start.8 = (bf16[96,864]{1,0:T(8,128)(2,1)S(1)}, bf16[96,864]{1,0:T(8,128)(2,1)S(1)}, u32[]{:S(2)}, u32[]{:S(2)}) collective-permute-start(bf16[96,864]{1,0:T(8,128)(2,1)S(1)} %shard_map.172.rest_0_), channel_id=1, source_target_pairs={{0,8},{4,12},{8,0},{12,4},{16,24},{20,28},{24,16},{28,20},{1,9},{5... | collective-permute-start | bytes 497672 | tf_op jit(solution)/shard_map/ppermute | solution.py:403
  29.0 7.0 %collective-permute-start.7 = (bf16[128,768]{1,0:T(8,128)(2,1)S(1)}, bf16[128,768]{1,0:T(8,128)(2,1)S(1)}, u32[]{:S(2)}, u32[]{:S(2)}) collective-permute-start(bf16[128,768]{1,0:T(8,128)(2,1)S(1)} %copy-done.1), channel_id=1, source_target_pairs={{0,2},{1,3},{2,0},{3,1},{4,6},{5,7},{6,4},{7,5},{8,10},{9,11},{10,... | collective-permute-start | bytes 589832 | tf_op jit(solution)/shard_map/ppermute | solution.py:403
  44.2 17.9 %collective-permute-start.16 = (bf16[4,96,864]{2,1,0:T(8,128)(2,1)S(1)}, bf16[4,96,864]{2,1,0:T(8,128)(2,1)S(1)}, u32[]{:S(2)}, u32[]{:S(2)}) collective-permute-start(bf16[4,96,864]{2,1,0:T(8,128)(2,1)S(1)} %pad_maximum_fusion), channel_id=1, source_target_pairs={{0,4},{4,0},{8,12},{12,8},{16,20},{20,16},{24,28},{28,24},{1,5},{5... | collective-permute-start | bytes 1990664 | tf_op jit(solution)/shard_map/ppermute | solution.py:403
  45.9 11.3 %collective-permute-start.12 = (bf16[256,768]{1,0:T(8,128)(2,1)S(1)}, bf16[256,768]{1,0:T(8,128)(2,1)S(1)}, u32[]{:S(2)}, u32[]{:S(2)}) collective-permute-start(bf16[256,768]{1,0:T(8,128)(2,1)S(1)} %add_convert_fusion.1.own), channel_id=1, source_target_pairs={{0,2},{1,3},{2,0},{3,1},{4,6},{5,7},{6,4},{7,5},{8,10},{9,11},{10,... | collective-permute-start | bytes 1179656 | tf_op jit(solution)/shard_map/ppermute | solution.py:403
  68.0 11.2 %collective-permute-start.18 = (bf16[256,768]{1,0:T(8,128)(2,1)S(1)}, bf16[256,768]{1,0:T(8,128)(2,1)S(1)}, u32[]{:S(2)}, u32[]{:S(2)}) collective-permute-start(bf16[256,768]{1,0:T(8,128)(2,1)S(1)} %add_convert_fusion.own), channel_id=1, source_target_pairs={{0,2},{1,3},{2,0},{3,1},{4,6},{5,7},{6,4},{7,5},{8,10},{9,11},{10,... | collective-permute-start | bytes 1179656 | tf_op jit(solution)/shard_map/ppermute | solution.py:403
  71.1 17.3 %collective-permute-start.20 = (bf16[4,96,864]{2,1,0:T(8,128)(2,1)S(1)}, bf16[4,96,864]{2,1,0:T(8,128)(2,1)S(1)}, u32[]{:S(2)}, u32[]{:S(2)}) collective-permute-start(bf16[4,96,864]{2,1,0:T(8,128)(2,1)S(1)} %get-tuple-element.133), channel_id=1, source_target_pairs={{0,4},{4,0},{8,12},{12,8},{16,20},{20,16},{24,28},{28,24},{1,5},{5... | collective-permute-start | bytes 1990664 | tf_op jit(solution)/shard_map/ppermute | solution.py:403
  79.8 17.6 %collective-permute-start.25 = (bf16[256,768]{1,0:T(8,128)(2,1)S(1)}, bf16[256,768]{1,0:T(8,128)(2,1)S(1)}, u32[]{:S(2)}, u32[]{:S(2)}) collective-permute-start(bf16[256,768]{1,0:T(8,128)(2,1)S(1)} %get-tuple-element.143), channel_id=1, source_target_pairs={{0,1},{1,0},{2,3},{3,2},{4,5},{5,4},{6,7},{7,6},{8,9},{9,8},{10,11... | collective-permute-start | bytes 1179656 | tf_op jit(solution)/shard_map/ppermute | solution.py:403
  95.3 19.1 %collective-permute-start.21 = (bf16[4,96,768]{2,1,0:T(8,128)(2,1)S(1)}, bf16[4,96,768]{2,1,0:T(8,128)(2,1)S(1)}, u32[]{:S(2)}, u32[]{:S(2)}) collective-permute-start(bf16[4,96,768]{2,1,0:T(8,128)(2,1)S(1)} %get-tuple-element.137), channel_id=1, source_target_pairs={{0,4},{4,0},{8,12},{12,8},{16,20},{20,16},{24,28},{28,24},{1,5},{5... | collective-permute-start | bytes 1769480 | tf_op jit(solution)/shard_map/ppermute | solution.py:403
  97.6 23.0 %collective-permute-start.33 = (bf16[256,768]{1,0:T(8,128)(2,1)S(1)}, bf16[256,768]{1,0:T(8,128)(2,1)S(1)}, u32[]{:S(2)}, u32[]{:S(2)}) collective-permute-start(bf16[256,768]{1,0:T(8,128)(2,1)S(1)} %pad_maximum_fusion.2), channel_id=1, source_target_pairs={{0,2},{1,3},{2,0},{3,1},{4,6},{5,7},{6,4},{7,5},{8,10},{9,11},{10,... | collective-permute-start | bytes 1179656 | tf_op jit(solution)/shard_map/ppermute | solution.py:403
  99.3 8.1 %collective-permute-start.27 = (bf16[96,864]{1,0:T(8,128)(2,1)S(1)}, bf16[96,864]{1,0:T(8,128)(2,1)S(1)}, u32[]{:S(2)}, u32[]{:S(2)}) collective-permute-start(bf16[96,864]{1,0:T(8,128)(2,1)S(1)} %get-tuple-element.148), channel_id=1, source_target_pairs={{0,8},{4,12},{8,0},{12,4},{16,24},{20,28},{24,16},{28,20},{1,9},{5... | collective-permute-start | bytes 497672 | tf_op jit(solution)/shard_map/ppermute | solution.py:403
  99.4 15.0 %collective-permute-start.28 = (bf16[96,864]{1,0:T(8,128)(2,1)S(1)}, bf16[96,864]{1,0:T(8,128)(2,1)S(1)}, u32[]{:S(2)}, u32[]{:S(2)}) collective-permute-start(bf16[96,864]{1,0:T(8,128)(2,1)S(1)} %get-tuple-element.149), channel_id=1, source_target_pairs={{0,16},{4,20},{8,24},{12,28},{16,0},{20,4},{24,8},{28,12},{1,17},{... | collective-permute-start | bytes 497672 | tf_op jit(solution)/shard_map/ppermute | solution.py:403
  102.0 12.4 %collective-permute-start.29 = (bf16[96,864]{1,0:T(8,128)(2,1)S(1)}, bf16[96,864]{1,0:T(8,128)(2,1)S(1)}, u32[]{:S(2)}, u32[]{:S(2)}) collective-permute-start(bf16[96,864]{1,0:T(8,128)(2,1)S(1)} %get-tuple-element.150), channel_id=1, source_target_pairs={{0,24},{4,28},{8,16},{12,20},{16,8},{20,12},{24,0},{28,4},{1,25},{... | collective-permute-start | bytes 497672 | tf_op jit(solution)/shard_map/ppermute | solution.py:403
  107.5 6.9 %collective-permute-start.26 = (f32[2,768]{1,0:T(2,128)S(1)}, f32[2,768]{1,0:T(2,128)S(1)}, u32[]{:S(2)}, u32[]{:S(2)}) collective-permute-start(f32[2,768]{1,0:T(2,128)S(1)} %add.21.gains), channel_id=1, source_target_pairs={{0,4},{4,0},{8,12},{12,8},{16,20},{20,16},{24,28},{28,24},{1,5},{5... | collective-permute-start | bytes 18440 | tf_op jit(solution)/shard_map/ppermute | solution.py:403
  114.5 7.5 %collective-permute-start.30 = (bf16[104,768]{1,0:T(8,128)(2,1)S(1)}, bf16[104,768]{1,0:T(8,128)(2,1)S(1)}, u32[]{:S(2)}, u32[]{:S(2)}) collective-permute-start(bf16[104,768]{1,0:T(8,128)(2,1)S(1)} %get-tuple-element.154), channel_id=1, source_target_pairs={{0,8},{4,12},{8,0},{12,4},{16,24},{20,28},{24,16},{28,20},{1,9},{5... | collective-permute-start | bytes 479240 | tf_op jit(solution)/shard_map/ppermute | solution.py:403
  117.2 13.5 %collective-permute-start.31 = (bf16[104,768]{1,0:T(8,128)(2,1)S(1)}, bf16[104,768]{1,0:T(8,128)(2,1)S(1)}, u32[]{:S(2)}, u32[]{:S(2)}) collective-permute-start(bf16[104,768]{1,0:T(8,128)(2,1)S(1)} %get-tuple-element.155), channel_id=1, source_target_pairs={{0,16},{4,20},{8,24},{12,28},{16,0},{20,4},{24,8},{28,12},{1,17},{... | collective-permute-start | bytes 479240 | tf_op jit(solution)/shard_map/ppermute | solution.py:403
  117.9 12.8 %collective-permute-start.32 = (bf16[104,768]{1,0:T(8,128)(2,1)S(1)}, bf16[104,768]{1,0:T(8,128)(2,1)S(1)}, u32[]{:S(2)}, u32[]{:S(2)}) collective-permute-start(bf16[104,768]{1,0:T(8,128)(2,1)S(1)} %get-tuple-element.156), channel_id=1, source_target_pairs={{0,24},{4,28},{8,16},{12,20},{16,8},{20,12},{24,0},{28,4},{1,25},{... | collective-permute-start | bytes 479240 | tf_op jit(solution)/shard_map/ppermute | solution.py:403
  (21 other events, 61.2 us)

commit v4 on v3

--- a/solution.py
+++ b/solution.py
@@ -25,13 +25,14 @@
     return lax.dot_general(left, right, dims, preferred_element_type=F32)
 
 
-def call(kernel, outs, args, scalars=(), scratch=(), flops=0):
+def call(kernel, outs, args, scalars=(), scratch=(), flops=0, space=pltpu.VMEM):
     size = sum(int(np.prod(a.shape)) * a.dtype.itemsize for a in list(args) + list(outs))
     return pl.pallas_call(
         kernel,
+        name=getattr(kernel, "func", kernel).__name__,
         out_shape=tuple(outs),
         in_specs=[pl.BlockSpec(memory_space=pltpu.SMEM)] * len(scalars)
-        + [pl.BlockSpec(memory_space=pltpu.VMEM)] * len(args),
+        + [pl.BlockSpec(memory_space=space)] * len(args),
         out_specs=tuple(pl.BlockSpec(memory_space=pltpu.VMEM) for _ in outs),
         scratch_shapes=list(scratch),
         compiler_params=pltpu.CompilerParams(vmem_limit_bytes=48 * 1024 * 1024),
@@ -77,12 +78,20 @@
     return (lane >= head * HEAD_DIM) & (lane < (head + 1) * HEAD_DIM)
 
 
-def pack_kernel(wide, tall, packed):
+def pack_kernel(wide_far, tall_far, packed, wide, tall, sems):
+    copies = [
+        pltpu.make_async_copy(wide_far, wide, sems.at[0]),
+        pltpu.make_async_copy(tall_far, tall, sems.at[1]),
+    ]
+    for copy in copies:
+        copy.start()
+    for copy in copies:
+        copy.wait()
     parts = [wide[j] for j in range(wide.shape[0])]
     packed[...] = jnp.concatenate(parts + [tall[...].T], axis=1)
 
 
-def prepare_kernel(ids, first, t0, t1, t2, t3, gain, freq, n1, cosine, sine):
+def prepare_kernel(ids, t0, t1, t2, t3, gain, freq, n1, cosine, sine):
     gain_row = gain[...].astype(F32)
     for i, source in enumerate((t0, t1, t2, t3)):
         unit, _ = normed(source[...].astype(F32))
@@ -91,7 +100,7 @@
     lane = lax.broadcasted_iota(jnp.int32, (WINDOW, 128), 1)
     sign = jnp.where(lane % HEAD_DIM < HEAD_DIM // 2, -1.0, 1.0)
     for b in range(4):
-        start = jnp.where(first[b] > 0, b, start)
+        start = jnp.where(ids[9 + b] > 0, b, start)
         place = lax.broadcasted_iota(jnp.int32, (WINDOW, 128), 0) + (b - start) * WINDOW
         angle = place.astype(F32) * freq[...]
         cosine[b * WINDOW : (b + 1) * WINDOW, :] = jnp.cos(angle)
@@ -110,7 +119,7 @@
         right[at, :] = value[:, cut:]
 
 
-def attend_kernel(offsets, n_pieces, rows, ids, count, first, n1, cosine, sine, *rest):
+def attend_kernel(offsets, n_pieces, rows, ids, n1, cosine, sine, *rest):
     pieces = rest[:n_pieces]
     q_out, k_out, v_out, probs_out, att_out, whole, out_w = rest[n_pieces : n_pieces + 7]
     k_pad, v_pad = rest[n_pieces + 7 :]
@@ -120,6 +129,8 @@
     heads = width // HEAD_DIM
     total_rows = q_out.shape[0]
     blocks = total_rows // WINDOW
+    count = [ids[5 + b] for b in range(blocks)]
+    first = [ids[5 + blocks + b] for b in range(blocks)]
     for pad in (k_pad, v_pad):
         pad[0:half, :] = jnp.zeros((half, width), BF)
         pad[half + total_rows :, :] = jnp.zeros((half, width), BF)
@@ -260,8 +271,8 @@
 
 
 def attend_back_kernel(
-    ids, gy, gy_far, out_w, q_in, k_in, v_in, probs_in, cosine, sine,
-    g_raw,
+    ids, gy, gy_far, out_w, q_in, k_in, v_in, probs_in, cosine, sine, n1, qkv_w, gain, gain_two,
+    g_raw, g_send, g_keep, gains,
     g_att_all, k_pad, v_pad, gk_pad, gv_pad, gq_all,
 ):
     half = WINDOW // 2
@@ -313,6 +324,17 @@
         turned = qk * c - swap_halves(qk) * s
         g_raw[rows_b, : 2 * width] = turned.astype(BF)
         g_raw[rows_b, 2 * width :] = gv_pad[inner, :].astype(BF)
+    gain_sum = jnp.zeros(gain_two.shape, F32)
+    for i in (2, 3, 0, 1):
+        at = slice((i % 2) * WINDOW, (i % 2 + 1) * WINDOW)
+        g_n1 = dot(g_raw[rows_of(ids[i]), :], qkv_w[...], NT)
+        gain_sum += jnp.sum(g_n1 * n1[rows_of(ids[i]), :].astype(F32), axis=0, keepdims=True)
+        if i < 2:
+            g_keep[at, :] = g_n1
+        else:
+            g_send[at, :] = g_n1.astype(BF)
+    gains[0:1, :] = gain_sum / gain[...].astype(F32)
+    gains[1:2, :] = gain_two[...]
 
 
 def attend_grads_kernel(slots, rows, ids, n1, g_raw, gy, gy_far, att, send, keep, total):
@@ -328,20 +350,6 @@
         keep[...] = jnp.zeros(keep.shape, BF)
 
 
-def first_back_kernel(ids, g_raw, qkv_w, n1, gain, gain_two, g_send, g_keep, gains):
-    gain_sum = jnp.zeros(gain_two.shape, F32)
-    for i in (2, 3, 0, 1):
-        at = slice((i % 2) * WINDOW, (i % 2 + 1) * WINDOW)
-        g_n1 = dot(g_raw[rows_of(ids[i]), :], qkv_w[...], NT)
-        gain_sum += jnp.sum(g_n1 * n1[rows_of(ids[i]), :].astype(F32), axis=0, keepdims=True)
-        if i < 2:
-            g_keep[at, :] = g_n1
-        else:
-            g_send[at, :] = g_n1.astype(BF)
-    gains[0:1, :] = gain_sum / gain[...].astype(F32)
-    gains[1:2, :] = gain_two[...]
-
-
 def merge_kernel(keep, got, first, *others):
     first[...] = keep[0].astype(F32) + got[0].astype(F32)
     for k, other in enumerate(others):
@@ -351,40 +359,43 @@
 EXTRA = 8
 
 
-def merge_gains_kernel(keep, got, gains, gains_got, first, *others):
+def merge_gains_kernel(keep, got, gains, gains_got, first, *rest):
+    others, total_out = rest[:-1], rest[-1]
     rows, columns = keep.shape[1:]
-    first[:rows, :] = keep[0].astype(F32) + got[0].astype(F32)
+    first[...] = keep[0].astype(F32) + got[0].astype(F32)
     total = gains[...] + gains_got[...]
+    total_out[...] = total
     high = total.astype(BF).astype(F32)
     low = (total - high).astype(BF).astype(F32)
-    first[rows:, :] = jnp.concatenate([total, jnp.zeros((EXTRA - 2, columns), F32)], axis=0)
     coded = jnp.concatenate([high, low, jnp.zeros((EXTRA - 4, columns), F32)], axis=0).astype(BF)
     for k, other in enumerate(others):
         other[:rows, :] = (keep[k + 1].astype(F32) + got[k + 1].astype(F32)).astype(BF)
         other[rows:, :] = coded
 
 
-def deliver_kernel(with_gains, first, *rest):
+def deliver_kernel(with_gains, count, first, *rest):
+    count_parts = len(rest) - 2
     if with_gains:
-        rows = first.shape[0] - EXTRA
-        parts = rest[:-4]
-        gains = first[rows : rows + 2, :]
-        for part in parts:
+        count_parts = len(rest) - 5
+        gains = rest[count_parts][...]
+        rows = first.shape[0]
+        for part in rest[:count_parts]:
             coded = part[rows:, :].astype(F32)
             gains = gains + coded[0:2, :] + coded[2:4, :]
-        rest[-4][...] = gains[0:1, :]
-        rest[-3][...] = gains[1:2, :]
-        total = first[:rows, :]
-        for part in parts:
-            total = total + part[:rows, :].astype(F32)
-    else:
-        total = first[...]
-        for part in rest[:-2]:
-            total = total + part[...].astype(F32)
+        for j in range(gains.shape[1] // 128):
+            rest[-4][j : j + 1, :] = gains[0:1, j * 128 : (j + 1) * 128]
+            rest[-3][j : j + 1, :] = gains[1:2, j * 128 : (j + 1) * 128]
+    total = first[...]
+    for part in rest[:count_parts]:
+        total = total + part[: first.shape[0], :].astype(F32)
     wide, turned = rest[-2:]
-    count, _, width = wide.shape
+    width = wide.shape[2]
     for j in range(count):
-        wide[j] = total[:, j * width : (j + 1) * width]
+        value = total[:, j * width : (j + 1) * width]
+        if with_gains:
+            wide[j] = value
+        else:
+            wide[:, j, :] = value
     turned[...] = total[:, count * width :].T
 
 
@@ -416,12 +427,22 @@
     pair_rows = 2 * WINDOW
     slots = n_dp // 2 if shard % 16 == 0 and n_dp % 2 == 0 and n_dp <= 8 else 0
     place = lax.axis_index("tensor").astype(jnp.int32)
-    ids = jnp.stack(
-        [place, place ^ 2, place ^ 1, place ^ 3, lax.axis_index("dp").astype(jnp.int32)]
+    ids = jnp.concatenate(
+        [
+            jnp.stack(
+                [place, place ^ 2, place ^ 1, place ^ 3, lax.axis_index("dp").astype(jnp.int32)]
+            ),
+            block_count,
+            block_first,
+        ]
     )
     core = functools.partial(swap, axis="tensor", bit=1, size=4)
     across = functools.partial(swap, axis="tensor", bit=2, size=4)
     dp = functools.partial(swap, axis="dp", size=n_dp)
+
+    def diagonal(values):
+        pairs = [(4 * d + t, 4 * (d ^ 1) + (t ^ 2)) for d in range(n_dp) for t in range(4)]
+        return lax.ppermute(values, ("dp", "tensor"), pairs)
 
     def along(value):
         if not slots:
@@ -431,6 +452,8 @@
     def aside(pieces):
         if not slots:
             return []
+        if len(pieces) == 1:
+            return [dp(pieces[0], bit=1)]
         return list(dp(jnp.stack(pieces), bit=1))
 
     def picked(own, near, far):
@@ -438,26 +461,32 @@
 
     def merge(keep, got, gains=()):
         _, rows, columns = keep.shape
-        rows += EXTRA if gains else 0
+        extra = EXTRA if gains else 0
         return call(
             merge_gains_kernel if gains else merge_kernel,
-            (shape(rows, columns, dtype=F32),) + (shape(rows, columns),) * (slots - 1),
+            (shape(rows, columns, dtype=F32),)
+            + (shape(rows + extra, columns),) * (slots - 1)
+            + ((shape(2, columns, dtype=F32),) if gains else ()),
             (keep, got, *gains),
         )
 
-    def deliver(parts, count, with_gains=False):
+    def deliver(parts, count, gains=()):
         columns = parts[0].shape[1]
         each = columns // (count + 1)
         if not slots:
             total = parts[0]
             return total[:, : count * each].reshape(shard, count, each), total[:, count * each :].T
-        *gains, wide, tall = call(
-            functools.partial(deliver_kernel, with_gains),
-            ((shape(1, columns, dtype=F32),) * 2 if with_gains else ())
-            + (shape(count, shard, each, dtype=F32), shape(each, shard, dtype=F32)),
-            parts,
+        with_gains = bool(gains)
+        whole = (count, shard, each) if with_gains else (shard, count, each)
+        *sums, wide, tall = call(
+            functools.partial(deliver_kernel, with_gains, count),
+            ((shape(columns // 128, 128, dtype=F32),) * 2 if with_gains else ())
+            + (shape(*whole, dtype=F32), shape(each, shard, dtype=F32)),
+            tuple(parts) + tuple(gains),
         )
-        return *(gain.reshape(columns) for gain in gains), jnp.transpose(wide, (1, 0, 2)), tall
+        if with_gains:
+            wide = jnp.transpose(wide, (1, 0, 2))
+        return *(gain.reshape(columns) for gain in sums), wide, tall
 
     def slot_shapes(columns):
         if not slots:
@@ -476,24 +505,43 @@
         count, _, each = wide.shape
         if not slots:
             return jnp.concatenate([*wide, tall.T], axis=1)
-        return call(pack_kernel, (shape(shard, count * each + tall.shape[0]),), (wide, tall))[0]
+        return call(
+            pack_kernel,
+            (shape(shard, count * each + tall.shape[0]),),
+            (wide, tall),
+            scratch=[
+                pltpu.VMEM(wide.shape, BF),
+                pltpu.VMEM(tall.shape, BF),
+                pltpu.SemaphoreType.DMA((2,)),
+            ],
+            space=pltpu.HBM,
+        )[0]
 
     qkv_own = pack(jnp.transpose(w_qkv, (1, 0, 2)), w_out)
-    qkv_near, tokens_across = pin((along(qkv_own), across(tokens)))
+    unit_own = pack(jnp.transpose(w_in, (1, 0, 2)), w_down)
+    qkv_near, qkv_side, unit_side, tokens_across, ids, gain_one, gain_two = pin(
+        (
+            along(qkv_own),
+            aside([qkv_own]),
+            aside([unit_own]),
+            across(tokens),
+            ids,
+            gain_one,
+            gain_two,
+        )
+    )
     token_blocks = (tokens, tokens_across, core(tokens), core(tokens_across))
-    qkv_far = aside([qkv_own] + qkv_near)
+    qkv_far = qkv_side + aside(qkv_near)
     n1, cosine, sine = call(
         prepare_kernel,
         (shape(total_rows, width), shape(total_rows, 128, dtype=F32), shape(total_rows, 128, dtype=F32)),
         token_blocks + (gain_one, freq),
-        (ids, block_first),
-    )
-    unit_own = pack(jnp.transpose(w_in, (1, 0, 2)), w_down)
+        (ids,),
+    )
     unit_own, cot, _ = pin((unit_own, cotangent, qkv_near))
     unit_near = along(unit_own)
     cot_across = across(cot)
-    qkv_far, n1, cot_across = pin((qkv_far, n1, cot_across))
-    cot_blocks = (cotangent, cot_across, core(cot), core(cot_across))
+    qkv_far, n1 = pin((qkv_far, n1))
     qkv_pieces = picked(qkv_own, qkv_near, qkv_far)
     flat = shape(total_rows, head_width)
     query, keys, values, probs, attended, qkv_w, out_w = call(
@@ -508,12 +556,13 @@
             shape(width, head_width),
         ),
         (n1, cosine, sine) + qkv_pieces,
-        (ids, block_count, block_first),
+        (ids,),
         [pltpu.VMEM((total_rows + WINDOW, head_width), BF)] * 2,
         flops=2 * total_rows * width * 3 * head_width,
     )
-    attended, unit_near = pin((attended, unit_near))
-    unit_far = aside([unit_own] + unit_near)
+    attended, unit_near, cot_across = pin((attended, unit_near, cot_across))
+    cot_blocks = (cotangent, cot_across, core(cot), core(cot_across))
+    unit_far = unit_side + aside(unit_near)
     unit_pieces = picked(unit_own, unit_near, unit_far)
     in_w, down_w = call(
         functools.partial(collect_kernel, offsets, len(unit_pieces), shard),
@@ -531,10 +580,11 @@
         flops=2 * total_rows * width * head_width,
     )
     a_sum = (a_keep + core(a_send).astype(F32)).astype(BF)
+    a_got = across(a_sum)
     h, n2 = call(
         middle_kernel,
         (pair_f32, pair_bf),
-        (a_sum, across(a_sum), token_blocks[0], token_blocks[1], gain_two),
+        (a_sum, a_got, token_blocks[0], token_blocks[1], gain_two),
     )
     n2_far = core(n2)
     u_send, u_keep, both, act = call(
@@ -562,10 +612,16 @@
         (u_sum, u_got, h, cot_blocks[0], cot_blocks[1], gain_two),
     )
     gy_far = core(gy)
-    (g_raw,) = call(
+    g_raw, g_send, g_keep, gains = call(
         attend_back_kernel,
-        (shape(total_rows, 3 * head_width),),
-        (gy, gy_far, out_w, query, keys, values, probs, cosine, sine),
+        (
+            shape(total_rows, 3 * head_width),
+            pair_bf,
+            pair_f32,
+            shape(2, width, dtype=F32),
+        ),
+        (gy, gy_far, out_w, query, keys, values, probs, cosine, sine, n1, qkv_w)
+        + (gain_one, gain_part_two),
         (ids,),
         [
             pltpu.VMEM((total_rows, head_width), BF),
@@ -575,31 +631,25 @@
             pltpu.VMEM((total_rows + WINDOW, head_width), F32),
             pltpu.VMEM((total_rows, head_width), F32),
         ],
-        flops=2 * total_rows * width * 3 * head_width,
     )
     if slots:
-        g_raw, in_got = pin((g_raw, dp(in_send, bit=1)))
-        in_parts = merge(in_keep, in_got)
+        g_raw, g_send, gains, in_got = pin((g_raw, g_send, gains, dp(in_send, bit=1)))
     att_send, att_keep = call(
         functools.partial(attend_grads_kernel, slots, shard),
         slot_shapes(4 * head_width),
         (n1, g_raw, gy, gy_far, attended),
         (ids,),
         [pltpu.VMEM((width, 4 * head_width), F32)],
-        flops=2 * total_rows * width * 4 * head_width,
-    )
-    g_raw, att_keep = pin((g_raw, att_keep))
-    g_send, g_keep, gains = call(
-        first_back_kernel,
-        (pair_bf, pair_f32, shape(2, width, dtype=F32)),
-        (g_raw, qkv_w, n1, gain_one, gain_part_two),
-        (ids,),
-        flops=2 * total_rows * width * 3 * head_width,
-    )
+    )
+    if slots:
+        in_got, att_keep = pin((in_got, att_keep))
+        in_parts = merge(in_keep, in_got)
+        in_near = [dp(in_parts[k], bit=2 * k) for k in range(1, slots)]
+        gains = gains + core(gains)
+        gains = gains + across(gains)
     g_core = core(g_send)
     if slots:
-        gains = gains + core(gains)
-        gains, g_core, b_core = pin((gains + across(gains), g_core, b_core))
+        gains, g_core, b_core = pin((gains, g_core, b_core))
     back = jnp.concatenate(
         [
             (g_keep[WINDOW:] + g_core[WINDOW:].astype(F32)).astype(BF),
@@ -613,10 +663,11 @@
         (g_keep, g_core, b_keep, b_core, across(back), h, tokens, gain_one, gh),
     )
     if slots:
-        in_parts = (in_parts[0], *(dp(in_parts[k], bit=2 * k) for k in range(1, slots)))
-        att_got, gains_got, in_parts = pin((dp(att_send, bit=1), dp(gains, bit=1), in_parts))
-        att_parts = merge(att_keep, att_got, (gains, gains_got))
+        att_got, in_near[0], gains_x = pin((dp(att_send, bit=1), in_near[0], dp(gains, bit=1)))
+        in_parts = (in_parts[0], *in_near)
+        *att_parts, gains = merge(att_keep, att_got, (gains, gains_x))
         att_parts = (att_parts[0], *(dp(att_parts[k], bit=2 * k) for k in range(1, slots)))
+        gains = [gains]
     else:
         gains = lax.psum(gains, ("dp", "tensor"))
         in_parts = (lax.psum_scatter(in_send, "dp", scatter_dimension=0, tiled=True),)
@@ -626,7 +677,7 @@
         (att_parts, mixed, input_grad, in_grad, down_grad)
     )
     if slots:
-        *gains, qkv_grad, out_grad = deliver(att_parts, 3, True)
+        *gains, qkv_grad, out_grad = deliver(att_parts, 3, gains)
     else:
         qkv_grad, out_grad = deliver(att_parts, 3)
     return (mixed, input_grad, gains[0], qkv_grad, out_grad, gains[1], in_grad, down_grad)

time: 134 us -> 125 us (0.933)
  waiting for transfers between devices: 61.7 us -> 51.8 us
    ppermute x34 -> x36, waiting for transfers between devices: 61.7 us -> 51.8 us  [swap(): return lax.ppermute(values, axis, [(i, i ^ bit) for i in range(size)])]
    pallas_call x18 -> x17, Pallas kernels: 28.8 us -> 29.7 us  [call(): pl.pallas_call(kernel, name=getattr(kernel, 'func', kernel).__name__, out...]
    unnamed x24 -> x25, local copies, waits for them, and re-layouts: 4.04 us -> 4.81 us
    ppermute x34 -> x36, starting transfers between devices: 36.3 us -> 36.6 us  [swap(): return lax.ppermute(values, axis, [(i, i ^ bit) for i in range(size)])]
  transfers between devices with their start and end apart: 34 -> 36, of which waited for: 15 -> 17; matrix products, arithmetic and copies ran while one was open for 0% -> 0% of each run, Pallas kernels for 18% -> 19%
where the time goes in v4:
time: 125 us; the launch traced here: 124 us
  waiting for transfers between devices  51.8 us (41%)
  starting transfers between devices  36.6 us (29%)
  Pallas kernels  29.7 us (24%)
  local copies, waits for them, and re-layouts  4.97 us (4%)
    ppermute x36, waiting for transfers between devices, swap(): return lax.ppermute(values, axis, [(i, i ^ bit) for i in range(size)])  51.8 us
    ppermute x36, starting transfers between devices, swap(): return lax.ppermute(values, axis, [(i, i ^ bit) for i in range(size)])  36.6 us
    pallas_call x17, Pallas kernels, call(): pl.pallas_call(kernel, name=getattr(kernel, 'func', kernel).__name__, out...  29.7 us
    unnamed x25, local copies, waits for them, and re-layouts  4.81 us
  transfers between devices with their start and end apart: 36, of which 17 were waited for; matrix products, arithmetic and copies ran while one was open for 0% of the time, Pallas kernels for 19%

profile of v4, /device:TPU:0, one launch (start us, length us, event | category | flops | bytes accessed | tf_op | source)
XLA Modules:
  0.0 124.5 jit_solution(1717154055329341036)
XLA Ops:
  2.8 3.0 %collective-permute-start.3 = (bf16[96,768]{1,0:T(8,128)(2,1)S(1)}, bf16[96,768]{1,0:T(8,128)(2,1)S(1)}, u32[]{:S(2)}, u32[]{:S(2)}) collective-permute-start(bf16[96,768]{1,0:T(8,128)(2,1)S(1)} %pack_kernel.2.rest_0_), channel_id=1, source_target_pairs={{0,4},{4,0},{8,12},{12,8},{16,20},{20,16},{24,28},{28,24},{1,5},{5... | collective-permute-start | bytes 442376 | tf_op jit(solution)/shard_map/ppermute | solution.py:414
  8.4 3.6 %collective-permute-start.2 = (bf16[96,768]{1,0:T(8,128)(2,1)S(1)}, bf16[96,768]{1,0:T(8,128)(2,1)S(1)}, u32[]{:S(2)}, u32[]{:S(2)}) collective-permute-start(bf16[96,768]{1,0:T(8,128)(2,1)S(1)} %pack_kernel.2.rest_0_), channel_id=1, source_target_pairs={{0,24},{4,28},{8,16},{12,20},{16,8},{20,12},{24,0},{28,4},{1,25},{... | collective-permute-start | bytes 442376 | tf_op jit(solution)/shard_map/ppermute | solution.py:414
  15.0 2.1 %collective-permute-done.2.rest_3_ = bf16[96,768]{1,0:T(8,128)(2,1)S(1)} collective-permute-done((bf16[96,768]{1,0:T(8,128)(2,1)S(1)}, bf16[96,768]{1,0:T(8,128)(2,1)S(1)}, u32[]{:S(2)}, u32[]{:S(2)}) %collective-permute-start.2) | collective-permute-done | bytes 147488 | tf_op jit(solution)/shard_map/ppermute | solution.py:414
  17.0 6.7 %collective-permute-done.1.rest_2_ = bf16[96,768]{1,0:T(8,128)(2,1)S(1)} collective-permute-done((bf16[96,768]{1,0:T(8,128)(2,1)S(1)}, bf16[96,768]{1,0:T(8,128)(2,1)S(1)}, u32[]{:S(2)}, u32[]{:S(2)}) %collective-permute-start.1) | collective-permute-done | bytes 147488 | tf_op jit(solution)/shard_map/ppermute | solution.py:414
  25.8 2.5 %collective-permute-start.11 = (bf16[96,864]{1,0:T(8,128)(2,1)S(1)}, bf16[96,864]{1,0:T(8,128)(2,1)S(1)}, u32[]{:S(2)}, u32[]{:S(2)}) collective-permute-start(bf16[96,864]{1,0:T(8,128)(2,1)S(1)} %pack_kernel.3.rest_0_), channel_id=1, source_target_pairs={{0,24},{4,28},{8,16},{12,20},{16,8},{20,12},{24,0},{28,4},{1,25},{... | collective-permute-start | bytes 497672 | tf_op jit(solution)/shard_map/ppermute | solution.py:414
  28.3 1.9 %collective-permute-start.9 = (bf16[96,864]{1,0:T(8,128)(2,1)S(1)}, bf16[96,864]{1,0:T(8,128)(2,1)S(1)}, u32[]{:S(2)}, u32[]{:S(2)}) collective-permute-start(bf16[96,864]{1,0:T(8,128)(2,1)S(1)} %pack_kernel.3.rest_0_), channel_id=1, source_target_pairs={{0,8},{4,12},{8,0},{12,4},{16,24},{20,28},{24,16},{28,20},{1,9},{5... | collective-permute-start | bytes 497672 | tf_op jit(solution)/shard_map/ppermute | solution.py:414
  30.7 2.0 %prepare_kernel.1 = (bf16[512,768]{1,0:T(8,128)(2,1)S(1)}, f32[512,128]{1,0:T(8,128)S(1)}, f32[512,128]{1,0:T(8,128)S(1)}) custom-call(s32[13]{0:T(128)S(1)} %concatenate.6.ids, bf16[128,768]{1,0:T(8,128)(2,1)S(1)} %copy-done, bf16[128,768]{1,0:T(8,128)(2,1)S(1)} %collective-permute-done.5.t1, bf16[128,768]{1,0:T(8,128)(2,1)S(1)} %collective-permute-done.7.t2, ...), custom_call_target="tpu_custom_call" | custom-call | flops 1 | bytes 1 | tf_op jit(solution)/shard_map/prepare_kernel/pallas_call | solution.py:30
  32.8 2.2 %collective-permute-done.6 = bf16[3,96,768]{2,1,0:T(8,128)(2,1)S(1)} collective-permute-done((bf16[3,96,768]{2,1,0:T(8,128)(2,1)S(1)}, bf16[3,96,768]{2,1,0:T(8,128)(2,1)S(1)}, u32[]{:S(2)}, u32[]{:S(2)}) %collective-permute-start.6) | collective-permute-done | bytes 442400 | tf_op jit(solution)/shard_map/ppermute | solution.py:414
  35.0 6.1 %attend_kernel.1 = (bf16[512,192]{1,0:T(8,128)(2,1)S(1)}, bf16[512,192]{1,0:T(8,128)(2,1)S(1)}, bf16[512,192]{1,0:T(8,128)(2,1)S(1)}, bf16[3,512,256]{2,1,0:T(8,...) custom-call(s32[13]{0:T(128)S(1)} %concatenate.6.ids, ...), custom_call_target="tpu_custom_call" | custom-call | flops 1 | bytes 1 | tf_op jit(solution)/shard_map/attend_kernel/pallas_call | solution.py:30
  43.5 1.7 %collective-permute-done.13 = bf16[256,768]{1,0:T(8,128)(2,1)S(1)} collective-permute-done((bf16[256,768]{1,0:T(8,128)(2,1)S(1)}, bf16[256,768]{1,0:T(8,128)(2,1)S(1)}, u32[]{:S(2)}, u32[]{:S(2)}) %collective-permute-start.13) | collective-permute-done | bytes 393248 | tf_op jit(solution)/shard_map/ppermute | solution.py:414
  47.5 9.1 %collective-permute-done.14.received = bf16[256,768]{1,0:T(8,128)(2,1)S(1)} collective-permute-done((bf16[256,768]{1,0:T(8,128)(2,1)S(1)}, bf16[256,768]{1,0:T(8,128)(2,1)S(1)}, u32[]{:S(2)}, u32[]{:S(2)}) %collective-permute-start.14) | collective-permute-done | bytes 393248 | tf_op jit(solution)/shard_map/ppermute | solution.py:414
  57.6 2.2 %collective-permute-done.18 = bf16[3,96,864]{2,1,0:T(8,128)(2,1)S(1)} collective-permute-done((bf16[3,96,864]{2,1,0:T(8,128)(2,1)S(1)}, bf16[3,96,864]{2,1,0:T(8,128)(2,1)S(1)}, u32[]{:S(2)}, u32[]{:S(2)}) %collective-permute-start.18) | collective-permute-done | bytes 497696 | tf_op jit(solution)/shard_map/ppermute | solution.py:414
  60.7 3.0 %units_kernel.1 = (bf16[256,768]{1,0:T(8,128)(2,1)S(1)}, f32[256,768]{1,0:T(8,128)S(1)}, bf16[512,576]{1,0:T(8,128)(2,1)S(1)}, bf16[512,288]{1,0:T(8,128)(2,1)S(1)}) custom-call(bf16[256,768]{1,0:T(8,128)(2,1)S(1)} %get-tuple-element.124.n2, bf16[256,768]{1,0:T(8,128)(2,1)S(1)} %collective-permute-done.15.n2_far, bf16[128,768]{1,0:T(8,128)(2,1)S(1)} %copy-done.1, ...), custom_call_target="tpu_custom_call" | custom-call | flops 1 | bytes 1 | tf_op jit(solution)/shard_map/units_kernel/pallas_call | solution.py:30
  67.0 2.5 %unit_grads_kernel.1 = (bf16[4,96,864]{2,1,0:T(8,128)(2,1)S(1)}, bf16[4,96,864]{2,1,0:T(8,128)(2,1)S(1)}, bf16[256,768]{1,0:T(8,128)(2,1)S(1)}, f32[256,768]{1,0:T(8,128)S(1)}) custom-call(s32[13]{0:T(128)S(1)} %concatenate.6.ids, bf16[256,768]{1,0:T(8,128)(2,1)S(1)} %get-tuple-element.124.n2, bf16[256,768]{1,0:T(8,128)(2,1)S(1)} %collective-permute-done.15.n2_far, ...), custom_call_target="tpu_custom_call" | custom-call | flops 1 | bytes 1 | tf_op jit(solution)/shard_map/unit_grads_kernel/pallas_call | solution.py:30
  71.0 5.8 %collective-permute-done.20.received = bf16[256,768]{1,0:T(8,128)(2,1)S(1)} collective-permute-done((bf16[256,768]{1,0:T(8,128)(2,1)S(1)}, bf16[256,768]{1,0:T(8,128)(2,1)S(1)}, u32[]{:S(2)}, u32[]{:S(2)}) %collective-permute-start.20) | collective-permute-done | bytes 393248 | tf_op jit(solution)/shard_map/ppermute | solution.py:414
  79.2 7.1 %attend_back_kernel.1 = (bf16[512,576]{1,0:T(8,128)(2,1)S(1)}, bf16[256,768]{1,0:T(8,128)(2,1)S(1)}, f32[256,768]{1,0:T(8,128)S(1)}, f32[2,768]{1,0:T(2,128)S(1)}) custom-call(s32[13]{0:T(128)S(1)} %concatenate.6.ids, bf16[256,768]{1,0:T(8,128)(2,1)S(1)} %get-tuple-element.139.gy, bf16[256,768]{1,0:T(8,128)(2,1)S(1)} %collective-permute-done.21.gy_far, ...), custom_call_target="tpu_custom_call" | custom-call | flops 1 | bytes 1 | tf_op jit(solution)/shard_map/attend_back_kernel/pallas_call | solution.py:30
  89.4 1.7 %attend_grads_kernel.1 = (bf16[4,96,768]{2,1,0:T(8,128)(2,1)S(1)}, bf16[4,96,768]{2,1,0:T(8,128)(2,1)S(1)}) custom-call(s32[13]{0:T(128)S(1)} %concatenate.6.ids, bf16[512,768]{1,0:T(8,128)(2,1)S(1)} %get-tuple-element.109.n1, bf16[512,576]{1,0:T(8,128)(2,1)S(1)} %get-tuple-element.151.g_raw, bf16[256,768]{1,0:T(8,128)(2,1)S(1)} %get-tuple-element.139.gy, ...), custom_call_target="tpu_custom_call" | custom-call | flops 1 | bytes 1 | tf_op jit(solution)/shard_map/attend_grads_kernel/pallas_call | solution.py:30
  94.3 1.7 %collective-permute-start.34 = (bf16[96,864]{1,0:T(8,128)(2,1)S(1)}, bf16[96,864]{1,0:T(8,128)(2,1)S(1)}, u32[]{:S(2)}, u32[]{:S(2)}) collective-permute-start(bf16[96,864]{1,0:T(8,128)(2,1)S(1)} %get-tuple-element.177), channel_id=1, source_target_pairs={{0,16},{4,20},{8,24},{12,28},{16,0},{20,4},{24,8},{28,12},{1,17},{... | collective-permute-start | bytes 497672 | tf_op jit(solution)/shard_map/ppermute | solution.py:414
  97.2 4.8 %collective-permute-done.24.rest_0_ = bf16[96,864]{1,0:T(8,128)(2,1)S(1)} collective-permute-done((bf16[96,864]{1,0:T(8,128)(2,1)S(1)}, bf16[96,864]{1,0:T(8,128)(2,1)S(1)}, u32[]{:S(2)}, u32[]{:S(2)}) %collective-permute-start.24) | collective-permute-done | bytes 165920 | tf_op jit(solution)/shard_map/ppermute | solution.py:414
  102.0 2.4 %collective-permute-start.35 = (bf16[96,864]{1,0:T(8,128)(2,1)S(1)}, bf16[96,864]{1,0:T(8,128)(2,1)S(1)}, u32[]{:S(2)}, u32[]{:S(2)}) collective-permute-start(bf16[96,864]{1,0:T(8,128)(2,1)S(1)} %get-tuple-element.178), channel_id=1, source_target_pairs={{0,24},{4,28},{8,16},{12,20},{16,8},{20,12},{24,0},{28,4},{1,25},{... | collective-permute-start | bytes 497672 | tf_op jit(solution)/shard_map/ppermute | solution.py:414
  104.5 2.0 %collective-permute-done.29.gains_got = f32[2,768]{1,0:T(2,128)S(1)} collective-permute-done((f32[2,768]{1,0:T(2,128)S(1)}, f32[2,768]{1,0:T(2,128)S(1)}, u32[]{:S(2)}, u32[]{:S(2)}) %collective-permute-start.29) | collective-permute-done | bytes 6176 | tf_op jit(solution)/shard_map/ppermute | solution.py:414
  106.7 2.4 %collective-permute-start.31 = (bf16[104,768]{1,0:T(8,128)(2,1)S(1)}, bf16[104,768]{1,0:T(8,128)(2,1)S(1)}, u32[]{:S(2)}, u32[]{:S(2)}) collective-permute-start(bf16[104,768]{1,0:T(8,128)(2,1)S(1)} %get-tuple-element.166), channel_id=1, source_target_pairs={{0,16},{4,20},{8,24},{12,28},{16,0},{20,4},{24,8},{28,12},{1,17},{... | collective-permute-start | bytes 479240 | tf_op jit(solution)/shard_map/ppermute | solution.py:414
  109.2 1.9 %collective-permute-start.32 = (bf16[104,768]{1,0:T(8,128)(2,1)S(1)}, bf16[104,768]{1,0:T(8,128)(2,1)S(1)}, u32[]{:S(2)}, u32[]{:S(2)}) collective-permute-start(bf16[104,768]{1,0:T(8,128)(2,1)S(1)} %get-tuple-element.167), channel_id=1, source_target_pairs={{0,24},{4,28},{8,16},{12,20},{16,8},{20,12},{24,0},{28,4},{1,25},{... | collective-permute-start | bytes 479240 | tf_op jit(solution)/shard_map/ppermute | solution.py:414
  114.0 9.6 %collective-permute-done.31.rest_1_ = bf16[104,768]{1,0:T(8,128)(2,1)S(1)} collective-permute-done((bf16[104,768]{1,0:T(8,128)(2,1)S(1)}, bf16[104,768]{1,0:T(8,128)(2,1)S(1)}, u32[]{:S(2)}, u32[]{:S(2)}) %collective-permute-start.31) | collective-permute-done | bytes 159776 | tf_op jit(solution)/shard_map/ppermute | solution.py:414
  (103 shorter events, 35.4 us)
Async XLA Ops:
  2.8 9.2 %collective-permute-start.3 = (bf16[96,768]{1,0:T(8,128)(2,1)S(1)}, bf16[96,768]{1,0:T(8,128)(2,1)S(1)}, u32[]{:S(2)}, u32[]{:S(2)}) collective-permute-start(bf16[96,768]{1,0:T(8,128)(2,1)S(1)} %pack_kernel.2.rest_0_), channel_id=1, source_target_pairs={{0,4},{4,0},{8,12},{12,8},{16,20},{20,16},{24,28},{28,24},{1,5},{5... | collective-permute-start | bytes 442376 | tf_op jit(solution)/shard_map/ppermute | solution.py:414
  5.8 17.9 %collective-permute-start.5 = (bf16[128,768]{1,0:T(8,128)(2,1)S(1)}, bf16[128,768]{1,0:T(8,128)(2,1)S(1)}, u32[]{:S(2)}, u32[]{:S(2)}) collective-permute-start(bf16[128,768]{1,0:T(8,128)(2,1)S(1)} %copy-done), channel_id=1, source_target_pairs={{0,2},{1,3},{2,0},{3,1},{4,6},{5,7},{6,4},{7,5},{8,10},{9,11},{10,... | collective-permute-start | bytes 589832 | tf_op jit(solution)/shard_map/ppermute | solution.py:414
  7.8 15.8 %collective-permute-start.4 = (bf16[96,864]{1,0:T(8,128)(2,1)S(1)}, bf16[96,864]{1,0:T(8,128)(2,1)S(1)}, u32[]{:S(2)}, u32[]{:S(2)}) collective-permute-start(bf16[96,864]{1,0:T(8,128)(2,1)S(1)} %pack_kernel.3.rest_0_), channel_id=1, source_target_pairs={{0,4},{4,0},{8,12},{12,8},{16,20},{20,16},{24,28},{28,24},{1,5},{5... | collective-permute-start | bytes 497672 | tf_op jit(solution)/shard_map/ppermute | solution.py:414
  8.4 8.6 %collective-permute-start.2 = (bf16[96,768]{1,0:T(8,128)(2,1)S(1)}, bf16[96,768]{1,0:T(8,128)(2,1)S(1)}, u32[]{:S(2)}, u32[]{:S(2)}) collective-permute-start(bf16[96,768]{1,0:T(8,128)(2,1)S(1)} %pack_kernel.2.rest_0_), channel_id=1, source_target_pairs={{0,24},{4,28},{8,16},{12,20},{16,8},{20,12},{24,0},{28,4},{1,25},{... | collective-permute-start | bytes 442376 | tf_op jit(solution)/shard_map/ppermute | solution.py:414
  12.0 11.6 %collective-permute-start.1 = (bf16[96,768]{1,0:T(8,128)(2,1)S(1)}, bf16[96,768]{1,0:T(8,128)(2,1)S(1)}, u32[]{:S(2)}, u32[]{:S(2)}) collective-permute-start(bf16[96,768]{1,0:T(8,128)(2,1)S(1)} %pack_kernel.2.rest_0_), channel_id=1, source_target_pairs={{0,16},{4,20},{8,24},{12,28},{16,0},{20,4},{24,8},{28,12},{1,17},{... | collective-permute-start | bytes 442376 | tf_op jit(solution)/shard_map/ppermute | solution.py:414
  12.0 11.6 %collective-permute-start = (bf16[96,768]{1,0:T(8,128)(2,1)S(1)}, bf16[96,768]{1,0:T(8,128)(2,1)S(1)}, u32[]{:S(2)}, u32[]{:S(2)}) collective-permute-start(bf16[96,768]{1,0:T(8,128)(2,1)S(1)} %pack_kernel.2.rest_0_), channel_id=1, source_target_pairs={{0,8},{4,12},{8,0},{12,4},{16,24},{20,28},{24,16},{28,20},{1,9},{5... | collective-permute-start | bytes 442376 | tf_op jit(solution)/shard_map/ppermute | solution.py:414
  23.8 11.2 %collective-permute-start.6 = (bf16[3,96,768]{2,1,0:T(8,128)(2,1)S(1)}, bf16[3,96,768]{2,1,0:T(8,128)(2,1)S(1)}, u32[]{:S(2)}, u32[]{:S(2)}) collective-permute-start(bf16[3,96,768]{2,1,0:T(8,128)(2,1)S(1)} %pad_maximum_fusion.1), channel_id=1, source_target_pairs={{0,4},{4,0},{8,12},{12,8},{16,20},{20,16},{24,28},{28,24},{1,5},{5... | collective-permute-start | bytes 1327112 | tf_op jit(solution)/shard_map/ppermute | solution.py:414
  25.8 16.3 %collective-permute-start.11 = (bf16[96,864]{1,0:T(8,128)(2,1)S(1)}, bf16[96,864]{1,0:T(8,128)(2,1)S(1)}, u32[]{:S(2)}, u32[]{:S(2)}) collective-permute-start(bf16[96,864]{1,0:T(8,128)(2,1)S(1)} %pack_kernel.3.rest_0_), channel_id=1, source_target_pairs={{0,24},{4,28},{8,16},{12,20},{16,8},{20,12},{24,0},{28,4},{1,25},{... | collective-permute-start | bytes 497672 | tf_op jit(solution)/shard_map/ppermute | solution.py:414
  28.3 14.0 %collective-permute-start.10 = (bf16[96,864]{1,0:T(8,128)(2,1)S(1)}, bf16[96,864]{1,0:T(8,128)(2,1)S(1)}, u32[]{:S(2)}, u32[]{:S(2)}) collective-permute-start(bf16[96,864]{1,0:T(8,128)(2,1)S(1)} %pack_kernel.3.rest_0_), channel_id=1, source_target_pairs={{0,16},{4,20},{8,24},{12,28},{16,0},{20,4},{24,8},{28,12},{1,17},{... | collective-permute-start | bytes 497672 | tf_op jit(solution)/shard_map/ppermute | solution.py:414
  28.3 14.0 %collective-permute-start.9 = (bf16[96,864]{1,0:T(8,128)(2,1)S(1)}, bf16[96,864]{1,0:T(8,128)(2,1)S(1)}, u32[]{:S(2)}, u32[]{:S(2)}) collective-permute-start(bf16[96,864]{1,0:T(8,128)(2,1)S(1)} %pack_kernel.3.rest_0_), channel_id=1, source_target_pairs={{0,8},{4,12},{8,0},{12,4},{16,24},{20,28},{24,16},{28,20},{1,9},{5... | collective-permute-start | bytes 497672 | tf_op jit(solution)/shard_map/ppermute | solution.py:414
  30.2 12.0 %collective-permute-start.12 = (bf16[128,768]{1,0:T(8,128)(2,1)S(1)}, bf16[128,768]{1,0:T(8,128)(2,1)S(1)}, u32[]{:S(2)}, u32[]{:S(2)}) collective-permute-start(bf16[128,768]{1,0:T(8,128)(2,1)S(1)} %copy-done.1), channel_id=1, source_target_pairs={{0,2},{1,3},{2,0},{3,1},{4,6},{5,7},{6,4},{7,5},{8,10},{9,11},{10,... | collective-permute-start | bytes 589832 | tf_op jit(solution)/shard_map/ppermute | solution.py:414
  45.4 11.2 %collective-permute-start.14 = (bf16[256,768]{1,0:T(8,128)(2,1)S(1)}, bf16[256,768]{1,0:T(8,128)(2,1)S(1)}, u32[]{:S(2)}, u32[]{:S(2)}) collective-permute-start(bf16[256,768]{1,0:T(8,128)(2,1)S(1)} %add_convert_fusion.1.own), channel_id=1, source_target_pairs={{0,2},{1,3},{2,0},{3,1},{4,6},{5,7},{6,4},{7,5},{8,10},{9,11},{10,... | collective-permute-start | bytes 1179656 | tf_op jit(solution)/shard_map/ppermute | solution.py:414
  46.2 13.6 %collective-permute-start.18 = (bf16[3,96,864]{2,1,0:T(8,128)(2,1)S(1)}, bf16[3,96,864]{2,1,0:T(8,128)(2,1)S(1)}, u32[]{:S(2)}, u32[]{:S(2)}) collective-permute-start(bf16[3,96,864]{2,1,0:T(8,128)(2,1)S(1)} %pad_maximum_fusion), channel_id=1, source_target_pairs={{0,4},{4,0},{8,12},{12,8},{16,20},{20,16},{24,28},{28,24},{1,5},{5... | collective-permute-start | bytes 1493000 | tf_op jit(solution)/shard_map/ppermute | solution.py:414
  65.6 11.2 %collective-permute-start.20 = (bf16[256,768]{1,0:T(8,128)(2,1)S(1)}, bf16[256,768]{1,0:T(8,128)(2,1)S(1)}, u32[]{:S(2)}, u32[]{:S(2)}) collective-permute-start(bf16[256,768]{1,0:T(8,128)(2,1)S(1)} %add_convert_fusion.own), channel_id=1, source_target_pairs={{0,2},{1,3},{2,0},{3,1},{4,6},{5,7},{6,4},{7,5},{8,10},{9,11},{10,... | collective-permute-start | bytes 1179656 | tf_op jit(solution)/shard_map/ppermute | solution.py:414
  69.5 17.3 %collective-permute-start.22 = (bf16[4,96,864]{2,1,0:T(8,128)(2,1)S(1)}, bf16[4,96,864]{2,1,0:T(8,128)(2,1)S(1)}, u32[]{:S(2)}, u32[]{:S(2)}) collective-permute-start(bf16[4,96,864]{2,1,0:T(8,128)(2,1)S(1)} %get-tuple-element.149), channel_id=1, source_target_pairs={{0,4},{4,0},{8,12},{12,8},{16,20},{20,16},{24,28},{28,24},{1,5},{5... | collective-permute-start | bytes 1990664 | tf_op jit(solution)/shard_map/ppermute | solution.py:414
  77.5 15.2 %collective-permute-start.28 = (bf16[256,768]{1,0:T(8,128)(2,1)S(1)}, bf16[256,768]{1,0:T(8,128)(2,1)S(1)}, u32[]{:S(2)}, u32[]{:S(2)}) collective-permute-start(bf16[256,768]{1,0:T(8,128)(2,1)S(1)} %get-tuple-element.160), channel_id=1, source_target_pairs={{0,1},{1,0},{2,3},{3,2},{4,5},{5,4},{6,7},{7,6},{8,9},{9,8},{10,11... | collective-permute-start | bytes 1179656 | tf_op jit(solution)/shard_map/ppermute | solution.py:414
  91.2 15.3 %collective-permute-start.23 = (bf16[4,96,768]{2,1,0:T(8,128)(2,1)S(1)}, bf16[4,96,768]{2,1,0:T(8,128)(2,1)S(1)}, u32[]{:S(2)}, u32[]{:S(2)}) collective-permute-start(bf16[4,96,768]{2,1,0:T(8,128)(2,1)S(1)} %get-tuple-element.154), channel_id=1, source_target_pairs={{0,4},{4,0},{8,12},{12,8},{16,20},{20,16},{24,28},{28,24},{1,5},{5... | collective-permute-start | bytes 1769480 | tf_op jit(solution)/shard_map/ppermute | solution.py:414
  92.9 19.2 %collective-permute-start.33 = (bf16[256,768]{1,0:T(8,128)(2,1)S(1)}, bf16[256,768]{1,0:T(8,128)(2,1)S(1)}, u32[]{:S(2)}, u32[]{:S(2)}) collective-permute-start(bf16[256,768]{1,0:T(8,128)(2,1)S(1)} %pad_maximum_fusion.2), channel_id=1, source_target_pairs={{0,2},{1,3},{2,0},{3,1},{4,6},{5,7},{6,4},{7,5},{8,10},{9,11},{10,... | collective-permute-start | bytes 1179656 | tf_op jit(solution)/shard_map/ppermute | solution.py:414
  94.2 7.8 %collective-permute-start.24 = (bf16[96,864]{1,0:T(8,128)(2,1)S(1)}, bf16[96,864]{1,0:T(8,128)(2,1)S(1)}, u32[]{:S(2)}, u32[]{:S(2)}) collective-permute-start(bf16[96,864]{1,0:T(8,128)(2,1)S(1)} %get-tuple-element.157), channel_id=1, source_target_pairs={{0,8},{4,12},{8,0},{12,4},{16,24},{20,28},{24,16},{28,20},{1,9},{5... | collective-permute-start | bytes 497672 | tf_op jit(solution)/shard_map/ppermute | solution.py:414
  94.3 14.9 %collective-permute-start.34 = (bf16[96,864]{1,0:T(8,128)(2,1)S(1)}, bf16[96,864]{1,0:T(8,128)(2,1)S(1)}, u32[]{:S(2)}, u32[]{:S(2)}) collective-permute-start(bf16[96,864]{1,0:T(8,128)(2,1)S(1)} %get-tuple-element.177), channel_id=1, source_target_pairs={{0,16},{4,20},{8,24},{12,28},{16,0},{20,4},{24,8},{28,12},{1,17},{... | collective-permute-start | bytes 497672 | tf_op jit(solution)/shard_map/ppermute | solution.py:414
  96.0 10.5 %collective-permute-start.29 = (f32[2,768]{1,0:T(2,128)S(1)}, f32[2,768]{1,0:T(2,128)S(1)}, u32[]{:S(2)}, u32[]{:S(2)}) collective-permute-start(f32[2,768]{1,0:T(2,128)S(1)} %add.21.gains), channel_id=1, source_target_pairs={{0,4},{4,0},{8,12},{12,8},{16,20},{20,16},{24,28},{28,24},{1,5},{5... | collective-permute-start | bytes 18440 | tf_op jit(solution)/shard_map/ppermute | solution.py:414
  102.0 9.1 %collective-permute-start.35 = (bf16[96,864]{1,0:T(8,128)(2,1)S(1)}, bf16[96,864]{1,0:T(8,128)(2,1)S(1)}, u32[]{:S(2)}, u32[]{:S(2)}) collective-permute-start(bf16[96,864]{1,0:T(8,128)(2,1)S(1)} %get-tuple-element.178), channel_id=1, source_target_pairs={{0,24},{4,28},{8,16},{12,20},{16,8},{20,12},{24,0},{28,4},{1,25},{... | collective-permute-start | bytes 497672 | tf_op jit(solution)/shard_map/ppermute | solution.py:414
  106.7 16.9 %collective-permute-start.31 = (bf16[104,768]{1,0:T(8,128)(2,1)S(1)}, bf16[104,768]{1,0:T(8,128)(2,1)S(1)}, u32[]{:S(2)}, u32[]{:S(2)}) collective-permute-start(bf16[104,768]{1,0:T(8,128)(2,1)S(1)} %get-tuple-element.166), channel_id=1, source_target_pairs={{0,16},{4,20},{8,24},{12,28},{16,0},{20,4},{24,8},{28,12},{1,17},{... | collective-permute-start | bytes 479240 | tf_op jit(solution)/shard_map/ppermute | solution.py:414
  109.2 14.4 %collective-permute-start.32 = (bf16[104,768]{1,0:T(8,128)(2,1)S(1)}, bf16[104,768]{1,0:T(8,128)(2,1)S(1)}, u32[]{:S(2)}, u32[]{:S(2)}) collective-permute-start(bf16[104,768]{1,0:T(8,128)(2,1)S(1)} %get-tuple-element.167), channel_id=1, source_target_pairs={{0,24},{4,28},{8,16},{12,20},{16,8},{20,12},{24,0},{28,4},{1,25},{... | collective-permute-start | bytes 479240 | tf_op jit(solution)/shard_map/ppermute | solution.py:414
  (24 other events, 76.8 us)

commit v5 on v4

--- a/solution.py
+++ b/solution.py
@@ -121,8 +121,8 @@
 
 def attend_kernel(offsets, n_pieces, rows, ids, n1, cosine, sine, *rest):
     pieces = rest[:n_pieces]
-    q_out, k_out, v_out, probs_out, att_out, whole, out_w = rest[n_pieces : n_pieces + 7]
-    k_pad, v_pad = rest[n_pieces + 7 :]
+    q_out, k_out, v_out, probs_out, att_out, whole, out_w, send, keep = rest[n_pieces : n_pieces + 9]
+    k_pad, v_pad = rest[n_pieces + 9 :]
     put_pieces(ids, offsets, pieces, whole, out_w, rows)
     half = WINDOW // 2
     width = q_out.shape[1]
@@ -152,6 +152,7 @@
     column = lax.broadcasted_iota(jnp.int32, (WINDOW, span), 1)
     row = lax.broadcasted_iota(jnp.int32, (WINDOW, span), 0)
     near = jnp.abs(row + half - column) <= half
+    lanes = [head_lanes((WINDOW, width), h) for h in range(heads)]
     for b in range(blocks):
         rows_b = slice(b * WINDOW, (b + 1) * WINDOW)
         span_b = slice(b * WINDOW, b * WINDOW + span)
@@ -165,29 +166,23 @@
         allowed = near & (column < limit) & (row < count[b])
         spare = (lax.broadcasted_iota(jnp.int32, (WINDOW, 1), 0) >= count[b]).astype(F32)
         q_b = q_out[rows_b, :]
-        keys = k_pad[span_b, :]
-        values = v_pad[span_b, :]
+        stacked = jnp.concatenate([jnp.where(mine, q_b, 0) for mine in lanes], axis=0)
+        scores = dot(stacked, k_pad[span_b, :], NT) * (HEAD_DIM**-0.5)
+        allowed = jnp.concatenate([allowed] * heads, axis=0)
+        masked = jnp.where(allowed, scores, NEG_FILL)
+        peak = jnp.max(masked, axis=-1, keepdims=True)
+        raised = jnp.where(allowed, jnp.exp(masked - peak), 0.0)
+        total = jnp.sum(raised, axis=-1, keepdims=True) + jnp.concatenate([spare] * heads, axis=0)
+        probs = (raised * (1.0 / total)).astype(BF)
+        parts = dot(probs, v_pad[span_b, :])
         mixed = jnp.zeros((WINDOW, width), F32)
-        for h in range(heads):
-            mine = head_lanes((WINDOW, width), h)
-            scores = dot(jnp.where(mine, q_b, 0), keys, NT) * (HEAD_DIM**-0.5)
-            masked = jnp.where(allowed, scores, NEG_FILL)
-            peak = jnp.max(masked, axis=-1, keepdims=True)
-            raised = jnp.where(allowed, jnp.exp(masked - peak), 0.0)
-            total = jnp.sum(raised, axis=-1, keepdims=True) + spare
-            probs = (raised * (1.0 / total)).astype(BF)
-            probs_out[h, rows_b, :] = probs
-            mixed = jnp.where(mine, dot(probs, values), mixed)
+        for h, mine in enumerate(lanes):
+            rows_h = slice(h * WINDOW, (h + 1) * WINDOW)
+            probs_out[h, rows_b, :] = probs[rows_h, :]
+            mixed = jnp.where(mine, parts[rows_h, :], mixed)
         att_out[rows_b, :] = mixed.astype(BF)
-
-
-def collect_kernel(offsets, n_pieces, rows, ids, *rest):
-    put_pieces(ids, offsets, rest[:n_pieces], rest[n_pieces], rest[n_pieces + 1], rows)
-
-
-def project_kernel(ids, att, out_w, send, keep):
-    for i in range(4):
-        part = dot(att[rows_of(ids[i]), :], out_w[...], NT)
+    for i in (2, 3, 0, 1):
+        part = dot(att_out[rows_of(ids[i]), :], out_w[...], NT)
         at = slice((i % 2) * WINDOW, (i % 2 + 1) * WINDOW)
         if i < 2:
             keep[at, :] = part
@@ -206,7 +201,9 @@
         n2_out[at, :] = (unit * gain[...].astype(F32)).astype(BF)
 
 
-def units_kernel(n2, n2_far, c0, c1, c2, c3, in_w, down_w, send, keep, both_out, act_out):
+def units_kernel(offsets, n_pieces, rows, ids, n2, n2_far, c0, c1, c2, c3, *rest):
+    send, keep, both_out, act_out, down_w, in_w = rest[n_pieces:]
+    put_pieces(ids, offsets, rest[:n_pieces], in_w, down_w, rows)
     units = act_out.shape[1]
     gate_w, up_w = in_w[:, :units], in_w[:, units:]
     for i in (2, 3, 0, 1):
@@ -288,6 +285,7 @@
         pad[0:half, :] = jnp.zeros((half, width), BF)
         pad[half + total_rows :, :] = jnp.zeros((half, width), BF)
         pad[half : half + total_rows, :] = source[...]
+    lanes = [head_lanes((WINDOW, width), h) for h in range(heads)]
     gk_pad[...] = jnp.zeros(gk_pad.shape, F32)
     gv_pad[...] = jnp.zeros(gv_pad.shape, F32)
     for b in range(blocks):
@@ -297,20 +295,19 @@
         q_b = q_in[rows_b, :]
         keys = k_pad[span_b, :]
         values = v_pad[span_b, :]
+        g_stacked = jnp.concatenate([jnp.where(mine, g_att, 0) for mine in lanes], axis=0)
+        q_stacked = jnp.concatenate([jnp.where(mine, q_b, 0) for mine in lanes], axis=0)
+        probs = jnp.concatenate([probs_in[h, rows_b, :] for h in range(heads)], axis=0)
+        wide = probs.astype(F32)
+        g_probs = dot(g_stacked, values, NT)
+        delta = jnp.sum(wide * g_probs, axis=-1, keepdims=True)
+        g_scores = (wide * (g_probs - delta)).astype(BF)
+        parts = dot(g_scores, keys)
         gq = jnp.zeros((WINDOW, width), F32)
-        gk = jnp.zeros((span, width), F32)
-        gv = jnp.zeros((span, width), F32)
-        for h in range(heads):
-            mine = head_lanes((WINDOW, width), h)
-            g_mine = jnp.where(mine, g_att, 0)
-            probs = probs_in[h, rows_b, :]
-            wide = probs.astype(F32)
-            g_probs = dot(g_mine, values, NT)
-            delta = jnp.sum(wide * g_probs, axis=-1, keepdims=True)
-            g_scores = (wide * (g_probs - delta)).astype(BF)
-            gq = jnp.where(mine, dot(g_scores, keys), gq)
-            gk = gk + dot(g_scores, jnp.where(mine, q_b, 0), TN)
-            gv = gv + dot(probs, g_mine, TN)
+        for h, mine in enumerate(lanes):
+            gq = jnp.where(mine, parts[h * WINDOW : (h + 1) * WINDOW, :], gq)
+        gk = dot(g_scores, q_stacked, TN)
+        gv = dot(probs, g_stacked, TN)
         gq_all[rows_b, :] = gq
         gk_pad[span_b, :] += gk
         gv_pad[span_b, :] += gv
@@ -444,10 +441,17 @@
         pairs = [(4 * d + t, 4 * (d ^ 1) + (t ^ 2)) for d in range(n_dp) for t in range(4)]
         return lax.ppermute(values, ("dp", "tensor"), pairs)
 
-    def along(value):
+    pin = lax.optimization_barrier
+
+    def along(value, wait=None):
         if not slots:
             return [lax.all_gather(value, "dp", axis=0, tiled=True)]
-        return [dp(value, bit=2 * k) for k in range(1, slots)]
+        pieces = {0: value}
+        for bit in reversed([1 << b for b in range(1, slots.bit_length())]):
+            pieces.update({have ^ bit: dp(piece, bit=bit) for have, piece in pieces.items()})
+            if wait is not None and len(pieces) == 2:
+                pieces[bit], _ = pin((pieces[bit], wait))
+        return [pieces[2 * k] for k in range(1, slots)]
 
     def aside(pieces):
         if not slots:
@@ -499,7 +503,6 @@
     freq = jnp.asarray(np.tile(freqs, 128 // (HEAD_DIM // 2))[None, :], F32)
 
     offsets = tuple(range(0, n_dp, 2)) + tuple(range(1, n_dp, 2)) if slots else None
-    pin = lax.optimization_barrier
 
     def pack(wide, tall):
         count, _, each = wide.shape
@@ -539,12 +542,14 @@
         (ids,),
     )
     unit_own, cot, _ = pin((unit_own, cotangent, qkv_near))
-    unit_near = along(unit_own)
+    unit_near = along(unit_own, n1)
     cot_across = across(cot)
     qkv_far, n1 = pin((qkv_far, n1))
     qkv_pieces = picked(qkv_own, qkv_near, qkv_far)
     flat = shape(total_rows, head_width)
-    query, keys, values, probs, attended, qkv_w, out_w = call(
+    pair_f32 = shape(pair_rows, width, dtype=F32)
+    pair_bf = shape(pair_rows, width)
+    query, keys, values, probs, attended, qkv_w, out_w, a_send, a_keep = call(
         functools.partial(attend_kernel, offsets, len(qkv_pieces), shard),
         (
             flat,
@@ -554,31 +559,18 @@
             flat,
             shape(width, 3 * head_width),
             shape(width, head_width),
+            pair_bf,
+            pair_f32,
         ),
         (n1, cosine, sine) + qkv_pieces,
         (ids,),
         [pltpu.VMEM((total_rows + WINDOW, head_width), BF)] * 2,
         flops=2 * total_rows * width * 3 * head_width,
     )
-    attended, unit_near, cot_across = pin((attended, unit_near, cot_across))
+    a_send, unit_near, cot_across = pin((a_send, unit_near, cot_across))
     cot_blocks = (cotangent, cot_across, core(cot), core(cot_across))
     unit_far = unit_side + aside(unit_near)
     unit_pieces = picked(unit_own, unit_near, unit_far)
-    in_w, down_w = call(
-        functools.partial(collect_kernel, offsets, len(unit_pieces), shard),
-        (shape(width, 2 * units), shape(width, units)),
-        unit_pieces,
-        (ids,),
-    )
-    pair_f32 = shape(pair_rows, width, dtype=F32)
-    pair_bf = shape(pair_rows, width)
-    a_send, a_keep = call(
-        project_kernel,
-        (pair_bf, pair_f32),
-        (attended, out_w),
-        (ids,),
-        flops=2 * total_rows * width * head_width,
-    )
     a_sum = (a_keep + core(a_send).astype(F32)).astype(BF)
     a_got = across(a_sum)
     h, n2 = call(
@@ -587,11 +579,18 @@
         (a_sum, a_got, token_blocks[0], token_blocks[1], gain_two),
     )
     n2_far = core(n2)
-    u_send, u_keep, both, act = call(
-        units_kernel,
-        (pair_bf, pair_f32, shape(total_rows, 2 * units), shape(total_rows, units)),
-        (n2, n2_far) + cot_blocks + (in_w, down_w),
-        flops=2 * total_rows * width * 5 * units,
+    u_send, u_keep, both, act, down_w = call(
+        functools.partial(units_kernel, offsets, len(unit_pieces), shard),
+        (
+            pair_bf,
+            pair_f32,
+            shape(total_rows, 2 * units),
+            shape(total_rows, units),
+            shape(width, units),
+        ),
+        (n2, n2_far) + cot_blocks + unit_pieces,
+        (ids,),
+        [pltpu.VMEM((width, 2 * units), BF)],
     )
     u_sum = (u_keep + core(u_send).astype(F32)).astype(BF)
     u_got = across(u_sum)

time: 125 us -> 120 us (0.960)
  Pallas kernels: 29.7 us -> 25.1 us
  starting transfers between devices: 36.6 us -> 37.9 us
    pallas_call x17 -> x15, Pallas kernels: 29.7 us -> 25.1 us  [call(): pl.pallas_call(kernel, name=getattr(kernel, 'func', kernel).__name__, out...]
    unnamed x25 -> x23, local copies, waits for them, and re-layouts: 4.81 us -> 3.8 us
  transfers between devices with their start and end apart: 36 -> 36, of which waited for: 17 -> 18; matrix products, arithmetic and copies ran while one was open for 0% -> 0% of each run, Pallas kernels for 19% -> 17%
where the time goes in v5:
time: 120 us; the launch traced here: 119 us
  waiting for transfers between devices  50.8 us (42%)
  starting transfers between devices  37.9 us (32%)
  Pallas kernels  25.1 us (21%)
  local copies, waits for them, and re-layouts  3.97 us (3%)
    ppermute x36, waiting for transfers between devices, swap(): return lax.ppermute(values, axis, [(i, i ^ bit) for i in range(size)])  50.8 us
    ppermute x36, starting transfers between devices, swap(): return lax.ppermute(values, axis, [(i, i ^ bit) for i in range(size)])  37.9 us
    pallas_call x15, Pallas kernels, call(): pl.pallas_call(kernel, name=getattr(kernel, 'func', kernel).__name__, out...  25.1 us
    unnamed x23, local copies, waits for them, and re-layouts  3.8 us
  transfers between devices with their start and end apart: 36, of which 18 were waited for; matrix products, arithmetic and copies ran while one was open for 0% of the time, Pallas kernels for 17%

profile of v5, /device:TPU:0, one launch (start us, length us, event | category | flops | bytes accessed | tf_op | source)
XLA Modules:
  0.0 119.0 jit_solution(14464732431624683662)
XLA Ops:
  2.8 4.1 %collective-permute-start.1 = (bf16[96,768]{1,0:T(8,128)(2,1)S(1)}, bf16[96,768]{1,0:T(8,128)(2,1)S(1)}, u32[]{:S(2)}, u32[]{:S(2)}) collective-permute-start(bf16[96,768]{1,0:T(8,128)(2,1)S(1)} %pack_kernel.2.rest_0_), channel_id=1, source_target_pairs={{0,16},{4,20},{8,24},{12,28},{16,0},{20,4},{24,8},{28,12},{1,17},{... | collective-permute-start | bytes 442376 | tf_op jit(solution)/shard_map/ppermute | solution.py:411
  17.8 2.4 %collective-permute-done.2.rest_3_ = bf16[96,768]{1,0:T(8,128)(2,1)S(1)} collective-permute-done((bf16[96,768]{1,0:T(8,128)(2,1)S(1)}, bf16[96,768]{1,0:T(8,128)(2,1)S(1)}, u32[]{:S(2)}, u32[]{:S(2)}) %collective-permute-start.2) | collective-permute-done | bytes 147488 | tf_op jit(solution)/shard_map/ppermute | solution.py:411
  22.4 1.8 %collective-permute-start.10 = (bf16[96,864]{1,0:T(8,128)(2,1)S(1)}, bf16[96,864]{1,0:T(8,128)(2,1)S(1)}, u32[]{:S(2)}, u32[]{:S(2)}) collective-permute-start(bf16[96,864]{1,0:T(8,128)(2,1)S(1)} %pack_kernel.3.rest_0_), channel_id=1, source_target_pairs={{0,16},{4,20},{8,24},{12,28},{16,0},{20,4},{24,8},{28,12},{1,17},{... | collective-permute-start | bytes 497672 | tf_op jit(solution)/shard_map/ppermute | solution.py:411
  24.2 1.7 %collective-permute-start.9 = (bf16[96,864]{1,0:T(8,128)(2,1)S(1)}, bf16[96,864]{1,0:T(8,128)(2,1)S(1)}, u32[]{:S(2)}, u32[]{:S(2)}) collective-permute-start(bf16[96,864]{1,0:T(8,128)(2,1)S(1)} %pack_kernel.3.rest_0_), channel_id=1, source_target_pairs={{0,8},{4,12},{8,0},{12,4},{16,24},{20,28},{24,16},{28,20},{1,9},{5... | collective-permute-start | bytes 497672 | tf_op jit(solution)/shard_map/ppermute | solution.py:411
  27.5 2.0 %prepare_kernel.1 = (bf16[512,768]{1,0:T(8,128)(2,1)S(1)}, f32[512,128]{1,0:T(8,128)S(1)}, f32[512,128]{1,0:T(8,128)S(1)}) custom-call(s32[13]{0:T(128)S(1)} %concatenate.6.ids, bf16[128,768]{1,0:T(8,128)(2,1)S(1)} %copy-done, bf16[128,768]{1,0:T(8,128)(2,1)S(1)} %collective-permute-done.5.t1, bf16[128,768]{1,0:T(8,128)(2,1)S(1)} %collective-permute-done.7.t2, ...), custom_call_target="tpu_custom_call" | custom-call | flops 1 | bytes 1 | tf_op jit(solution)/shard_map/prepare_kernel/pallas_call | solution.py:30
  29.5 3.9 %collective-permute-done.10.rest_2_ = bf16[96,864]{1,0:T(8,128)(2,1)S(1)} collective-permute-done((bf16[96,864]{1,0:T(8,128)(2,1)S(1)}, bf16[96,864]{1,0:T(8,128)(2,1)S(1)}, u32[]{:S(2)}, u32[]{:S(2)}) %collective-permute-start.10) | collective-permute-done | bytes 165920 | tf_op jit(solution)/shard_map/ppermute | solution.py:411
  33.4 4.2 %attend_kernel.1 = (bf16[512,192]{1,0:T(8,128)(2,1)S(1)}, bf16[512,192]{1,0:T(8,128)(2,1)S(1)}, bf16[512,192]{1,0:T(8,128)(2,1)S(1)}, bf16[3,512,256]{2,1,0:T(8,...) custom-call(s32[13]{0:T(128)S(1)} %concatenate.6.ids, ...), custom_call_target="tpu_custom_call" | custom-call | flops 1 | bytes 1 | tf_op jit(solution)/shard_map/attend_kernel/pallas_call | solution.py:30
  39.3 1.7 %collective-permute-done.13 = bf16[256,768]{1,0:T(8,128)(2,1)S(1)} collective-permute-done((bf16[256,768]{1,0:T(8,128)(2,1)S(1)}, bf16[256,768]{1,0:T(8,128)(2,1)S(1)}, u32[]{:S(2)}, u32[]{:S(2)}) %collective-permute-start.13) | collective-permute-done | bytes 393248 | tf_op jit(solution)/shard_map/ppermute | solution.py:411
  42.3 10.0 %collective-permute-done.14.received = bf16[256,768]{1,0:T(8,128)(2,1)S(1)} collective-permute-done((bf16[256,768]{1,0:T(8,128)(2,1)S(1)}, bf16[256,768]{1,0:T(8,128)(2,1)S(1)}, u32[]{:S(2)}, u32[]{:S(2)}) %collective-permute-start.14) | collective-permute-done | bytes 393248 | tf_op jit(solution)/shard_map/ppermute | solution.py:411
  53.3 1.9 %collective-permute-done.18 = bf16[3,96,864]{2,1,0:T(8,128)(2,1)S(1)} collective-permute-done((bf16[3,96,864]{2,1,0:T(8,128)(2,1)S(1)}, bf16[3,96,864]{2,1,0:T(8,128)(2,1)S(1)}, u32[]{:S(2)}, u32[]{:S(2)}) %collective-permute-start.18) | collective-permute-done | bytes 497696 | tf_op jit(solution)/shard_map/ppermute | solution.py:411
  55.3 3.8 %units_kernel.1 = (bf16[256,768]{1,0:T(8,128)(2,1)S(1)}, f32[256,768]{1,0:T(8,128)S(1)}, bf16[512,576]{1,0:T(8,128)(2,1)S(1)}, bf16[512,288]{1,0:T(8,128)(2,1)S(1)}, bf16[768,288]{1,0:T(8,128)(2,1)S(1)}) custom-call(s32[13]{0:T(128)S(1)} %concatenate.6.ids, bf16[256,768]{1,0:T(8,128)(2,1)S(1)} %get-tuple-element.123.n2, ...), custom_call_target="tpu_custom_call" | custom-call | flops 1 | bytes 1 | tf_op jit(solution)/shard_map/units_kernel/pallas_call | solution.py:30
  59.2 1.7 %collective-permute-done.19 = bf16[256,768]{1,0:T(8,128)(2,1)S(1)} collective-permute-done((bf16[256,768]{1,0:T(8,128)(2,1)S(1)}, bf16[256,768]{1,0:T(8,128)(2,1)S(1)}, u32[]{:S(2)}, u32[]{:S(2)}) %collective-permute-start.19) | collective-permute-done | bytes 393248 | tf_op jit(solution)/shard_map/ppermute | solution.py:411
  61.0 1.7 %collective-permute-start.20 = (bf16[256,768]{1,0:T(8,128)(2,1)S(1)}, bf16[256,768]{1,0:T(8,128)(2,1)S(1)}, u32[]{:S(2)}, u32[]{:S(2)}) collective-permute-start(bf16[256,768]{1,0:T(8,128)(2,1)S(1)} %add_convert_fusion.own), channel_id=1, source_target_pairs={{0,2},{1,3},{2,0},{3,1},{4,6},{5,7},{6,4},{7,5},{8,10},{9,11},{10,... | collective-permute-start | bytes 1179656 | tf_op jit(solution)/shard_map/ppermute | solution.py:411
  62.7 2.4 %unit_grads_kernel.1 = (bf16[4,96,864]{2,1,0:T(8,128)(2,1)S(1)}, bf16[4,96,864]{2,1,0:T(8,128)(2,1)S(1)}, bf16[256,768]{1,0:T(8,128)(2,1)S(1)}, f32[256,768]{1,0:T(8,128)S(1)}) custom-call(s32[13]{0:T(128)S(1)} %concatenate.6.ids, bf16[256,768]{1,0:T(8,128)(2,1)S(1)} %get-tuple-element.123.n2, bf16[256,768]{1,0:T(8,128)(2,1)S(1)} %collective-permute-done.15.n2_far, ...), custom_call_target="tpu_custom_call" | custom-call | flops 1 | bytes 1 | tf_op jit(solution)/shard_map/unit_grads_kernel/pallas_call | solution.py:30
  65.5 6.7 %collective-permute-done.20.received = bf16[256,768]{1,0:T(8,128)(2,1)S(1)} collective-permute-done((bf16[256,768]{1,0:T(8,128)(2,1)S(1)}, bf16[256,768]{1,0:T(8,128)(2,1)S(1)}, u32[]{:S(2)}, u32[]{:S(2)}) %collective-permute-start.20) | collective-permute-done | bytes 393248 | tf_op jit(solution)/shard_map/ppermute | solution.py:411
  74.8 5.8 %attend_back_kernel.1 = (bf16[512,576]{1,0:T(8,128)(2,1)S(1)}, bf16[256,768]{1,0:T(8,128)(2,1)S(1)}, f32[256,768]{1,0:T(8,128)S(1)}, f32[2,768]{1,0:T(2,128)S(1)}) custom-call(s32[13]{0:T(128)S(1)} %concatenate.6.ids, bf16[256,768]{1,0:T(8,128)(2,1)S(1)} %get-tuple-element.137.gy, bf16[256,768]{1,0:T(8,128)(2,1)S(1)} %collective-permute-done.21.gy_far, ...), custom_call_target="tpu_custom_call" | custom-call | flops 1 | bytes 1 | tf_op jit(solution)/shard_map/attend_back_kernel/pallas_call | solution.py:30
  80.6 1.7 %collective-permute-done.22.got = bf16[4,96,864]{2,1,0:T(8,128)(2,1)S(1)} collective-permute-done((bf16[4,96,864]{2,1,0:T(8,128)(2,1)S(1)}, bf16[4,96,864]{2,1,0:T(8,128)(2,1)S(1)}, u32[]{:S(2)}, u32[]{:S(2)}) %collective-permute-start.22) | collective-permute-done | bytes 663584 | tf_op jit(solution)/shard_map/ppermute | solution.py:411
  84.5 1.7 %attend_grads_kernel.1 = (bf16[4,96,768]{2,1,0:T(8,128)(2,1)S(1)}, bf16[4,96,768]{2,1,0:T(8,128)(2,1)S(1)}) custom-call(s32[13]{0:T(128)S(1)} %concatenate.6.ids, bf16[512,768]{1,0:T(8,128)(2,1)S(1)} %get-tuple-element.109.n1, bf16[512,576]{1,0:T(8,128)(2,1)S(1)} %get-tuple-element.150.g_raw, bf16[256,768]{1,0:T(8,128)(2,1)S(1)} %get-tuple-element.137.gy, ...), custom_call_target="tpu_custom_call" | custom-call | flops 1 | bytes 1 | tf_op jit(solution)/shard_map/attend_grads_kernel/pallas_call | solution.py:30
  89.8 3.4 %collective-permute-start.34 = (bf16[96,864]{1,0:T(8,128)(2,1)S(1)}, bf16[96,864]{1,0:T(8,128)(2,1)S(1)}, u32[]{:S(2)}, u32[]{:S(2)}) collective-permute-start(bf16[96,864]{1,0:T(8,128)(2,1)S(1)} %get-tuple-element.177), channel_id=1, source_target_pairs={{0,16},{4,20},{8,24},{12,28},{16,0},{20,4},{24,8},{28,12},{1,17},{... | collective-permute-start | bytes 497672 | tf_op jit(solution)/shard_map/ppermute | solution.py:411
  93.9 3.3 %collective-permute-done.24.rest_0_ = bf16[96,864]{1,0:T(8,128)(2,1)S(1)} collective-permute-done((bf16[96,864]{1,0:T(8,128)(2,1)S(1)}, bf16[96,864]{1,0:T(8,128)(2,1)S(1)}, u32[]{:S(2)}, u32[]{:S(2)}) %collective-permute-start.24) | collective-permute-done | bytes 165920 | tf_op jit(solution)/shard_map/ppermute | solution.py:411
  97.2 2.5 %collective-permute-start.35 = (bf16[96,864]{1,0:T(8,128)(2,1)S(1)}, bf16[96,864]{1,0:T(8,128)(2,1)S(1)}, u32[]{:S(2)}, u32[]{:S(2)}) collective-permute-start(bf16[96,864]{1,0:T(8,128)(2,1)S(1)} %get-tuple-element.178), channel_id=1, source_target_pairs={{0,24},{4,28},{8,16},{12,20},{16,8},{20,12},{24,0},{28,4},{1,25},{... | collective-permute-start | bytes 497672 | tf_op jit(solution)/shard_map/ppermute | solution.py:411
  99.7 1.8 %collective-permute-done.29.gains_got = f32[2,768]{1,0:T(2,128)S(1)} collective-permute-done((f32[2,768]{1,0:T(2,128)S(1)}, f32[2,768]{1,0:T(2,128)S(1)}, u32[]{:S(2)}, u32[]{:S(2)}) %collective-permute-start.29) | collective-permute-done | bytes 6176 | tf_op jit(solution)/shard_map/ppermute | solution.py:411
  103.0 3.4 %collective-permute-start.31 = (bf16[104,768]{1,0:T(8,128)(2,1)S(1)}, bf16[104,768]{1,0:T(8,128)(2,1)S(1)}, u32[]{:S(2)}, u32[]{:S(2)}) collective-permute-start(bf16[104,768]{1,0:T(8,128)(2,1)S(1)} %get-tuple-element.166), channel_id=1, source_target_pairs={{0,16},{4,20},{8,24},{12,28},{16,0},{20,4},{24,8},{28,12},{1,17},{... | collective-permute-start | bytes 479240 | tf_op jit(solution)/shard_map/ppermute | solution.py:411
  109.9 8.3 %collective-permute-done.31.rest_1_ = bf16[104,768]{1,0:T(8,128)(2,1)S(1)} collective-permute-done((bf16[104,768]{1,0:T(8,128)(2,1)S(1)}, bf16[104,768]{1,0:T(8,128)(2,1)S(1)}, u32[]{:S(2)}, u32[]{:S(2)}) %collective-permute-start.31) | collective-permute-done | bytes 159776 | tf_op jit(solution)/shard_map/ppermute | solution.py:411
  (99 shorter events, 36.2 us)
Async XLA Ops:
  2.8 11.2 %collective-permute-start.1 = (bf16[96,768]{1,0:T(8,128)(2,1)S(1)}, bf16[96,768]{1,0:T(8,128)(2,1)S(1)}, u32[]{:S(2)}, u32[]{:S(2)}) collective-permute-start(bf16[96,768]{1,0:T(8,128)(2,1)S(1)} %pack_kernel.2.rest_0_), channel_id=1, source_target_pairs={{0,16},{4,20},{8,24},{12,28},{16,0},{20,4},{24,8},{28,12},{1,17},{... | collective-permute-start | bytes 442376 | tf_op jit(solution)/shard_map/ppermute | solution.py:411
  6.9 10.9 %collective-permute-start.5 = (bf16[128,768]{1,0:T(8,128)(2,1)S(1)}, bf16[128,768]{1,0:T(8,128)(2,1)S(1)}, u32[]{:S(2)}, u32[]{:S(2)}) collective-permute-start(bf16[128,768]{1,0:T(8,128)(2,1)S(1)} %copy-done), channel_id=1, source_target_pairs={{0,2},{1,3},{2,0},{3,1},{4,6},{5,7},{6,4},{7,5},{8,10},{9,11},{10,... | collective-permute-start | bytes 589832 | tf_op jit(solution)/shard_map/ppermute | solution.py:411
  8.9 8.9 %collective-permute-start.4 = (bf16[96,864]{1,0:T(8,128)(2,1)S(1)}, bf16[96,864]{1,0:T(8,128)(2,1)S(1)}, u32[]{:S(2)}, u32[]{:S(2)}) collective-permute-start(bf16[96,864]{1,0:T(8,128)(2,1)S(1)} %pack_kernel.3.rest_0_), channel_id=1, source_target_pairs={{0,4},{4,0},{8,12},{12,8},{16,20},{20,16},{24,28},{28,24},{1,5},{5... | collective-permute-start | bytes 497672 | tf_op jit(solution)/shard_map/ppermute | solution.py:411
  10.5 7.2 %collective-permute-start.3 = (bf16[96,768]{1,0:T(8,128)(2,1)S(1)}, bf16[96,768]{1,0:T(8,128)(2,1)S(1)}, u32[]{:S(2)}, u32[]{:S(2)}) collective-permute-start(bf16[96,768]{1,0:T(8,128)(2,1)S(1)} %pack_kernel.2.rest_0_), channel_id=1, source_target_pairs={{0,4},{4,0},{8,12},{12,8},{16,20},{20,16},{24,28},{28,24},{1,5},{5... | collective-permute-start | bytes 442376 | tf_op jit(solution)/shard_map/ppermute | solution.py:411
  11.0 6.8 %collective-permute-start = (bf16[96,768]{1,0:T(8,128)(2,1)S(1)}, bf16[96,768]{1,0:T(8,128)(2,1)S(1)}, u32[]{:S(2)}, u32[]{:S(2)}) collective-permute-start(bf16[96,768]{1,0:T(8,128)(2,1)S(1)} %pack_kernel.2.rest_0_), channel_id=1, source_target_pairs={{0,8},{4,12},{8,0},{12,4},{16,24},{20,28},{24,16},{28,20},{1,9},{5... | collective-permute-start | bytes 442376 | tf_op jit(solution)/shard_map/ppermute | solution.py:411
  14.0 6.2 %collective-permute-start.2 = (bf16[96,768]{1,0:T(8,128)(2,1)S(1)}, bf16[96,768]{1,0:T(8,128)(2,1)S(1)}, u32[]{:S(2)}, u32[]{:S(2)}) collective-permute-start(bf16[96,768]{1,0:T(8,128)(2,1)S(1)} %collective-permute-done.1.rest_2_), channel_id=1, source_target_pairs={{0,8},{4,12},{8,0},{12,4},{16,24},{20,28},{24,16},{28,20},{1,9},{5... | collective-permute-start | bytes 442376 | tf_op jit(solution)/shard_map/ppermute | solution.py:411
  20.3 13.1 %collective-permute-start.6 = (bf16[3,96,768]{2,1,0:T(8,128)(2,1)S(1)}, bf16[3,96,768]{2,1,0:T(8,128)(2,1)S(1)}, u32[]{:S(2)}, u32[]{:S(2)}) collective-permute-start(bf16[3,96,768]{2,1,0:T(8,128)(2,1)S(1)} %pad_maximum_fusion.1), channel_id=1, source_target_pairs={{0,4},{4,0},{8,12},{12,8},{16,20},{20,16},{24,28},{28,24},{1,5},{5... | collective-permute-start | bytes 1327112 | tf_op jit(solution)/shard_map/ppermute | solution.py:411
  22.4 11.0 %collective-permute-start.10 = (bf16[96,864]{1,0:T(8,128)(2,1)S(1)}, bf16[96,864]{1,0:T(8,128)(2,1)S(1)}, u32[]{:S(2)}, u32[]{:S(2)}) collective-permute-start(bf16[96,864]{1,0:T(8,128)(2,1)S(1)} %pack_kernel.3.rest_0_), channel_id=1, source_target_pairs={{0,16},{4,20},{8,24},{12,28},{16,0},{20,4},{24,8},{28,12},{1,17},{... | collective-permute-start | bytes 497672 | tf_op jit(solution)/shard_map/ppermute | solution.py:411
  24.2 13.4 %collective-permute-start.9 = (bf16[96,864]{1,0:T(8,128)(2,1)S(1)}, bf16[96,864]{1,0:T(8,128)(2,1)S(1)}, u32[]{:S(2)}, u32[]{:S(2)}) collective-permute-start(bf16[96,864]{1,0:T(8,128)(2,1)S(1)} %pack_kernel.3.rest_0_), channel_id=1, source_target_pairs={{0,8},{4,12},{8,0},{12,4},{16,24},{20,28},{24,16},{28,20},{1,9},{5... | collective-permute-start | bytes 497672 | tf_op jit(solution)/shard_map/ppermute | solution.py:411
  26.0 11.7 %collective-permute-start.12 = (bf16[128,768]{1,0:T(8,128)(2,1)S(1)}, bf16[128,768]{1,0:T(8,128)(2,1)S(1)}, u32[]{:S(2)}, u32[]{:S(2)}) collective-permute-start(bf16[128,768]{1,0:T(8,128)(2,1)S(1)} %copy-done.1), channel_id=1, source_target_pairs={{0,2},{1,3},{2,0},{3,1},{4,6},{5,7},{6,4},{7,5},{8,10},{9,11},{10,... | collective-permute-start | bytes 589832 | tf_op jit(solution)/shard_map/ppermute | solution.py:411
  41.1 11.2 %collective-permute-start.14 = (bf16[256,768]{1,0:T(8,128)(2,1)S(1)}, bf16[256,768]{1,0:T(8,128)(2,1)S(1)}, u32[]{:S(2)}, u32[]{:S(2)}) collective-permute-start(bf16[256,768]{1,0:T(8,128)(2,1)S(1)} %add_convert_fusion.1.own), channel_id=1, source_target_pairs={{0,2},{1,3},{2,0},{3,1},{4,6},{5,7},{6,4},{7,5},{8,10},{9,11},{10,... | collective-permute-start | bytes 1179656 | tf_op jit(solution)/shard_map/ppermute | solution.py:411
  41.7 13.6 %collective-permute-start.18 = (bf16[3,96,864]{2,1,0:T(8,128)(2,1)S(1)}, bf16[3,96,864]{2,1,0:T(8,128)(2,1)S(1)}, u32[]{:S(2)}, u32[]{:S(2)}) collective-permute-start(bf16[3,96,864]{2,1,0:T(8,128)(2,1)S(1)} %pad_maximum_fusion), channel_id=1, source_target_pairs={{0,4},{4,0},{8,12},{12,8},{16,20},{20,16},{24,28},{28,24},{1,5},{5... | collective-permute-start | bytes 1493000 | tf_op jit(solution)/shard_map/ppermute | solution.py:411
  61.0 11.2 %collective-permute-start.20 = (bf16[256,768]{1,0:T(8,128)(2,1)S(1)}, bf16[256,768]{1,0:T(8,128)(2,1)S(1)}, u32[]{:S(2)}, u32[]{:S(2)}) collective-permute-start(bf16[256,768]{1,0:T(8,128)(2,1)S(1)} %add_convert_fusion.own), channel_id=1, source_target_pairs={{0,2},{1,3},{2,0},{3,1},{4,6},{5,7},{6,4},{7,5},{8,10},{9,11},{10,... | collective-permute-start | bytes 1179656 | tf_op jit(solution)/shard_map/ppermute | solution.py:411
  65.0 17.3 %collective-permute-start.22 = (bf16[4,96,864]{2,1,0:T(8,128)(2,1)S(1)}, bf16[4,96,864]{2,1,0:T(8,128)(2,1)S(1)}, u32[]{:S(2)}, u32[]{:S(2)}) collective-permute-start(bf16[4,96,864]{2,1,0:T(8,128)(2,1)S(1)} %get-tuple-element.148), channel_id=1, source_target_pairs={{0,4},{4,0},{8,12},{12,8},{16,20},{20,16},{24,28},{28,24},{1,5},{5... | collective-permute-start | bytes 1990664 | tf_op jit(solution)/shard_map/ppermute | solution.py:411
  73.1 14.6 %collective-permute-start.28 = (bf16[256,768]{1,0:T(8,128)(2,1)S(1)}, bf16[256,768]{1,0:T(8,128)(2,1)S(1)}, u32[]{:S(2)}, u32[]{:S(2)}) collective-permute-start(bf16[256,768]{1,0:T(8,128)(2,1)S(1)} %get-tuple-element.160), channel_id=1, source_target_pairs={{0,1},{1,0},{2,3},{3,2},{4,5},{5,4},{6,7},{7,6},{8,9},{9,8},{10,11... | collective-permute-start | bytes 1179656 | tf_op jit(solution)/shard_map/ppermute | solution.py:411
  86.2 15.3 %collective-permute-start.23 = (bf16[4,96,768]{2,1,0:T(8,128)(2,1)S(1)}, bf16[4,96,768]{2,1,0:T(8,128)(2,1)S(1)}, u32[]{:S(2)}, u32[]{:S(2)}) collective-permute-start(bf16[4,96,768]{2,1,0:T(8,128)(2,1)S(1)} %get-tuple-element.154), channel_id=1, source_target_pairs={{0,4},{4,0},{8,12},{12,8},{16,20},{20,16},{24,28},{28,24},{1,5},{5... | collective-permute-start | bytes 1769480 | tf_op jit(solution)/shard_map/ppermute | solution.py:411
  87.8 20.8 %collective-permute-start.33 = (bf16[256,768]{1,0:T(8,128)(2,1)S(1)}, bf16[256,768]{1,0:T(8,128)(2,1)S(1)}, u32[]{:S(2)}, u32[]{:S(2)}) collective-permute-start(bf16[256,768]{1,0:T(8,128)(2,1)S(1)} %pad_maximum_fusion.2), channel_id=1, source_target_pairs={{0,2},{1,3},{2,0},{3,1},{4,6},{5,7},{6,4},{7,5},{8,10},{9,11},{10,... | collective-permute-start | bytes 1179656 | tf_op jit(solution)/shard_map/ppermute | solution.py:411
  88.7 8.5 %collective-permute-start.24 = (bf16[96,864]{1,0:T(8,128)(2,1)S(1)}, bf16[96,864]{1,0:T(8,128)(2,1)S(1)}, u32[]{:S(2)}, u32[]{:S(2)}) collective-permute-start(bf16[96,864]{1,0:T(8,128)(2,1)S(1)} %get-tuple-element.157), channel_id=1, source_target_pairs={{0,8},{4,12},{8,0},{12,4},{16,24},{20,28},{24,16},{28,20},{1,9},{5... | collective-permute-start | bytes 497672 | tf_op jit(solution)/shard_map/ppermute | solution.py:411
  89.8 16.6 %collective-permute-start.34 = (bf16[96,864]{1,0:T(8,128)(2,1)S(1)}, bf16[96,864]{1,0:T(8,128)(2,1)S(1)}, u32[]{:S(2)}, u32[]{:S(2)}) collective-permute-start(bf16[96,864]{1,0:T(8,128)(2,1)S(1)} %get-tuple-element.177), channel_id=1, source_target_pairs={{0,16},{4,20},{8,24},{12,28},{16,0},{20,4},{24,8},{28,12},{1,17},{... | collective-permute-start | bytes 497672 | tf_op jit(solution)/shard_map/ppermute | solution.py:411
  93.2 8.3 %collective-permute-start.29 = (f32[2,768]{1,0:T(2,128)S(1)}, f32[2,768]{1,0:T(2,128)S(1)}, u32[]{:S(2)}, u32[]{:S(2)}) collective-permute-start(f32[2,768]{1,0:T(2,128)S(1)} %add.21.gains), channel_id=1, source_target_pairs={{0,4},{4,0},{8,12},{12,8},{16,20},{20,16},{24,28},{28,24},{1,5},{5... | collective-permute-start | bytes 18440 | tf_op jit(solution)/shard_map/ppermute | solution.py:411
  97.2 10.5 %collective-permute-start.35 = (bf16[96,864]{1,0:T(8,128)(2,1)S(1)}, bf16[96,864]{1,0:T(8,128)(2,1)S(1)}, u32[]{:S(2)}, u32[]{:S(2)}) collective-permute-start(bf16[96,864]{1,0:T(8,128)(2,1)S(1)} %get-tuple-element.178), channel_id=1, source_target_pairs={{0,24},{4,28},{8,16},{12,20},{16,8},{20,12},{24,0},{28,4},{1,25},{... | collective-permute-start | bytes 497672 | tf_op jit(solution)/shard_map/ppermute | solution.py:411
  101.7 8.2 %collective-permute-start.30 = (bf16[104,768]{1,0:T(8,128)(2,1)S(1)}, bf16[104,768]{1,0:T(8,128)(2,1)S(1)}, u32[]{:S(2)}, u32[]{:S(2)}) collective-permute-start(bf16[104,768]{1,0:T(8,128)(2,1)S(1)} %get-tuple-element.165), channel_id=1, source_target_pairs={{0,8},{4,12},{8,0},{12,4},{16,24},{20,28},{24,16},{28,20},{1,9},{5... | collective-permute-start | bytes 479240 | tf_op jit(solution)/shard_map/ppermute | solution.py:411
  103.0 15.1 %collective-permute-start.31 = (bf16[104,768]{1,0:T(8,128)(2,1)S(1)}, bf16[104,768]{1,0:T(8,128)(2,1)S(1)}, u32[]{:S(2)}, u32[]{:S(2)}) collective-permute-start(bf16[104,768]{1,0:T(8,128)(2,1)S(1)} %get-tuple-element.166), channel_id=1, source_target_pairs={{0,16},{4,20},{8,24},{12,28},{16,0},{20,4},{24,8},{28,12},{1,17},{... | collective-permute-start | bytes 479240 | tf_op jit(solution)/shard_map/ppermute | solution.py:411
  106.4 11.7 %collective-permute-start.32 = (bf16[104,768]{1,0:T(8,128)(2,1)S(1)}, bf16[104,768]{1,0:T(8,128)(2,1)S(1)}, u32[]{:S(2)}, u32[]{:S(2)}) collective-permute-start(bf16[104,768]{1,0:T(8,128)(2,1)S(1)} %get-tuple-element.167), channel_id=1, source_target_pairs={{0,24},{4,28},{8,16},{12,20},{16,8},{20,12},{24,0},{28,4},{1,25},{... | collective-permute-start | bytes 479240 | tf_op jit(solution)/shard_map/ppermute | solution.py:411
  (23 other events, 74.5 us)

commit v6 on v5

--- a/solution.py
+++ b/solution.py
@@ -122,13 +122,14 @@
 def attend_kernel(offsets, n_pieces, rows, ids, n1, cosine, sine, *rest):
     pieces = rest[:n_pieces]
     q_out, k_out, v_out, probs_out, att_out, whole, out_w, send, keep = rest[n_pieces : n_pieces + 9]
-    k_pad, v_pad = rest[n_pieces + 9 :]
+    k_pad, v_pad, raw_all = rest[n_pieces + 9 :]
     put_pieces(ids, offsets, pieces, whole, out_w, rows)
     half = WINDOW // 2
     width = q_out.shape[1]
     heads = width // HEAD_DIM
     total_rows = q_out.shape[0]
     blocks = total_rows // WINDOW
+    raw_all[...] = dot(n1[...], whole[...])
     count = [ids[5 + b] for b in range(blocks)]
     first = [ids[5 + blocks + b] for b in range(blocks)]
     for pad in (k_pad, v_pad):
@@ -136,7 +137,7 @@
         pad[half + total_rows :, :] = jnp.zeros((half, width), BF)
     for b in range(blocks):
         rows_b = slice(b * WINDOW, (b + 1) * WINDOW)
-        raw = dot(n1[rows_b, :], whole[...])
+        raw = raw_all[rows_b, :]
         c = jnp.concatenate([cosine[rows_b, :]] * 3, axis=1)
         s = jnp.concatenate([sine[rows_b, :]] * 3, axis=1)
         qk = raw[:, : 2 * width]
@@ -201,29 +202,34 @@
         n2_out[at, :] = (unit * gain[...].astype(F32)).astype(BF)
 
 
-def units_kernel(offsets, n_pieces, rows, ids, n2, n2_far, c0, c1, c2, c3, *rest):
-    send, keep, both_out, act_out, down_w, in_w = rest[n_pieces:]
+def units_rows(rows_n, rows_g, in_w, down_w, both_out, act_out, gate, up, g_act):
+    units = act_out.shape[1]
+    gate[...] = dot(rows_n[...], in_w[:, :units])
+    up[...] = dot(rows_n[...], in_w[:, units:])
+    g_act[...] = dot(jnp.concatenate([block[...] for block in rows_g], axis=0), down_w[...])
+    step = 64
+    for start in range(0, act_out.shape[0], step):
+        at = slice(start, start + step)
+        gate_c, up_c, g_c = gate[at, :], up[at, :], g_act[at, :]
+        phi = 0.5 * (1.0 + lax.erf(gate_c * np.float32(np.sqrt(0.5))))
+        gelu = gate_c * phi
+        slope = phi + gate_c * (
+            jnp.exp(-0.5 * gate_c * gate_c) * np.float32(1.0 / np.sqrt(2.0 * np.pi))
+        )
+        act_out[at, :] = (gelu * up_c).astype(BF)
+        both_out[at, :] = jnp.concatenate([g_c * up_c * slope, g_c * gelu], axis=1).astype(BF)
+    return dot(both_out[...], in_w[...], NT)
+
+
+def units_far_kernel(offsets, n_pieces, rows, ids, n2_far, c2, c3, *rest):
+    send, both_out, act_out, in_w, down_w, *temps = rest[n_pieces:]
     put_pieces(ids, offsets, rest[:n_pieces], in_w, down_w, rows)
-    units = act_out.shape[1]
-    gate_w, up_w = in_w[:, :units], in_w[:, units:]
-    for i in (2, 3, 0, 1):
-        at = slice((i % 2) * WINDOW, (i % 2 + 1) * WINDOW)
-        rows_n = (n2 if i < 2 else n2_far)[at, :]
-        rows_g = (c0, c1, c2, c3)[i][...]
-        gate = dot(rows_n, gate_w)
-        up = dot(rows_n, up_w)
-        g_act = dot(rows_g, down_w[...])
-        phi = 0.5 * (1.0 + lax.erf(gate * np.float32(np.sqrt(0.5))))
-        gelu = gate * phi
-        slope = phi + gate * (jnp.exp(-0.5 * gate * gate) * np.float32(1.0 / np.sqrt(2.0 * np.pi)))
-        act_out[i * WINDOW : (i + 1) * WINDOW, :] = (gelu * up).astype(BF)
-        g_both = jnp.concatenate([g_act * up * slope, g_act * gelu], axis=1).astype(BF)
-        both_out[i * WINDOW : (i + 1) * WINDOW, :] = g_both
-        part = dot(g_both, in_w[...], NT)
-        if i < 2:
-            keep[at, :] = part
-        else:
-            send[at, :] = part.astype(BF)
+    part = units_rows(n2_far, (c2, c3), in_w, down_w, both_out, act_out, *temps)
+    send[...] = part.astype(BF)
+
+
+def units_near_kernel(n2, c0, c1, in_w, down_w, keep, both_out, act_out, *temps):
+    keep[...] = units_rows(n2, (c0, c1), in_w, down_w, both_out, act_out, *temps)
 
 
 def emit_slots(ids, slots, rows, total, send, keep):
@@ -235,22 +241,21 @@
 
 
 def unit_grads_kernel(
-    slots, rows, ids, n2, n2_far, c0, c1, c2, c3, both, act, down_w, send, keep, b_send, b_keep, total
+    slots, rows, ids, n2, n2_far, c0, c1, c2, c3, both, both_far, act, act_far, down_w,
+    send, keep, b_send, b_keep, total,
 ):
-    pair = 2 * WINDOW
     units2 = both.shape[1]
-    in_part = dot(n2[...], both[:pair, :], TN) + dot(n2_far[...], both[pair:, :], TN)
-    total[:, :units2] = in_part
-    gz = jnp.concatenate([c0[...], c1[...], c2[...], c3[...]], axis=0)
-    down_part = dot(gz, act[...], TN)
-    total[:, units2:] = down_part
+    total[:, :units2] = dot(n2[...], both[...], TN) + dot(n2_far[...], both_far[...], TN)
+    gz = jnp.concatenate([c0[...], c1[...]], axis=0)
+    gz_far = jnp.concatenate([c2[...], c3[...]], axis=0)
+    total[:, units2:] = dot(gz, act[...], TN) + dot(gz_far, act_far[...], TN)
     if slots:
         emit_slots(ids, slots, rows, total, send, keep)
     else:
         send[...] = total[...]
         keep[...] = jnp.zeros(keep.shape, BF)
-    b_keep[...] = dot(act[:pair, :], down_w[...], NT)
-    b_send[...] = dot(act[pair:, :], down_w[...], NT).astype(BF)
+    b_keep[...] = dot(act[...], down_w[...], NT)
+    b_send[...] = dot(act_far[...], down_w[...], NT).astype(BF)
 
 
 def residual_kernel(own, received, h, c0, c1, gain, gh_out, gy_out, gain_out):
@@ -270,17 +275,17 @@
 def attend_back_kernel(
     ids, gy, gy_far, out_w, q_in, k_in, v_in, probs_in, cosine, sine, n1, qkv_w, gain, gain_two,
     g_raw, g_send, g_keep, gains,
-    g_att_all, k_pad, v_pad, gk_pad, gv_pad, gq_all,
+    g_att_all, k_pad, v_pad, gk_pad, gv_pad, gq_all, g_all,
 ):
     half = WINDOW // 2
     total_rows, width = q_in.shape
     heads = width // HEAD_DIM
     blocks = total_rows // WINDOW
     span = 2 * WINDOW
-    for i in range(4):
-        source = gy if i < 2 else gy_far
-        part = dot(source[(i % 2) * WINDOW : (i % 2 + 1) * WINDOW, :], out_w[...])
-        g_att_all[rows_of(ids[i]), :] = part.astype(BF)
+    for i in (0, 2):
+        part = dot((gy_far if i else gy)[...], out_w[...]).astype(BF)
+        g_att_all[rows_of(ids[i]), :] = part[:WINDOW, :]
+        g_att_all[rows_of(ids[i + 1]), :] = part[WINDOW:, :]
     for pad, source in ((k_pad, k_in), (v_pad, v_in)):
         pad[0:half, :] = jnp.zeros((half, width), BF)
         pad[half + total_rows :, :] = jnp.zeros((half, width), BF)
@@ -321,10 +326,12 @@
         turned = qk * c - swap_halves(qk) * s
         g_raw[rows_b, : 2 * width] = turned.astype(BF)
         g_raw[rows_b, 2 * width :] = gv_pad[inner, :].astype(BF)
+    ordered = jnp.concatenate([g_raw[rows_of(ids[i]), :] for i in range(4)], axis=0)
+    g_all[...] = dot(ordered, qkv_w[...], NT)
     gain_sum = jnp.zeros(gain_two.shape, F32)
-    for i in (2, 3, 0, 1):
+    for i in range(4):
         at = slice((i % 2) * WINDOW, (i % 2 + 1) * WINDOW)
-        g_n1 = dot(g_raw[rows_of(ids[i]), :], qkv_w[...], NT)
+        g_n1 = g_all[i * WINDOW : (i + 1) * WINDOW, :]
         gain_sum += jnp.sum(g_n1 * n1[rows_of(ids[i]), :].astype(F32), axis=0, keepdims=True)
         if i < 2:
             g_keep[at, :] = g_n1
@@ -564,7 +571,8 @@
         ),
         (n1, cosine, sine) + qkv_pieces,
         (ids,),
-        [pltpu.VMEM((total_rows + WINDOW, head_width), BF)] * 2,
+        [pltpu.VMEM((total_rows + WINDOW, head_width), BF)] * 2
+        + [pltpu.VMEM((total_rows, 3 * head_width), F32)],
         flops=2 * total_rows * width * 3 * head_width,
     )
     a_send, unit_near, cot_across = pin((a_send, unit_near, cot_across))
@@ -579,18 +587,19 @@
         (a_sum, a_got, token_blocks[0], token_blocks[1], gain_two),
     )
     n2_far = core(n2)
-    u_send, u_keep, both, act, down_w = call(
-        functools.partial(units_kernel, offsets, len(unit_pieces), shard),
-        (
-            pair_bf,
-            pair_f32,
-            shape(total_rows, 2 * units),
-            shape(total_rows, units),
-            shape(width, units),
-        ),
-        (n2, n2_far) + cot_blocks + unit_pieces,
+    halves = (shape(pair_rows, 2 * units), shape(pair_rows, units))
+    u_send, both_far, act_far, in_w, down_w = call(
+        functools.partial(units_far_kernel, offsets, len(unit_pieces), shard),
+        (pair_bf,) + halves + (shape(width, 2 * units), shape(width, units)),
+        (n2_far,) + cot_blocks[2:] + unit_pieces,
         (ids,),
-        [pltpu.VMEM((width, 2 * units), BF)],
+        [pltpu.VMEM((pair_rows, units), F32)] * 3,
+    )
+    u_keep, both, act = call(
+        units_near_kernel,
+        (pair_f32,) + halves,
+        (n2,) + cot_blocks[:2] + (in_w, down_w),
+        scratch=[pltpu.VMEM((pair_rows, units), F32)] * 3,
     )
     u_sum = (u_keep + core(u_send).astype(F32)).astype(BF)
     u_got = across(u_sum)
@@ -598,7 +607,7 @@
     in_send, in_keep, b_send, b_keep = call(
         functools.partial(unit_grads_kernel, slots, shard),
         s_shapes + (pair_bf, pair_f32),
-        (n2, n2_far) + cot_blocks + (both, act, down_w),
+        (n2, n2_far) + cot_blocks + (both, both_far, act, act_far, down_w),
         (ids,),
         [pltpu.VMEM((width, 3 * units), F32)],
         flops=2 * total_rows * width * 4 * units,
@@ -629,6 +638,7 @@
             pltpu.VMEM((total_rows + WINDOW, head_width), F32),
             pltpu.VMEM((total_rows + WINDOW, head_width), F32),
             pltpu.VMEM((total_rows, head_width), F32),
+            pltpu.VMEM((total_rows, width), F32),
         ],
     )
     if slots:

time: 120 us -> 118 us (0.983)
  waiting for transfers between devices: 50.8 us -> 46 us
  starting transfers between devices: 37.9 us -> 41.5 us
    ppermute x36, waiting for transfers between devices: 50.8 us -> 46 us  [swap(): return lax.ppermute(values, axis, [(i, i ^ bit) for i in range(size)])]
    ppermute x36, starting transfers between devices: 37.9 us -> 41.5 us  [swap(): return lax.ppermute(values, axis, [(i, i ^ bit) for i in range(size)])]
    pallas_call x15 -> x16, Pallas kernels: 25.1 us -> 24.4 us  [call(): pl.pallas_call(kernel, name=getattr(kernel, 'func', kernel).__name__, out...]
  transfers between devices with their start and end apart: 36 -> 36, of which waited for: 18 -> 17; matrix products, arithmetic and copies ran while one was open for 0% -> 0% of each run, Pallas kernels for 17% -> 18%
where the time goes in v6:
time: 118 us; the launch traced here: 117 us
  waiting for transfers between devices  46 us (39%)
  starting transfers between devices  41.5 us (35%)
  Pallas kernels  24.4 us (21%)
  local copies, waits for them, and re-layouts  3.97 us (3%)
    ppermute x36, waiting for transfers between devices, swap(): return lax.ppermute(values, axis, [(i, i ^ bit) for i in range(size)])  46 us
    ppermute x36, starting transfers between devices, swap(): return lax.ppermute(values, axis, [(i, i ^ bit) for i in range(size)])  41.5 us
    pallas_call x16, Pallas kernels, call(): pl.pallas_call(kernel, name=getattr(kernel, 'func', kernel).__name__, out...  24.4 us
    unnamed x23, local copies, waits for them, and re-layouts  3.8 us
  transfers between devices with their start and end apart: 36, of which 17 were waited for; matrix products, arithmetic and copies ran while one was open for 0% of the time, Pallas kernels for 18%

profile of v6, /device:TPU:0, one launch (start us, length us, event | category | flops | bytes accessed | tf_op | source)
XLA Modules:
  0.0 117.2 jit_solution(3484710596878561883)
XLA Ops:
  2.8 4.1 %collective-permute-start.1 = (bf16[96,768]{1,0:T(8,128)(2,1)S(1)}, bf16[96,768]{1,0:T(8,128)(2,1)S(1)}, u32[]{:S(2)}, u32[]{:S(2)}) collective-permute-start(bf16[96,768]{1,0:T(8,128)(2,1)S(1)} %pack_kernel.2.rest_0_), channel_id=1, source_target_pairs={{0,16},{4,20},{8,24},{12,28},{16,0},{20,4},{24,8},{28,12},{1,17},{... | collective-permute-start | bytes 442376 | tf_op jit(solution)/shard_map/ppermute | solution.py:418
  17.7 2.5 %collective-permute-done.2.rest_3_ = bf16[96,768]{1,0:T(8,128)(2,1)S(1)} collective-permute-done((bf16[96,768]{1,0:T(8,128)(2,1)S(1)}, bf16[96,768]{1,0:T(8,128)(2,1)S(1)}, u32[]{:S(2)}, u32[]{:S(2)}) %collective-permute-start.2) | collective-permute-done | bytes 147488 | tf_op jit(solution)/shard_map/ppermute | solution.py:418
  21.6 2.6 %collective-permute-start.10 = (bf16[96,864]{1,0:T(8,128)(2,1)S(1)}, bf16[96,864]{1,0:T(8,128)(2,1)S(1)}, u32[]{:S(2)}, u32[]{:S(2)}) collective-permute-start(bf16[96,864]{1,0:T(8,128)(2,1)S(1)} %pack_kernel.3.rest_0_), channel_id=1, source_target_pairs={{0,16},{4,20},{8,24},{12,28},{16,0},{20,4},{24,8},{28,12},{1,17},{... | collective-permute-start | bytes 497672 | tf_op jit(solution)/shard_map/ppermute | solution.py:418
  24.2 1.7 %collective-permute-start.9 = (bf16[96,864]{1,0:T(8,128)(2,1)S(1)}, bf16[96,864]{1,0:T(8,128)(2,1)S(1)}, u32[]{:S(2)}, u32[]{:S(2)}) collective-permute-start(bf16[96,864]{1,0:T(8,128)(2,1)S(1)} %pack_kernel.3.rest_0_), channel_id=1, source_target_pairs={{0,8},{4,12},{8,0},{12,4},{16,24},{20,28},{24,16},{28,20},{1,9},{5... | collective-permute-start | bytes 497672 | tf_op jit(solution)/shard_map/ppermute | solution.py:418
  27.5 2.0 %prepare_kernel.1 = (bf16[512,768]{1,0:T(8,128)(2,1)S(1)}, f32[512,128]{1,0:T(8,128)S(1)}, f32[512,128]{1,0:T(8,128)S(1)}) custom-call(s32[13]{0:T(128)S(1)} %concatenate.6.ids, bf16[128,768]{1,0:T(8,128)(2,1)S(1)} %copy-done, bf16[128,768]{1,0:T(8,128)(2,1)S(1)} %collective-permute-done.5.t1, bf16[128,768]{1,0:T(8,128)(2,1)S(1)} %collective-permute-done.7.t2, ...), custom_call_target="tpu_custom_call" | custom-call | flops 1 | bytes 1 | tf_op jit(solution)/shard_map/prepare_kernel/pallas_call | solution.py:30
  29.5 3.0 %collective-permute-done.10.rest_2_ = bf16[96,864]{1,0:T(8,128)(2,1)S(1)} collective-permute-done((bf16[96,864]{1,0:T(8,128)(2,1)S(1)}, bf16[96,864]{1,0:T(8,128)(2,1)S(1)}, u32[]{:S(2)}, u32[]{:S(2)}) %collective-permute-start.10) | collective-permute-done | bytes 165920 | tf_op jit(solution)/shard_map/ppermute | solution.py:418
  33.2 4.3 %attend_kernel.1 = (bf16[512,192]{1,0:T(8,128)(2,1)S(1)}, bf16[512,192]{1,0:T(8,128)(2,1)S(1)}, bf16[512,192]{1,0:T(8,128)(2,1)S(1)}, bf16[3,512,256]{2,1,0:T(8,...) custom-call(s32[13]{0:T(128)S(1)} %concatenate.6.ids, ...), custom_call_target="tpu_custom_call" | custom-call | flops 1 | bytes 1 | tf_op jit(solution)/shard_map/attend_kernel/pallas_call | solution.py:30
  38.0 1.7 %collective-permute-done.13 = bf16[256,768]{1,0:T(8,128)(2,1)S(1)} collective-permute-done((bf16[256,768]{1,0:T(8,128)(2,1)S(1)}, bf16[256,768]{1,0:T(8,128)(2,1)S(1)}, u32[]{:S(2)}, u32[]{:S(2)}) %collective-permute-start.13) | collective-permute-done | bytes 393248 | tf_op jit(solution)/shard_map/ppermute | solution.py:418
  39.8 1.8 %collective-permute-start.14 = (bf16[256,768]{1,0:T(8,128)(2,1)S(1)}, bf16[256,768]{1,0:T(8,128)(2,1)S(1)}, u32[]{:S(2)}, u32[]{:S(2)}) collective-permute-start(bf16[256,768]{1,0:T(8,128)(2,1)S(1)} %add_convert_fusion.1.own), channel_id=1, source_target_pairs={{0,2},{1,3},{2,0},{3,1},{4,6},{5,7},{6,4},{7,5},{8,10},{9,11},{10,... | collective-permute-start | bytes 1179656 | tf_op jit(solution)/shard_map/ppermute | solution.py:418
  42.0 9.0 %collective-permute-done.14.received = bf16[256,768]{1,0:T(8,128)(2,1)S(1)} collective-permute-done((bf16[256,768]{1,0:T(8,128)(2,1)S(1)}, bf16[256,768]{1,0:T(8,128)(2,1)S(1)}, u32[]{:S(2)}, u32[]{:S(2)}) %collective-permute-start.14) | collective-permute-done | bytes 393248 | tf_op jit(solution)/shard_map/ppermute | solution.py:418
  52.0 3.2 %collective-permute-done.18 = bf16[3,96,864]{2,1,0:T(8,128)(2,1)S(1)} collective-permute-done((bf16[3,96,864]{2,1,0:T(8,128)(2,1)S(1)}, bf16[3,96,864]{2,1,0:T(8,128)(2,1)S(1)}, u32[]{:S(2)}, u32[]{:S(2)}) %collective-permute-start.18) | collective-permute-done | bytes 497696 | tf_op jit(solution)/shard_map/ppermute | solution.py:418
  55.3 2.0 %units_far_kernel.1 = (bf16[256,768]{1,0:T(8,128)(2,1)S(1)}, bf16[256,576]{1,0:T(8,128)(2,1)S(1)}, bf16[256,288]{1,0:T(8,128)(2,1)S(1)}, bf16[768,576]{1,0:T(8,128)(2,1)S(1)}, bf16[768,288]{1,0:T(8,128)(2,1)S(1)}) custom-call(s32[13]{0:T(128)S(1)} %concatenate.6.ids, bf16[256,768]{1,0:T(8,128)(2,1)S(1)} %collective-permute-done.15.n2_far, ...), custom_call_target="tpu_custom_call" | custom-call | flops 1 | bytes 1 | tf_op jit(solution)/shard_map/units_far_kernel/pallas_call | solution.py:30
  59.6 2.3 %unit_grads_kernel.1 = (bf16[4,96,864]{2,1,0:T(8,128)(2,1)S(1)}, bf16[4,96,864]{2,1,0:T(8,128)(2,1)S(1)}, bf16[256,768]{1,0:T(8,128)(2,1)S(1)}, f32[256,768]{1,0:T(8,128)S(1)}) custom-call(s32[13]{0:T(128)S(1)} %concatenate.6.ids, bf16[256,768]{1,0:T(8,128)(2,1)S(1)} %get-tuple-element.126.n2, bf16[256,768]{1,0:T(8,128)(2,1)S(1)} %collective-permute-done.15.n2_far, ...), custom_call_target="tpu_custom_call" | custom-call | flops 1 | bytes 1 | tf_op jit(solution)/shard_map/unit_grads_kernel/pallas_call | solution.py:30
  61.9 1.8 %collective-permute-start.22 = (bf16[4,96,864]{2,1,0:T(8,128)(2,1)S(1)}, bf16[4,96,864]{2,1,0:T(8,128)(2,1)S(1)}, u32[]{:S(2)}, u32[]{:S(2)}) collective-permute-start(bf16[4,96,864]{2,1,0:T(8,128)(2,1)S(1)} %get-tuple-element.154), channel_id=1, source_target_pairs={{0,4},{4,0},{8,12},{12,8},{16,20},{20,16},{24,28},{28,24},{1,5},{5... | collective-permute-start | bytes 1990664 | tf_op jit(solution)/shard_map/ppermute | solution.py:418
  63.7 6.9 %collective-permute-done.20.received = bf16[256,768]{1,0:T(8,128)(2,1)S(1)} collective-permute-done((bf16[256,768]{1,0:T(8,128)(2,1)S(1)}, bf16[256,768]{1,0:T(8,128)(2,1)S(1)}, u32[]{:S(2)}, u32[]{:S(2)}) %collective-permute-start.20) | collective-permute-done | bytes 393248 | tf_op jit(solution)/shard_map/ppermute | solution.py:418
  73.0 5.4 %attend_back_kernel.1 = (bf16[512,576]{1,0:T(8,128)(2,1)S(1)}, bf16[256,768]{1,0:T(8,128)(2,1)S(1)}, f32[256,768]{1,0:T(8,128)S(1)}, f32[2,768]{1,0:T(2,128)S(1)}) custom-call(s32[13]{0:T(128)S(1)} %concatenate.6.ids, bf16[256,768]{1,0:T(8,128)(2,1)S(1)} %get-tuple-element.143.gy, bf16[256,768]{1,0:T(8,128)(2,1)S(1)} %collective-permute-done.21.gy_far, ...), custom_call_target="tpu_custom_call" | custom-call | flops 1 | bytes 1 | tf_op jit(solution)/shard_map/attend_back_kernel/pallas_call | solution.py:30
  82.7 1.7 %attend_grads_kernel.1 = (bf16[4,96,768]{2,1,0:T(8,128)(2,1)S(1)}, bf16[4,96,768]{2,1,0:T(8,128)(2,1)S(1)}) custom-call(s32[13]{0:T(128)S(1)} %concatenate.6.ids, bf16[512,768]{1,0:T(8,128)(2,1)S(1)} %get-tuple-element.112.n1, bf16[512,576]{1,0:T(8,128)(2,1)S(1)} %get-tuple-element.156.g_raw, bf16[256,768]{1,0:T(8,128)(2,1)S(1)} %get-tuple-element.143.gy, ...), custom_call_target="tpu_custom_call" | custom-call | flops 1 | bytes 1 | tf_op jit(solution)/shard_map/attend_grads_kernel/pallas_call | solution.py:30
  85.0 1.8 %collective-permute-start.33 = (bf16[256,768]{1,0:T(8,128)(2,1)S(1)}, bf16[256,768]{1,0:T(8,128)(2,1)S(1)}, u32[]{:S(2)}, u32[]{:S(2)}) collective-permute-start(bf16[256,768]{1,0:T(8,128)(2,1)S(1)} %pad_maximum_fusion.2), channel_id=1, source_target_pairs={{0,2},{1,3},{2,0},{3,1},{4,6},{5,7},{6,4},{7,5},{8,10},{9,11},{10,... | collective-permute-start | bytes 1179656 | tf_op jit(solution)/shard_map/ppermute | solution.py:418
  88.1 3.4 %collective-permute-start.34 = (bf16[96,864]{1,0:T(8,128)(2,1)S(1)}, bf16[96,864]{1,0:T(8,128)(2,1)S(1)}, u32[]{:S(2)}, u32[]{:S(2)}) collective-permute-start(bf16[96,864]{1,0:T(8,128)(2,1)S(1)} %get-tuple-element.183), channel_id=1, source_target_pairs={{0,16},{4,20},{8,24},{12,28},{16,0},{20,4},{24,8},{28,12},{1,17},{... | collective-permute-start | bytes 497672 | tf_op jit(solution)/shard_map/ppermute | solution.py:418
  92.2 3.3 %collective-permute-done.24.rest_0_ = bf16[96,864]{1,0:T(8,128)(2,1)S(1)} collective-permute-done((bf16[96,864]{1,0:T(8,128)(2,1)S(1)}, bf16[96,864]{1,0:T(8,128)(2,1)S(1)}, u32[]{:S(2)}, u32[]{:S(2)}) %collective-permute-start.24) | collective-permute-done | bytes 165920 | tf_op jit(solution)/shard_map/ppermute | solution.py:418
  95.5 2.5 %collective-permute-start.35 = (bf16[96,864]{1,0:T(8,128)(2,1)S(1)}, bf16[96,864]{1,0:T(8,128)(2,1)S(1)}, u32[]{:S(2)}, u32[]{:S(2)}) collective-permute-start(bf16[96,864]{1,0:T(8,128)(2,1)S(1)} %get-tuple-element.184), channel_id=1, source_target_pairs={{0,24},{4,28},{8,16},{12,20},{16,8},{20,12},{24,0},{28,4},{1,25},{... | collective-permute-start | bytes 497672 | tf_op jit(solution)/shard_map/ppermute | solution.py:418
  98.0 1.8 %collective-permute-done.29.gains_got = f32[2,768]{1,0:T(2,128)S(1)} collective-permute-done((f32[2,768]{1,0:T(2,128)S(1)}, f32[2,768]{1,0:T(2,128)S(1)}, u32[]{:S(2)}, u32[]{:S(2)}) %collective-permute-start.29) | collective-permute-done | bytes 6176 | tf_op jit(solution)/shard_map/ppermute | solution.py:418
  101.2 3.4 %collective-permute-start.31 = (bf16[104,768]{1,0:T(8,128)(2,1)S(1)}, bf16[104,768]{1,0:T(8,128)(2,1)S(1)}, u32[]{:S(2)}, u32[]{:S(2)}) collective-permute-start(bf16[104,768]{1,0:T(8,128)(2,1)S(1)} %get-tuple-element.172), channel_id=1, source_target_pairs={{0,16},{4,20},{8,24},{12,28},{16,0},{20,4},{24,8},{28,12},{1,17},{... | collective-permute-start | bytes 479240 | tf_op jit(solution)/shard_map/ppermute | solution.py:418
  108.1 8.3 %collective-permute-done.31.rest_1_ = bf16[104,768]{1,0:T(8,128)(2,1)S(1)} collective-permute-done((bf16[104,768]{1,0:T(8,128)(2,1)S(1)}, bf16[104,768]{1,0:T(8,128)(2,1)S(1)}, u32[]{:S(2)}, u32[]{:S(2)}) %collective-permute-start.31) | collective-permute-done | bytes 159776 | tf_op jit(solution)/shard_map/ppermute | solution.py:418
  (100 shorter events, 35.8 us)
Async XLA Ops:
  2.8 11.2 %collective-permute-start.1 = (bf16[96,768]{1,0:T(8,128)(2,1)S(1)}, bf16[96,768]{1,0:T(8,128)(2,1)S(1)}, u32[]{:S(2)}, u32[]{:S(2)}) collective-permute-start(bf16[96,768]{1,0:T(8,128)(2,1)S(1)} %pack_kernel.2.rest_0_), channel_id=1, source_target_pairs={{0,16},{4,20},{8,24},{12,28},{16,0},{20,4},{24,8},{28,12},{1,17},{... | collective-permute-start | bytes 442376 | tf_op jit(solution)/shard_map/ppermute | solution.py:418
  6.9 10.8 %collective-permute-start.5 = (bf16[128,768]{1,0:T(8,128)(2,1)S(1)}, bf16[128,768]{1,0:T(8,128)(2,1)S(1)}, u32[]{:S(2)}, u32[]{:S(2)}) collective-permute-start(bf16[128,768]{1,0:T(8,128)(2,1)S(1)} %copy-done), channel_id=1, source_target_pairs={{0,2},{1,3},{2,0},{3,1},{4,6},{5,7},{6,4},{7,5},{8,10},{9,11},{10,... | collective-permute-start | bytes 589832 | tf_op jit(solution)/shard_map/ppermute | solution.py:418
  8.9 8.8 %collective-permute-start.4 = (bf16[96,864]{1,0:T(8,128)(2,1)S(1)}, bf16[96,864]{1,0:T(8,128)(2,1)S(1)}, u32[]{:S(2)}, u32[]{:S(2)}) collective-permute-start(bf16[96,864]{1,0:T(8,128)(2,1)S(1)} %pack_kernel.3.rest_0_), channel_id=1, source_target_pairs={{0,4},{4,0},{8,12},{12,8},{16,20},{20,16},{24,28},{28,24},{1,5},{5... | collective-permute-start | bytes 497672 | tf_op jit(solution)/shard_map/ppermute | solution.py:418
  10.5 6.7 %collective-permute-start = (bf16[96,768]{1,0:T(8,128)(2,1)S(1)}, bf16[96,768]{1,0:T(8,128)(2,1)S(1)}, u32[]{:S(2)}, u32[]{:S(2)}) collective-permute-start(bf16[96,768]{1,0:T(8,128)(2,1)S(1)} %pack_kernel.2.rest_0_), channel_id=1, source_target_pairs={{0,8},{4,12},{8,0},{12,4},{16,24},{20,28},{24,16},{28,20},{1,9},{5... | collective-permute-start | bytes 442376 | tf_op jit(solution)/shard_map/ppermute | solution.py:418
  14.0 6.2 %collective-permute-start.2 = (bf16[96,768]{1,0:T(8,128)(2,1)S(1)}, bf16[96,768]{1,0:T(8,128)(2,1)S(1)}, u32[]{:S(2)}, u32[]{:S(2)}) collective-permute-start(bf16[96,768]{1,0:T(8,128)(2,1)S(1)} %collective-permute-done.1.rest_2_), channel_id=1, source_target_pairs={{0,8},{4,12},{8,0},{12,4},{16,24},{20,28},{24,16},{28,20},{1,9},{5... | collective-permute-start | bytes 442376 | tf_op jit(solution)/shard_map/ppermute | solution.py:418
  20.3 12.9 %collective-permute-start.6 = (bf16[3,96,768]{2,1,0:T(8,128)(2,1)S(1)}, bf16[3,96,768]{2,1,0:T(8,128)(2,1)S(1)}, u32[]{:S(2)}, u32[]{:S(2)}) collective-permute-start(bf16[3,96,768]{2,1,0:T(8,128)(2,1)S(1)} %pad_maximum_fusion.1), channel_id=1, source_target_pairs={{0,4},{4,0},{8,12},{12,8},{16,20},{20,16},{24,28},{28,24},{1,5},{5... | collective-permute-start | bytes 1327112 | tf_op jit(solution)/shard_map/ppermute | solution.py:418
  21.1 6.4 %collective-permute-start.8 = (bf16[128,768]{1,0:T(8,128)(2,1)S(1)}, bf16[128,768]{1,0:T(8,128)(2,1)S(1)}, u32[]{:S(2)}, u32[]{:S(2)}) collective-permute-start(bf16[128,768]{1,0:T(8,128)(2,1)S(1)} %collective-permute-done.5.t1), channel_id=1, source_target_pairs={{0,1},{1,0},{2,3},{3,2},{4,5},{5,4},{6,7},{7,6},{8,9},{9,8},{10,11... | collective-permute-start | bytes 589832 | tf_op jit(solution)/shard_map/ppermute | solution.py:418
  21.6 11.0 %collective-permute-start.10 = (bf16[96,864]{1,0:T(8,128)(2,1)S(1)}, bf16[96,864]{1,0:T(8,128)(2,1)S(1)}, u32[]{:S(2)}, u32[]{:S(2)}) collective-permute-start(bf16[96,864]{1,0:T(8,128)(2,1)S(1)} %pack_kernel.3.rest_0_), channel_id=1, source_target_pairs={{0,16},{4,20},{8,24},{12,28},{16,0},{20,4},{24,8},{28,12},{1,17},{... | collective-permute-start | bytes 497672 | tf_op jit(solution)/shard_map/ppermute | solution.py:418
  24.2 13.3 %collective-permute-start.9 = (bf16[96,864]{1,0:T(8,128)(2,1)S(1)}, bf16[96,864]{1,0:T(8,128)(2,1)S(1)}, u32[]{:S(2)}, u32[]{:S(2)}) collective-permute-start(bf16[96,864]{1,0:T(8,128)(2,1)S(1)} %pack_kernel.3.rest_0_), channel_id=1, source_target_pairs={{0,8},{4,12},{8,0},{12,4},{16,24},{20,28},{24,16},{28,20},{1,9},{5... | collective-permute-start | bytes 497672 | tf_op jit(solution)/shard_map/ppermute | solution.py:418
  26.0 11.6 %collective-permute-start.12 = (bf16[128,768]{1,0:T(8,128)(2,1)S(1)}, bf16[128,768]{1,0:T(8,128)(2,1)S(1)}, u32[]{:S(2)}, u32[]{:S(2)}) collective-permute-start(bf16[128,768]{1,0:T(8,128)(2,1)S(1)} %copy-done.1), channel_id=1, source_target_pairs={{0,2},{1,3},{2,0},{3,1},{4,6},{5,7},{6,4},{7,5},{8,10},{9,11},{10,... | collective-permute-start | bytes 589832 | tf_op jit(solution)/shard_map/ppermute | solution.py:418
  39.8 11.2 %collective-permute-start.14 = (bf16[256,768]{1,0:T(8,128)(2,1)S(1)}, bf16[256,768]{1,0:T(8,128)(2,1)S(1)}, u32[]{:S(2)}, u32[]{:S(2)}) collective-permute-start(bf16[256,768]{1,0:T(8,128)(2,1)S(1)} %add_convert_fusion.1.own), channel_id=1, source_target_pairs={{0,2},{1,3},{2,0},{3,1},{4,6},{5,7},{6,4},{7,5},{8,10},{9,11},{10,... | collective-permute-start | bytes 1179656 | tf_op jit(solution)/shard_map/ppermute | solution.py:418
  41.7 13.6 %collective-permute-start.18 = (bf16[3,96,864]{2,1,0:T(8,128)(2,1)S(1)}, bf16[3,96,864]{2,1,0:T(8,128)(2,1)S(1)}, u32[]{:S(2)}, u32[]{:S(2)}) collective-permute-start(bf16[3,96,864]{2,1,0:T(8,128)(2,1)S(1)} %pad_maximum_fusion), channel_id=1, source_target_pairs={{0,4},{4,0},{8,12},{12,8},{16,20},{20,16},{24,28},{28,24},{1,5},{5... | collective-permute-start | bytes 1493000 | tf_op jit(solution)/shard_map/ppermute | solution.py:418
  59.3 11.3 %collective-permute-start.20 = (bf16[256,768]{1,0:T(8,128)(2,1)S(1)}, bf16[256,768]{1,0:T(8,128)(2,1)S(1)}, u32[]{:S(2)}, u32[]{:S(2)}) collective-permute-start(bf16[256,768]{1,0:T(8,128)(2,1)S(1)} %add_convert_fusion.own), channel_id=1, source_target_pairs={{0,2},{1,3},{2,0},{3,1},{4,6},{5,7},{6,4},{7,5},{8,10},{9,11},{10,... | collective-permute-start | bytes 1179656 | tf_op jit(solution)/shard_map/ppermute | solution.py:418
  61.9 17.4 %collective-permute-start.22 = (bf16[4,96,864]{2,1,0:T(8,128)(2,1)S(1)}, bf16[4,96,864]{2,1,0:T(8,128)(2,1)S(1)}, u32[]{:S(2)}, u32[]{:S(2)}) collective-permute-start(bf16[4,96,864]{2,1,0:T(8,128)(2,1)S(1)} %get-tuple-element.154), channel_id=1, source_target_pairs={{0,4},{4,0},{8,12},{12,8},{16,20},{20,16},{24,28},{28,24},{1,5},{5... | collective-permute-start | bytes 1990664 | tf_op jit(solution)/shard_map/ppermute | solution.py:418
  71.2 13.6 %collective-permute-start.28 = (bf16[256,768]{1,0:T(8,128)(2,1)S(1)}, bf16[256,768]{1,0:T(8,128)(2,1)S(1)}, u32[]{:S(2)}, u32[]{:S(2)}) collective-permute-start(bf16[256,768]{1,0:T(8,128)(2,1)S(1)} %get-tuple-element.166), channel_id=1, source_target_pairs={{0,1},{1,0},{2,3},{3,2},{4,5},{5,4},{6,7},{7,6},{8,9},{9,8},{10,11... | collective-permute-start | bytes 1179656 | tf_op jit(solution)/shard_map/ppermute | solution.py:418
  84.5 15.3 %collective-permute-start.23 = (bf16[4,96,768]{2,1,0:T(8,128)(2,1)S(1)}, bf16[4,96,768]{2,1,0:T(8,128)(2,1)S(1)}, u32[]{:S(2)}, u32[]{:S(2)}) collective-permute-start(bf16[4,96,768]{2,1,0:T(8,128)(2,1)S(1)} %get-tuple-element.160), channel_id=1, source_target_pairs={{0,4},{4,0},{8,12},{12,8},{16,20},{20,16},{24,28},{28,24},{1,5},{5... | collective-permute-start | bytes 1769480 | tf_op jit(solution)/shard_map/ppermute | solution.py:418
  85.0 21.9 %collective-permute-start.33 = (bf16[256,768]{1,0:T(8,128)(2,1)S(1)}, bf16[256,768]{1,0:T(8,128)(2,1)S(1)}, u32[]{:S(2)}, u32[]{:S(2)}) collective-permute-start(bf16[256,768]{1,0:T(8,128)(2,1)S(1)} %pad_maximum_fusion.2), channel_id=1, source_target_pairs={{0,2},{1,3},{2,0},{3,1},{4,6},{5,7},{6,4},{7,5},{8,10},{9,11},{10,... | collective-permute-start | bytes 1179656 | tf_op jit(solution)/shard_map/ppermute | solution.py:418
  87.0 8.5 %collective-permute-start.24 = (bf16[96,864]{1,0:T(8,128)(2,1)S(1)}, bf16[96,864]{1,0:T(8,128)(2,1)S(1)}, u32[]{:S(2)}, u32[]{:S(2)}) collective-permute-start(bf16[96,864]{1,0:T(8,128)(2,1)S(1)} %get-tuple-element.163), channel_id=1, source_target_pairs={{0,8},{4,12},{8,0},{12,4},{16,24},{20,28},{24,16},{28,20},{1,9},{5... | collective-permute-start | bytes 497672 | tf_op jit(solution)/shard_map/ppermute | solution.py:418
  88.1 16.5 %collective-permute-start.34 = (bf16[96,864]{1,0:T(8,128)(2,1)S(1)}, bf16[96,864]{1,0:T(8,128)(2,1)S(1)}, u32[]{:S(2)}, u32[]{:S(2)}) collective-permute-start(bf16[96,864]{1,0:T(8,128)(2,1)S(1)} %get-tuple-element.183), channel_id=1, source_target_pairs={{0,16},{4,20},{8,24},{12,28},{16,0},{20,4},{24,8},{28,12},{1,17},{... | collective-permute-start | bytes 497672 | tf_op jit(solution)/shard_map/ppermute | solution.py:418
  91.5 8.3 %collective-permute-start.29 = (f32[2,768]{1,0:T(2,128)S(1)}, f32[2,768]{1,0:T(2,128)S(1)}, u32[]{:S(2)}, u32[]{:S(2)}) collective-permute-start(f32[2,768]{1,0:T(2,128)S(1)} %add.21.gains), channel_id=1, source_target_pairs={{0,4},{4,0},{8,12},{12,8},{16,20},{20,16},{24,28},{28,24},{1,5},{5... | collective-permute-start | bytes 18440 | tf_op jit(solution)/shard_map/ppermute | solution.py:418
  95.5 10.4 %collective-permute-start.35 = (bf16[96,864]{1,0:T(8,128)(2,1)S(1)}, bf16[96,864]{1,0:T(8,128)(2,1)S(1)}, u32[]{:S(2)}, u32[]{:S(2)}) collective-permute-start(bf16[96,864]{1,0:T(8,128)(2,1)S(1)} %get-tuple-element.184), channel_id=1, source_target_pairs={{0,24},{4,28},{8,16},{12,20},{16,8},{20,12},{24,0},{28,4},{1,25},{... | collective-permute-start | bytes 497672 | tf_op jit(solution)/shard_map/ppermute | solution.py:418
  99.9 8.2 %collective-permute-start.30 = (bf16[104,768]{1,0:T(8,128)(2,1)S(1)}, bf16[104,768]{1,0:T(8,128)(2,1)S(1)}, u32[]{:S(2)}, u32[]{:S(2)}) collective-permute-start(bf16[104,768]{1,0:T(8,128)(2,1)S(1)} %get-tuple-element.171), channel_id=1, source_target_pairs={{0,8},{4,12},{8,0},{12,4},{16,24},{20,28},{24,16},{28,20},{1,9},{5... | collective-permute-start | bytes 479240 | tf_op jit(solution)/shard_map/ppermute | solution.py:418
  101.2 15.1 %collective-permute-start.31 = (bf16[104,768]{1,0:T(8,128)(2,1)S(1)}, bf16[104,768]{1,0:T(8,128)(2,1)S(1)}, u32[]{:S(2)}, u32[]{:S(2)}) collective-permute-start(bf16[104,768]{1,0:T(8,128)(2,1)S(1)} %get-tuple-element.172), channel_id=1, source_target_pairs={{0,16},{4,20},{8,24},{12,28},{16,0},{20,4},{24,8},{28,12},{1,17},{... | collective-permute-start | bytes 479240 | tf_op jit(solution)/shard_map/ppermute | solution.py:418
  104.6 11.7 %collective-permute-start.32 = (bf16[104,768]{1,0:T(8,128)(2,1)S(1)}, bf16[104,768]{1,0:T(8,128)(2,1)S(1)}, u32[]{:S(2)}, u32[]{:S(2)}) collective-permute-start(bf16[104,768]{1,0:T(8,128)(2,1)S(1)} %get-tuple-element.173), channel_id=1, source_target_pairs={{0,24},{4,28},{8,16},{12,20},{16,8},{20,12},{24,0},{28,4},{1,25},{... | collective-permute-start | bytes 479240 | tf_op jit(solution)/shard_map/ppermute | solution.py:418
  (23 other events, 79.0 us)

commit v7 on v6

--- a/solution.py
+++ b/solution.py
@@ -444,10 +444,6 @@
     across = functools.partial(swap, axis="tensor", bit=2, size=4)
     dp = functools.partial(swap, axis="dp", size=n_dp)
 
-    def diagonal(values):
-        pairs = [(4 * d + t, 4 * (d ^ 1) + (t ^ 2)) for d in range(n_dp) for t in range(4)]
-        return lax.ppermute(values, ("dp", "tensor"), pairs)
-
     pin = lax.optimization_barrier
 
     def along(value, wait=None):
@@ -672,7 +668,7 @@
         (g_keep, g_core, b_keep, b_core, across(back), h, tokens, gain_one, gh),
     )
     if slots:
-        att_got, in_near[0], gains_x = pin((dp(att_send, bit=1), in_near[0], dp(gains, bit=1)))
+        att_got, in_near[-1], gains_x = pin((dp(att_send, bit=1), in_near[-1], dp(gains, bit=1)))
         in_parts = (in_parts[0], *in_near)
         *att_parts, gains = merge(att_keep, att_got, (gains, gains_x))
         att_parts = (att_parts[0], *(dp(att_parts[k], bit=2 * k) for k in range(1, slots)))

time: 118 us -> 117 us (level)
  starting transfers between devices: 41.5 us -> 39.1 us
  waiting for transfers between devices: 46 us -> 48.1 us
    ppermute x36, starting transfers between devices: 41.5 us -> 39.1 us  [swap(): return lax.ppermute(values, axis, [(i, i ^ bit) for i in range(size)])]
    ppermute x36, waiting for transfers between devices: 46 us -> 48.1 us  [swap(): return lax.ppermute(values, axis, [(i, i ^ bit) for i in range(size)])]
  transfers between devices with their start and end apart: 36 -> 36, of which waited for: 17 -> 18; matrix products, arithmetic and copies ran while one was open for 0% -> 0% of each run, Pallas kernels for 18% -> 18%
where the time goes in v7:
time: 117 us
  waiting for transfers between devices  48.1 us (41%)
  starting transfers between devices  39.1 us (33%)
  Pallas kernels  24.4 us (21%)
  local copies, waits for them, and re-layouts  3.97 us (3%)
    ppermute x36, waiting for transfers between devices, swap(): return lax.ppermute(values, axis, [(i, i ^ bit) for i in range(size)])  48.1 us
    ppermute x36, starting transfers between devices, swap(): return lax.ppermute(values, axis, [(i, i ^ bit) for i in range(size)])  39.1 us
    pallas_call x16, Pallas kernels, call(): pl.pallas_call(kernel, name=getattr(kernel, 'func', kernel).__name__, out...  24.4 us
    unnamed x23, local copies, waits for them, and re-layouts  3.8 us
  transfers between devices with their start and end apart: 36, of which 18 were waited for; matrix products, arithmetic and copies ran while one was open for 0% of the time, Pallas kernels for 18%

profile of v7, /device:TPU:0, one launch (start us, length us, event | category | flops | bytes accessed | tf_op | source)
XLA Modules:
  0.0 116.9 jit_solution(7663248541941188360)
XLA Ops:
  2.8 4.1 %collective-permute-start.1 = (bf16[96,768]{1,0:T(8,128)(2,1)S(1)}, bf16[96,768]{1,0:T(8,128)(2,1)S(1)}, u32[]{:S(2)}, u32[]{:S(2)}) collective-permute-start(bf16[96,768]{1,0:T(8,128)(2,1)S(1)} %pack_kernel.2.rest_0_), channel_id=1, source_target_pairs={{0,16},{4,20},{8,24},{12,28},{16,0},{20,4},{24,8},{28,12},{1,17},{... | collective-permute-start | bytes 442376 | tf_op jit(solution)/shard_map/ppermute | solution.py:418
  17.7 2.5 %collective-permute-done.2.rest_3_ = bf16[96,768]{1,0:T(8,128)(2,1)S(1)} collective-permute-done((bf16[96,768]{1,0:T(8,128)(2,1)S(1)}, bf16[96,768]{1,0:T(8,128)(2,1)S(1)}, u32[]{:S(2)}, u32[]{:S(2)}) %collective-permute-start.2) | collective-permute-done | bytes 147488 | tf_op jit(solution)/shard_map/ppermute | solution.py:418
  21.6 2.6 %collective-permute-start.10 = (bf16[96,864]{1,0:T(8,128)(2,1)S(1)}, bf16[96,864]{1,0:T(8,128)(2,1)S(1)}, u32[]{:S(2)}, u32[]{:S(2)}) collective-permute-start(bf16[96,864]{1,0:T(8,128)(2,1)S(1)} %pack_kernel.3.rest_0_), channel_id=1, source_target_pairs={{0,16},{4,20},{8,24},{12,28},{16,0},{20,4},{24,8},{28,12},{1,17},{... | collective-permute-start | bytes 497672 | tf_op jit(solution)/shard_map/ppermute | solution.py:418
  24.2 1.7 %collective-permute-start.9 = (bf16[96,864]{1,0:T(8,128)(2,1)S(1)}, bf16[96,864]{1,0:T(8,128)(2,1)S(1)}, u32[]{:S(2)}, u32[]{:S(2)}) collective-permute-start(bf16[96,864]{1,0:T(8,128)(2,1)S(1)} %pack_kernel.3.rest_0_), channel_id=1, source_target_pairs={{0,8},{4,12},{8,0},{12,4},{16,24},{20,28},{24,16},{28,20},{1,9},{5... | collective-permute-start | bytes 497672 | tf_op jit(solution)/shard_map/ppermute | solution.py:418
  27.5 2.0 %prepare_kernel.1 = (bf16[512,768]{1,0:T(8,128)(2,1)S(1)}, f32[512,128]{1,0:T(8,128)S(1)}, f32[512,128]{1,0:T(8,128)S(1)}) custom-call(s32[13]{0:T(128)S(1)} %concatenate.6.ids, bf16[128,768]{1,0:T(8,128)(2,1)S(1)} %copy-done, bf16[128,768]{1,0:T(8,128)(2,1)S(1)} %collective-permute-done.5.t1, bf16[128,768]{1,0:T(8,128)(2,1)S(1)} %collective-permute-done.7.t2, ...), custom_call_target="tpu_custom_call" | custom-call | flops 1 | bytes 1 | tf_op jit(solution)/shard_map/prepare_kernel/pallas_call | solution.py:30
  29.5 3.0 %collective-permute-done.10.rest_2_ = bf16[96,864]{1,0:T(8,128)(2,1)S(1)} collective-permute-done((bf16[96,864]{1,0:T(8,128)(2,1)S(1)}, bf16[96,864]{1,0:T(8,128)(2,1)S(1)}, u32[]{:S(2)}, u32[]{:S(2)}) %collective-permute-start.10) | collective-permute-done | bytes 165920 | tf_op jit(solution)/shard_map/ppermute | solution.py:418
  33.2 4.3 %attend_kernel.1 = (bf16[512,192]{1,0:T(8,128)(2,1)S(1)}, bf16[512,192]{1,0:T(8,128)(2,1)S(1)}, bf16[512,192]{1,0:T(8,128)(2,1)S(1)}, bf16[3,512,256]{2,1,0:T(8,...) custom-call(s32[13]{0:T(128)S(1)} %concatenate.6.ids, ...), custom_call_target="tpu_custom_call" | custom-call | flops 1 | bytes 1 | tf_op jit(solution)/shard_map/attend_kernel/pallas_call | solution.py:30
  38.0 1.7 %collective-permute-done.13 = bf16[256,768]{1,0:T(8,128)(2,1)S(1)} collective-permute-done((bf16[256,768]{1,0:T(8,128)(2,1)S(1)}, bf16[256,768]{1,0:T(8,128)(2,1)S(1)}, u32[]{:S(2)}, u32[]{:S(2)}) %collective-permute-start.13) | collective-permute-done | bytes 393248 | tf_op jit(solution)/shard_map/ppermute | solution.py:418
  39.8 1.8 %collective-permute-start.14 = (bf16[256,768]{1,0:T(8,128)(2,1)S(1)}, bf16[256,768]{1,0:T(8,128)(2,1)S(1)}, u32[]{:S(2)}, u32[]{:S(2)}) collective-permute-start(bf16[256,768]{1,0:T(8,128)(2,1)S(1)} %add_convert_fusion.1.own), channel_id=1, source_target_pairs={{0,2},{1,3},{2,0},{3,1},{4,6},{5,7},{6,4},{7,5},{8,10},{9,11},{10,... | collective-permute-start | bytes 1179656 | tf_op jit(solution)/shard_map/ppermute | solution.py:418
  42.0 9.0 %collective-permute-done.14.received = bf16[256,768]{1,0:T(8,128)(2,1)S(1)} collective-permute-done((bf16[256,768]{1,0:T(8,128)(2,1)S(1)}, bf16[256,768]{1,0:T(8,128)(2,1)S(1)}, u32[]{:S(2)}, u32[]{:S(2)}) %collective-permute-start.14) | collective-permute-done | bytes 393248 | tf_op jit(solution)/shard_map/ppermute | solution.py:418
  52.0 3.2 %collective-permute-done.18 = bf16[3,96,864]{2,1,0:T(8,128)(2,1)S(1)} collective-permute-done((bf16[3,96,864]{2,1,0:T(8,128)(2,1)S(1)}, bf16[3,96,864]{2,1,0:T(8,128)(2,1)S(1)}, u32[]{:S(2)}, u32[]{:S(2)}) %collective-permute-start.18) | collective-permute-done | bytes 497696 | tf_op jit(solution)/shard_map/ppermute | solution.py:418
  55.3 2.0 %units_far_kernel.1 = (bf16[256,768]{1,0:T(8,128)(2,1)S(1)}, bf16[256,576]{1,0:T(8,128)(2,1)S(1)}, bf16[256,288]{1,0:T(8,128)(2,1)S(1)}, bf16[768,576]{1,0:T(8,128)(2,1)S(1)}, bf16[768,288]{1,0:T(8,128)(2,1)S(1)}) custom-call(s32[13]{0:T(128)S(1)} %concatenate.6.ids, bf16[256,768]{1,0:T(8,128)(2,1)S(1)} %collective-permute-done.15.n2_far, ...), custom_call_target="tpu_custom_call" | custom-call | flops 1 | bytes 1 | tf_op jit(solution)/shard_map/units_far_kernel/pallas_call | solution.py:30
  59.6 2.3 %unit_grads_kernel.1 = (bf16[4,96,864]{2,1,0:T(8,128)(2,1)S(1)}, bf16[4,96,864]{2,1,0:T(8,128)(2,1)S(1)}, bf16[256,768]{1,0:T(8,128)(2,1)S(1)}, f32[256,768]{1,0:T(8,128)S(1)}) custom-call(s32[13]{0:T(128)S(1)} %concatenate.6.ids, bf16[256,768]{1,0:T(8,128)(2,1)S(1)} %get-tuple-element.126.n2, bf16[256,768]{1,0:T(8,128)(2,1)S(1)} %collective-permute-done.15.n2_far, ...), custom_call_target="tpu_custom_call" | custom-call | flops 1 | bytes 1 | tf_op jit(solution)/shard_map/unit_grads_kernel/pallas_call | solution.py:30
  61.9 1.8 %collective-permute-start.22 = (bf16[4,96,864]{2,1,0:T(8,128)(2,1)S(1)}, bf16[4,96,864]{2,1,0:T(8,128)(2,1)S(1)}, u32[]{:S(2)}, u32[]{:S(2)}) collective-permute-start(bf16[4,96,864]{2,1,0:T(8,128)(2,1)S(1)} %get-tuple-element.154), channel_id=1, source_target_pairs={{0,4},{4,0},{8,12},{12,8},{16,20},{20,16},{24,28},{28,24},{1,5},{5... | collective-permute-start | bytes 1990664 | tf_op jit(solution)/shard_map/ppermute | solution.py:418
  63.7 6.9 %collective-permute-done.20.received = bf16[256,768]{1,0:T(8,128)(2,1)S(1)} collective-permute-done((bf16[256,768]{1,0:T(8,128)(2,1)S(1)}, bf16[256,768]{1,0:T(8,128)(2,1)S(1)}, u32[]{:S(2)}, u32[]{:S(2)}) %collective-permute-start.20) | collective-permute-done | bytes 393248 | tf_op jit(solution)/shard_map/ppermute | solution.py:418
  73.0 5.4 %attend_back_kernel.1 = (bf16[512,576]{1,0:T(8,128)(2,1)S(1)}, bf16[256,768]{1,0:T(8,128)(2,1)S(1)}, f32[256,768]{1,0:T(8,128)S(1)}, f32[2,768]{1,0:T(2,128)S(1)}) custom-call(s32[13]{0:T(128)S(1)} %concatenate.6.ids, bf16[256,768]{1,0:T(8,128)(2,1)S(1)} %get-tuple-element.143.gy, bf16[256,768]{1,0:T(8,128)(2,1)S(1)} %collective-permute-done.21.gy_far, ...), custom_call_target="tpu_custom_call" | custom-call | flops 1 | bytes 1 | tf_op jit(solution)/shard_map/attend_back_kernel/pallas_call | solution.py:30
  81.0 1.7 %collective-permute-start.26 = (f32[2,768]{1,0:T(2,128)S(1)}, f32[2,768]{1,0:T(2,128)S(1)}, u32[]{:S(2)}, u32[]{:S(2)}) collective-permute-start(f32[2,768]{1,0:T(2,128)S(1)} %add.20), channel_id=1, source_target_pairs={{0,2},{1,3},{2,0},{3,1},{4,6},{5,7},{6,4},{7,5},{8,10},{9,11},{10,... | collective-permute-start | bytes 18440 | tf_op jit(solution)/shard_map/ppermute | solution.py:418
  82.7 1.7 %attend_grads_kernel.1 = (bf16[4,96,768]{2,1,0:T(8,128)(2,1)S(1)}, bf16[4,96,768]{2,1,0:T(8,128)(2,1)S(1)}) custom-call(s32[13]{0:T(128)S(1)} %concatenate.6.ids, bf16[512,768]{1,0:T(8,128)(2,1)S(1)} %get-tuple-element.112.n1, bf16[512,576]{1,0:T(8,128)(2,1)S(1)} %get-tuple-element.156.g_raw, bf16[256,768]{1,0:T(8,128)(2,1)S(1)} %get-tuple-element.143.gy, ...), custom_call_target="tpu_custom_call" | custom-call | flops 1 | bytes 1 | tf_op jit(solution)/shard_map/attend_grads_kernel/pallas_call | solution.py:30
  85.0 1.8 %collective-permute-start.33 = (bf16[256,768]{1,0:T(8,128)(2,1)S(1)}, bf16[256,768]{1,0:T(8,128)(2,1)S(1)}, u32[]{:S(2)}, u32[]{:S(2)}) collective-permute-start(bf16[256,768]{1,0:T(8,128)(2,1)S(1)} %pad_maximum_fusion.2), channel_id=1, source_target_pairs={{0,2},{1,3},{2,0},{3,1},{4,6},{5,7},{6,4},{7,5},{8,10},{9,11},{10,... | collective-permute-start | bytes 1179656 | tf_op jit(solution)/shard_map/ppermute | solution.py:418
  87.0 3.9 %collective-permute-start.24 = (bf16[96,864]{1,0:T(8,128)(2,1)S(1)}, bf16[96,864]{1,0:T(8,128)(2,1)S(1)}, u32[]{:S(2)}, u32[]{:S(2)}) collective-permute-start(bf16[96,864]{1,0:T(8,128)(2,1)S(1)} %get-tuple-element.163), channel_id=1, source_target_pairs={{0,24},{4,28},{8,16},{12,20},{16,8},{20,12},{24,0},{28,4},{1,25},{... | collective-permute-start | bytes 497672 | tf_op jit(solution)/shard_map/ppermute | solution.py:418
  91.6 4.6 %collective-permute-done.24.rest_2_ = bf16[96,864]{1,0:T(8,128)(2,1)S(1)} collective-permute-done((bf16[96,864]{1,0:T(8,128)(2,1)S(1)}, bf16[96,864]{1,0:T(8,128)(2,1)S(1)}, u32[]{:S(2)}, u32[]{:S(2)}) %collective-permute-start.24) | collective-permute-done | bytes 165920 | tf_op jit(solution)/shard_map/ppermute | solution.py:418
  96.2 1.9 %collective-permute-start.35 = (bf16[96,864]{1,0:T(8,128)(2,1)S(1)}, bf16[96,864]{1,0:T(8,128)(2,1)S(1)}, u32[]{:S(2)}, u32[]{:S(2)}) collective-permute-start(bf16[96,864]{1,0:T(8,128)(2,1)S(1)} %get-tuple-element.183), channel_id=1, source_target_pairs={{0,16},{4,20},{8,24},{12,28},{16,0},{20,4},{24,8},{28,12},{1,17},{... | collective-permute-start | bytes 497672 | tf_op jit(solution)/shard_map/ppermute | solution.py:418
  101.2 3.4 %collective-permute-start.31 = (bf16[104,768]{1,0:T(8,128)(2,1)S(1)}, bf16[104,768]{1,0:T(8,128)(2,1)S(1)}, u32[]{:S(2)}, u32[]{:S(2)}) collective-permute-start(bf16[104,768]{1,0:T(8,128)(2,1)S(1)} %get-tuple-element.172), channel_id=1, source_target_pairs={{0,16},{4,20},{8,24},{12,28},{16,0},{20,4},{24,8},{28,12},{1,17},{... | collective-permute-start | bytes 479240 | tf_op jit(solution)/shard_map/ppermute | solution.py:418
  108.3 7.8 %collective-permute-done.31.rest_1_ = bf16[104,768]{1,0:T(8,128)(2,1)S(1)} collective-permute-done((bf16[104,768]{1,0:T(8,128)(2,1)S(1)}, bf16[104,768]{1,0:T(8,128)(2,1)S(1)}, u32[]{:S(2)}, u32[]{:S(2)}) %collective-permute-start.31) | collective-permute-done | bytes 159776 | tf_op jit(solution)/shard_map/ppermute | solution.py:418
  (100 shorter events, 34.7 us)
Async XLA Ops:
  2.8 11.2 %collective-permute-start.1 = (bf16[96,768]{1,0:T(8,128)(2,1)S(1)}, bf16[96,768]{1,0:T(8,128)(2,1)S(1)}, u32[]{:S(2)}, u32[]{:S(2)}) collective-permute-start(bf16[96,768]{1,0:T(8,128)(2,1)S(1)} %pack_kernel.2.rest_0_), channel_id=1, source_target_pairs={{0,16},{4,20},{8,24},{12,28},{16,0},{20,4},{24,8},{28,12},{1,17},{... | collective-permute-start | bytes 442376 | tf_op jit(solution)/shard_map/ppermute | solution.py:418
  6.9 10.8 %collective-permute-start.5 = (bf16[128,768]{1,0:T(8,128)(2,1)S(1)}, bf16[128,768]{1,0:T(8,128)(2,1)S(1)}, u32[]{:S(2)}, u32[]{:S(2)}) collective-permute-start(bf16[128,768]{1,0:T(8,128)(2,1)S(1)} %copy-done), channel_id=1, source_target_pairs={{0,2},{1,3},{2,0},{3,1},{4,6},{5,7},{6,4},{7,5},{8,10},{9,11},{10,... | collective-permute-start | bytes 589832 | tf_op jit(solution)/shard_map/ppermute | solution.py:418
  8.9 8.8 %collective-permute-start.4 = (bf16[96,864]{1,0:T(8,128)(2,1)S(1)}, bf16[96,864]{1,0:T(8,128)(2,1)S(1)}, u32[]{:S(2)}, u32[]{:S(2)}) collective-permute-start(bf16[96,864]{1,0:T(8,128)(2,1)S(1)} %pack_kernel.3.rest_0_), channel_id=1, source_target_pairs={{0,4},{4,0},{8,12},{12,8},{16,20},{20,16},{24,28},{28,24},{1,5},{5... | collective-permute-start | bytes 497672 | tf_op jit(solution)/shard_map/ppermute | solution.py:418
  10.5 6.7 %collective-permute-start = (bf16[96,768]{1,0:T(8,128)(2,1)S(1)}, bf16[96,768]{1,0:T(8,128)(2,1)S(1)}, u32[]{:S(2)}, u32[]{:S(2)}) collective-permute-start(bf16[96,768]{1,0:T(8,128)(2,1)S(1)} %pack_kernel.2.rest_0_), channel_id=1, source_target_pairs={{0,8},{4,12},{8,0},{12,4},{16,24},{20,28},{24,16},{28,20},{1,9},{5... | collective-permute-start | bytes 442376 | tf_op jit(solution)/shard_map/ppermute | solution.py:418
  14.0 6.2 %collective-permute-start.2 = (bf16[96,768]{1,0:T(8,128)(2,1)S(1)}, bf16[96,768]{1,0:T(8,128)(2,1)S(1)}, u32[]{:S(2)}, u32[]{:S(2)}) collective-permute-start(bf16[96,768]{1,0:T(8,128)(2,1)S(1)} %collective-permute-done.1.rest_2_), channel_id=1, source_target_pairs={{0,8},{4,12},{8,0},{12,4},{16,24},{20,28},{24,16},{28,20},{1,9},{5... | collective-permute-start | bytes 442376 | tf_op jit(solution)/shard_map/ppermute | solution.py:418
  20.3 12.9 %collective-permute-start.6 = (bf16[3,96,768]{2,1,0:T(8,128)(2,1)S(1)}, bf16[3,96,768]{2,1,0:T(8,128)(2,1)S(1)}, u32[]{:S(2)}, u32[]{:S(2)}) collective-permute-start(bf16[3,96,768]{2,1,0:T(8,128)(2,1)S(1)} %pad_maximum_fusion.1), channel_id=1, source_target_pairs={{0,4},{4,0},{8,12},{12,8},{16,20},{20,16},{24,28},{28,24},{1,5},{5... | collective-permute-start | bytes 1327112 | tf_op jit(solution)/shard_map/ppermute | solution.py:418
  21.1 6.4 %collective-permute-start.8 = (bf16[128,768]{1,0:T(8,128)(2,1)S(1)}, bf16[128,768]{1,0:T(8,128)(2,1)S(1)}, u32[]{:S(2)}, u32[]{:S(2)}) collective-permute-start(bf16[128,768]{1,0:T(8,128)(2,1)S(1)} %collective-permute-done.5.t1), channel_id=1, source_target_pairs={{0,1},{1,0},{2,3},{3,2},{4,5},{5,4},{6,7},{7,6},{8,9},{9,8},{10,11... | collective-permute-start | bytes 589832 | tf_op jit(solution)/shard_map/ppermute | solution.py:418
  21.6 11.0 %collective-permute-start.10 = (bf16[96,864]{1,0:T(8,128)(2,1)S(1)}, bf16[96,864]{1,0:T(8,128)(2,1)S(1)}, u32[]{:S(2)}, u32[]{:S(2)}) collective-permute-start(bf16[96,864]{1,0:T(8,128)(2,1)S(1)} %pack_kernel.3.rest_0_), channel_id=1, source_target_pairs={{0,16},{4,20},{8,24},{12,28},{16,0},{20,4},{24,8},{28,12},{1,17},{... | collective-permute-start | bytes 497672 | tf_op jit(solution)/shard_map/ppermute | solution.py:418
  24.2 13.3 %collective-permute-start.9 = (bf16[96,864]{1,0:T(8,128)(2,1)S(1)}, bf16[96,864]{1,0:T(8,128)(2,1)S(1)}, u32[]{:S(2)}, u32[]{:S(2)}) collective-permute-start(bf16[96,864]{1,0:T(8,128)(2,1)S(1)} %pack_kernel.3.rest_0_), channel_id=1, source_target_pairs={{0,8},{4,12},{8,0},{12,4},{16,24},{20,28},{24,16},{28,20},{1,9},{5... | collective-permute-start | bytes 497672 | tf_op jit(solution)/shard_map/ppermute | solution.py:418
  26.0 11.6 %collective-permute-start.12 = (bf16[128,768]{1,0:T(8,128)(2,1)S(1)}, bf16[128,768]{1,0:T(8,128)(2,1)S(1)}, u32[]{:S(2)}, u32[]{:S(2)}) collective-permute-start(bf16[128,768]{1,0:T(8,128)(2,1)S(1)} %copy-done.1), channel_id=1, source_target_pairs={{0,2},{1,3},{2,0},{3,1},{4,6},{5,7},{6,4},{7,5},{8,10},{9,11},{10,... | collective-permute-start | bytes 589832 | tf_op jit(solution)/shard_map/ppermute | solution.py:418
  39.8 11.2 %collective-permute-start.14 = (bf16[256,768]{1,0:T(8,128)(2,1)S(1)}, bf16[256,768]{1,0:T(8,128)(2,1)S(1)}, u32[]{:S(2)}, u32[]{:S(2)}) collective-permute-start(bf16[256,768]{1,0:T(8,128)(2,1)S(1)} %add_convert_fusion.1.own), channel_id=1, source_target_pairs={{0,2},{1,3},{2,0},{3,1},{4,6},{5,7},{6,4},{7,5},{8,10},{9,11},{10,... | collective-permute-start | bytes 1179656 | tf_op jit(solution)/shard_map/ppermute | solution.py:418
  41.7 13.6 %collective-permute-start.18 = (bf16[3,96,864]{2,1,0:T(8,128)(2,1)S(1)}, bf16[3,96,864]{2,1,0:T(8,128)(2,1)S(1)}, u32[]{:S(2)}, u32[]{:S(2)}) collective-permute-start(bf16[3,96,864]{2,1,0:T(8,128)(2,1)S(1)} %pad_maximum_fusion), channel_id=1, source_target_pairs={{0,4},{4,0},{8,12},{12,8},{16,20},{20,16},{24,28},{28,24},{1,5},{5... | collective-permute-start | bytes 1493000 | tf_op jit(solution)/shard_map/ppermute | solution.py:418
  59.3 11.3 %collective-permute-start.20 = (bf16[256,768]{1,0:T(8,128)(2,1)S(1)}, bf16[256,768]{1,0:T(8,128)(2,1)S(1)}, u32[]{:S(2)}, u32[]{:S(2)}) collective-permute-start(bf16[256,768]{1,0:T(8,128)(2,1)S(1)} %add_convert_fusion.own), channel_id=1, source_target_pairs={{0,2},{1,3},{2,0},{3,1},{4,6},{5,7},{6,4},{7,5},{8,10},{9,11},{10,... | collective-permute-start | bytes 1179656 | tf_op jit(solution)/shard_map/ppermute | solution.py:418
  61.9 17.4 %collective-permute-start.22 = (bf16[4,96,864]{2,1,0:T(8,128)(2,1)S(1)}, bf16[4,96,864]{2,1,0:T(8,128)(2,1)S(1)}, u32[]{:S(2)}, u32[]{:S(2)}) collective-permute-start(bf16[4,96,864]{2,1,0:T(8,128)(2,1)S(1)} %get-tuple-element.154), channel_id=1, source_target_pairs={{0,4},{4,0},{8,12},{12,8},{16,20},{20,16},{24,28},{28,24},{1,5},{5... | collective-permute-start | bytes 1990664 | tf_op jit(solution)/shard_map/ppermute | solution.py:418
  71.2 13.6 %collective-permute-start.28 = (bf16[256,768]{1,0:T(8,128)(2,1)S(1)}, bf16[256,768]{1,0:T(8,128)(2,1)S(1)}, u32[]{:S(2)}, u32[]{:S(2)}) collective-permute-start(bf16[256,768]{1,0:T(8,128)(2,1)S(1)} %get-tuple-element.166), channel_id=1, source_target_pairs={{0,1},{1,0},{2,3},{3,2},{4,5},{5,4},{6,7},{7,6},{8,9},{9,8},{10,11... | collective-permute-start | bytes 1179656 | tf_op jit(solution)/shard_map/ppermute | solution.py:418
  84.5 15.3 %collective-permute-start.23 = (bf16[4,96,768]{2,1,0:T(8,128)(2,1)S(1)}, bf16[4,96,768]{2,1,0:T(8,128)(2,1)S(1)}, u32[]{:S(2)}, u32[]{:S(2)}) collective-permute-start(bf16[4,96,768]{2,1,0:T(8,128)(2,1)S(1)} %get-tuple-element.160), channel_id=1, source_target_pairs={{0,4},{4,0},{8,12},{12,8},{16,20},{20,16},{24,28},{28,24},{1,5},{5... | collective-permute-start | bytes 1769480 | tf_op jit(solution)/shard_map/ppermute | solution.py:418
  85.0 20.6 %collective-permute-start.33 = (bf16[256,768]{1,0:T(8,128)(2,1)S(1)}, bf16[256,768]{1,0:T(8,128)(2,1)S(1)}, u32[]{:S(2)}, u32[]{:S(2)}) collective-permute-start(bf16[256,768]{1,0:T(8,128)(2,1)S(1)} %pad_maximum_fusion.2), channel_id=1, source_target_pairs={{0,2},{1,3},{2,0},{3,1},{4,6},{5,7},{6,4},{7,5},{8,10},{9,11},{10,... | collective-permute-start | bytes 1179656 | tf_op jit(solution)/shard_map/ppermute | solution.py:418
  87.0 9.2 %collective-permute-start.24 = (bf16[96,864]{1,0:T(8,128)(2,1)S(1)}, bf16[96,864]{1,0:T(8,128)(2,1)S(1)}, u32[]{:S(2)}, u32[]{:S(2)}) collective-permute-start(bf16[96,864]{1,0:T(8,128)(2,1)S(1)} %get-tuple-element.163), channel_id=1, source_target_pairs={{0,24},{4,28},{8,16},{12,20},{16,8},{20,12},{24,0},{28,4},{1,25},{... | collective-permute-start | bytes 497672 | tf_op jit(solution)/shard_map/ppermute | solution.py:418
  90.9 13.7 %collective-permute-start.34 = (bf16[96,864]{1,0:T(8,128)(2,1)S(1)}, bf16[96,864]{1,0:T(8,128)(2,1)S(1)}, u32[]{:S(2)}, u32[]{:S(2)}) collective-permute-start(bf16[96,864]{1,0:T(8,128)(2,1)S(1)} %get-tuple-element.182), channel_id=1, source_target_pairs={{0,8},{4,12},{8,0},{12,4},{16,24},{20,28},{24,16},{28,20},{1,9},{5... | collective-permute-start | bytes 497672 | tf_op jit(solution)/shard_map/ppermute | solution.py:418
  90.9 8.8 %collective-permute-start.29 = (f32[2,768]{1,0:T(2,128)S(1)}, f32[2,768]{1,0:T(2,128)S(1)}, u32[]{:S(2)}, u32[]{:S(2)}) collective-permute-start(f32[2,768]{1,0:T(2,128)S(1)} %add.21.gains), channel_id=1, source_target_pairs={{0,4},{4,0},{8,12},{12,8},{16,20},{20,16},{24,28},{28,24},{1,5},{5... | collective-permute-start | bytes 18440 | tf_op jit(solution)/shard_map/ppermute | solution.py:418
  96.2 8.4 %collective-permute-start.35 = (bf16[96,864]{1,0:T(8,128)(2,1)S(1)}, bf16[96,864]{1,0:T(8,128)(2,1)S(1)}, u32[]{:S(2)}, u32[]{:S(2)}) collective-permute-start(bf16[96,864]{1,0:T(8,128)(2,1)S(1)} %get-tuple-element.183), channel_id=1, source_target_pairs={{0,16},{4,20},{8,24},{12,28},{16,0},{20,4},{24,8},{28,12},{1,17},{... | collective-permute-start | bytes 497672 | tf_op jit(solution)/shard_map/ppermute | solution.py:418
  99.9 8.4 %collective-permute-start.30 = (bf16[104,768]{1,0:T(8,128)(2,1)S(1)}, bf16[104,768]{1,0:T(8,128)(2,1)S(1)}, u32[]{:S(2)}, u32[]{:S(2)}) collective-permute-start(bf16[104,768]{1,0:T(8,128)(2,1)S(1)} %get-tuple-element.171), channel_id=1, source_target_pairs={{0,8},{4,12},{8,0},{12,4},{16,24},{20,28},{24,16},{28,20},{1,9},{5... | collective-permute-start | bytes 479240 | tf_op jit(solution)/shard_map/ppermute | solution.py:418
  101.2 14.8 %collective-permute-start.31 = (bf16[104,768]{1,0:T(8,128)(2,1)S(1)}, bf16[104,768]{1,0:T(8,128)(2,1)S(1)}, u32[]{:S(2)}, u32[]{:S(2)}) collective-permute-start(bf16[104,768]{1,0:T(8,128)(2,1)S(1)} %get-tuple-element.172), channel_id=1, source_target_pairs={{0,16},{4,20},{8,24},{12,28},{16,0},{20,4},{24,8},{28,12},{1,17},{... | collective-permute-start | bytes 479240 | tf_op jit(solution)/shard_map/ppermute | solution.py:418
  104.6 11.4 %collective-permute-start.32 = (bf16[104,768]{1,0:T(8,128)(2,1)S(1)}, bf16[104,768]{1,0:T(8,128)(2,1)S(1)}, u32[]{:S(2)}, u32[]{:S(2)}) collective-permute-start(bf16[104,768]{1,0:T(8,128)(2,1)S(1)} %get-tuple-element.173), channel_id=1, source_target_pairs={{0,24},{4,28},{8,16},{12,20},{16,8},{20,12},{24,0},{28,4},{1,25},{... | collective-permute-start | bytes 479240 | tf_op jit(solution)/shard_map/ppermute | solution.py:418
  (23 other events, 79.0 us)

commit v8 on v7

--- a/solution.py
+++ b/solution.py
@@ -91,11 +91,13 @@
     packed[...] = jnp.concatenate(parts + [tall[...].T], axis=1)
 
 
-def prepare_kernel(ids, t0, t1, t2, t3, gain, freq, n1, cosine, sine):
+def prepare_kernel(ids, t0, t1, t2, t3, gain, freq, n1, n1_turned, cosine, sine):
     gain_row = gain[...].astype(F32)
     for i, source in enumerate((t0, t1, t2, t3)):
         unit, _ = normed(source[...].astype(F32))
-        n1[rows_of(ids[i]), :] = (unit * gain_row).astype(BF)
+        rows = (unit * gain_row).astype(BF)
+        n1[rows_of(ids[i]), :] = rows
+        n1_turned[:, pl.ds(pl.multiple_of(ids[i] * WINDOW, WINDOW), WINDOW)] = rows.T
     start = jnp.int32(0)
     lane = lax.broadcasted_iota(jnp.int32, (WINDOW, 128), 1)
     sign = jnp.where(lane % HEAD_DIM < HEAD_DIM // 2, -1.0, 1.0)
@@ -341,9 +343,9 @@
     gains[1:2, :] = gain_two[...]
 
 
-def attend_grads_kernel(slots, rows, ids, n1, g_raw, gy, gy_far, att, send, keep, total):
+def attend_grads_kernel(slots, rows, ids, n1_turned, g_raw, gy, gy_far, att, send, keep, total):
     columns = g_raw.shape[1]
-    total[:, :columns] = dot(n1[...], g_raw[...], TN)
+    total[:, :columns] = dot(n1_turned[...], g_raw[...])
     near = jnp.concatenate([att[rows_of(ids[i]), :] for i in (0, 1)], axis=0)
     far = jnp.concatenate([att[rows_of(ids[i]), :] for i in (2, 3)], axis=0)
     total[:, columns:] = dot(gy[...], near, TN) + dot(gy_far[...], far, TN)
@@ -538,9 +540,14 @@
     )
     token_blocks = (tokens, tokens_across, core(tokens), core(tokens_across))
     qkv_far = qkv_side + aside(qkv_near)
-    n1, cosine, sine = call(
+    n1, n1_turned, cosine, sine = call(
         prepare_kernel,
-        (shape(total_rows, width), shape(total_rows, 128, dtype=F32), shape(total_rows, 128, dtype=F32)),
+        (
+            shape(total_rows, width),
+            shape(width, total_rows),
+            shape(total_rows, 128, dtype=F32),
+            shape(total_rows, 128, dtype=F32),
+        ),
         token_blocks + (gain_one, freq),
         (ids,),
     )
@@ -642,7 +649,7 @@
     att_send, att_keep = call(
         functools.partial(attend_grads_kernel, slots, shard),
         slot_shapes(4 * head_width),
-        (n1, g_raw, gy, gy_far, attended),
+        (n1_turned, g_raw, gy, gy_far, attended),
         (ids,),
         [pltpu.VMEM((width, 4 * head_width), F32)],
     )

time: 117 us -> 117 us (level)
  no operation moved by 1% of the time
where the time goes in v8:
time: 117 us
  waiting for transfers between devices  47.9 us (41%)
  starting transfers between devices  39.1 us (33%)
  Pallas kernels  24.6 us (21%)
  local copies, waits for them, and re-layouts  3.97 us (3%)
    ppermute x36, waiting for transfers between devices, swap(): return lax.ppermute(values, axis, [(i, i ^ bit) for i in range(size)])  47.9 us
    ppermute x36, starting transfers between devices, swap(): return lax.ppermute(values, axis, [(i, i ^ bit) for i in range(size)])  39.1 us
    pallas_call x16, Pallas kernels, call(): pl.pallas_call(kernel, name=getattr(kernel, 'func', kernel).__name__, out...  24.6 us
    unnamed x23, local copies, waits for them, and re-layouts  3.8 us
  transfers between devices with their start and end apart: 36, of which 18 were waited for; matrix products, arithmetic and copies ran while one was open for 0% of the time, Pallas kernels for 18%

profile of v8, /device:TPU:0, one launch (start us, length us, event | category | flops | bytes accessed | tf_op | source)
XLA Modules:
  0.0 116.9 jit_solution(10309103919689797203)
XLA Ops:
  2.8 4.1 %collective-permute-start.1 = (bf16[96,768]{1,0:T(8,128)(2,1)S(1)}, bf16[96,768]{1,0:T(8,128)(2,1)S(1)}, u32[]{:S(2)}, u32[]{:S(2)}) collective-permute-start(bf16[96,768]{1,0:T(8,128)(2,1)S(1)} %pack_kernel.2.rest_0_), channel_id=1, source_target_pairs={{0,16},{4,20},{8,24},{12,28},{16,0},{20,4},{24,8},{28,12},{1,17},{... | collective-permute-start | bytes 442376 | tf_op jit(solution)/shard_map/ppermute | solution.py:420
  17.7 2.5 %collective-permute-done.2.rest_3_ = bf16[96,768]{1,0:T(8,128)(2,1)S(1)} collective-permute-done((bf16[96,768]{1,0:T(8,128)(2,1)S(1)}, bf16[96,768]{1,0:T(8,128)(2,1)S(1)}, u32[]{:S(2)}, u32[]{:S(2)}) %collective-permute-start.2) | collective-permute-done | bytes 147488 | tf_op jit(solution)/shard_map/ppermute | solution.py:420
  21.6 2.6 %collective-permute-start.10 = (bf16[96,864]{1,0:T(8,128)(2,1)S(1)}, bf16[96,864]{1,0:T(8,128)(2,1)S(1)}, u32[]{:S(2)}, u32[]{:S(2)}) collective-permute-start(bf16[96,864]{1,0:T(8,128)(2,1)S(1)} %pack_kernel.3.rest_0_), channel_id=1, source_target_pairs={{0,16},{4,20},{8,24},{12,28},{16,0},{20,4},{24,8},{28,12},{1,17},{... | collective-permute-start | bytes 497672 | tf_op jit(solution)/shard_map/ppermute | solution.py:420
  24.2 1.7 %collective-permute-start.9 = (bf16[96,864]{1,0:T(8,128)(2,1)S(1)}, bf16[96,864]{1,0:T(8,128)(2,1)S(1)}, u32[]{:S(2)}, u32[]{:S(2)}) collective-permute-start(bf16[96,864]{1,0:T(8,128)(2,1)S(1)} %pack_kernel.3.rest_0_), channel_id=1, source_target_pairs={{0,8},{4,12},{8,0},{12,4},{16,24},{20,28},{24,16},{28,20},{1,9},{5... | collective-permute-start | bytes 497672 | tf_op jit(solution)/shard_map/ppermute | solution.py:420
  27.5 2.2 %prepare_kernel.1 = (bf16[512,768]{1,0:T(8,128)(2,1)S(1)}, bf16[768,512]{1,0:T(8,128)(2,1)S(1)}, f32[512,128]{1,0:T(8,128)S(1)}, f32[512,128]{1,0:T(8,128)S(1)}) custom-call(s32[13]{0:T(128)S(1)} %concatenate.6.ids, bf16[128,768]{1,0:T(8,128)(2,1)S(1)} %copy-done, bf16[128,768]{1,0:T(8,128)(2,1)S(1)} %collective-permute-done.5.t1, ...), custom_call_target="tpu_custom_call" | custom-call | flops 1 | bytes 1 | tf_op jit(solution)/shard_map/prepare_kernel/pallas_call | solution.py:30
  29.7 2.8 %collective-permute-done.10.rest_2_ = bf16[96,864]{1,0:T(8,128)(2,1)S(1)} collective-permute-done((bf16[96,864]{1,0:T(8,128)(2,1)S(1)}, bf16[96,864]{1,0:T(8,128)(2,1)S(1)}, u32[]{:S(2)}, u32[]{:S(2)}) %collective-permute-start.10) | collective-permute-done | bytes 165920 | tf_op jit(solution)/shard_map/ppermute | solution.py:420
  33.2 4.3 %attend_kernel.1 = (bf16[512,192]{1,0:T(8,128)(2,1)S(1)}, bf16[512,192]{1,0:T(8,128)(2,1)S(1)}, bf16[512,192]{1,0:T(8,128)(2,1)S(1)}, bf16[3,512,256]{2,1,0:T(8,...) custom-call(s32[13]{0:T(128)S(1)} %concatenate.6.ids, ...), custom_call_target="tpu_custom_call" | custom-call | flops 1 | bytes 1 | tf_op jit(solution)/shard_map/attend_kernel/pallas_call | solution.py:30
  38.0 1.7 %collective-permute-done.13 = bf16[256,768]{1,0:T(8,128)(2,1)S(1)} collective-permute-done((bf16[256,768]{1,0:T(8,128)(2,1)S(1)}, bf16[256,768]{1,0:T(8,128)(2,1)S(1)}, u32[]{:S(2)}, u32[]{:S(2)}) %collective-permute-start.13) | collective-permute-done | bytes 393248 | tf_op jit(solution)/shard_map/ppermute | solution.py:420
  39.8 1.8 %collective-permute-start.14 = (bf16[256,768]{1,0:T(8,128)(2,1)S(1)}, bf16[256,768]{1,0:T(8,128)(2,1)S(1)}, u32[]{:S(2)}, u32[]{:S(2)}) collective-permute-start(bf16[256,768]{1,0:T(8,128)(2,1)S(1)} %add_convert_fusion.1.own), channel_id=1, source_target_pairs={{0,2},{1,3},{2,0},{3,1},{4,6},{5,7},{6,4},{7,5},{8,10},{9,11},{10,... | collective-permute-start | bytes 1179656 | tf_op jit(solution)/shard_map/ppermute | solution.py:420
  42.0 9.0 %collective-permute-done.14.received = bf16[256,768]{1,0:T(8,128)(2,1)S(1)} collective-permute-done((bf16[256,768]{1,0:T(8,128)(2,1)S(1)}, bf16[256,768]{1,0:T(8,128)(2,1)S(1)}, u32[]{:S(2)}, u32[]{:S(2)}) %collective-permute-start.14) | collective-permute-done | bytes 393248 | tf_op jit(solution)/shard_map/ppermute | solution.py:420
  52.0 3.2 %collective-permute-done.18 = bf16[3,96,864]{2,1,0:T(8,128)(2,1)S(1)} collective-permute-done((bf16[3,96,864]{2,1,0:T(8,128)(2,1)S(1)}, bf16[3,96,864]{2,1,0:T(8,128)(2,1)S(1)}, u32[]{:S(2)}, u32[]{:S(2)}) %collective-permute-start.18) | collective-permute-done | bytes 497696 | tf_op jit(solution)/shard_map/ppermute | solution.py:420
  55.3 2.1 %units_far_kernel.1 = (bf16[256,768]{1,0:T(8,128)(2,1)S(1)}, bf16[256,576]{1,0:T(8,128)(2,1)S(1)}, bf16[256,288]{1,0:T(8,128)(2,1)S(1)}, bf16[768,576]{1,0:T(8,128)(2,1)S(1)}, bf16[768,288]{1,0:T(8,128)(2,1)S(1)}) custom-call(s32[13]{0:T(128)S(1)} %concatenate.6.ids, bf16[256,768]{1,0:T(8,128)(2,1)S(1)} %collective-permute-done.15.n2_far, ...), custom_call_target="tpu_custom_call" | custom-call | flops 1 | bytes 1 | tf_op jit(solution)/shard_map/units_far_kernel/pallas_call | solution.py:30
  59.6 2.3 %unit_grads_kernel.1 = (bf16[4,96,864]{2,1,0:T(8,128)(2,1)S(1)}, bf16[4,96,864]{2,1,0:T(8,128)(2,1)S(1)}, bf16[256,768]{1,0:T(8,128)(2,1)S(1)}, f32[256,768]{1,0:T(8,128)S(1)}) custom-call(s32[13]{0:T(128)S(1)} %concatenate.6.ids, bf16[256,768]{1,0:T(8,128)(2,1)S(1)} %get-tuple-element.127.n2, bf16[256,768]{1,0:T(8,128)(2,1)S(1)} %collective-permute-done.15.n2_far, ...), custom_call_target="tpu_custom_call" | custom-call | flops 1 | bytes 1 | tf_op jit(solution)/shard_map/unit_grads_kernel/pallas_call | solution.py:30
  61.9 1.8 %collective-permute-start.22 = (bf16[4,96,864]{2,1,0:T(8,128)(2,1)S(1)}, bf16[4,96,864]{2,1,0:T(8,128)(2,1)S(1)}, u32[]{:S(2)}, u32[]{:S(2)}) collective-permute-start(bf16[4,96,864]{2,1,0:T(8,128)(2,1)S(1)} %get-tuple-element.155), channel_id=1, source_target_pairs={{0,4},{4,0},{8,12},{12,8},{16,20},{20,16},{24,28},{28,24},{1,5},{5... | collective-permute-start | bytes 1990664 | tf_op jit(solution)/shard_map/ppermute | solution.py:420
  63.7 6.9 %collective-permute-done.20.received = bf16[256,768]{1,0:T(8,128)(2,1)S(1)} collective-permute-done((bf16[256,768]{1,0:T(8,128)(2,1)S(1)}, bf16[256,768]{1,0:T(8,128)(2,1)S(1)}, u32[]{:S(2)}, u32[]{:S(2)}) %collective-permute-start.20) | collective-permute-done | bytes 393248 | tf_op jit(solution)/shard_map/ppermute | solution.py:420
  72.9 5.4 %attend_back_kernel.1 = (bf16[512,576]{1,0:T(8,128)(2,1)S(1)}, bf16[256,768]{1,0:T(8,128)(2,1)S(1)}, f32[256,768]{1,0:T(8,128)S(1)}, f32[2,768]{1,0:T(2,128)S(1)}) custom-call(s32[13]{0:T(128)S(1)} %concatenate.6.ids, bf16[256,768]{1,0:T(8,128)(2,1)S(1)} %get-tuple-element.144.gy, bf16[256,768]{1,0:T(8,128)(2,1)S(1)} %collective-permute-done.21.gy_far, ...), custom_call_target="tpu_custom_call" | custom-call | flops 1 | bytes 1 | tf_op jit(solution)/shard_map/attend_back_kernel/pallas_call | solution.py:30
  81.0 1.7 %collective-permute-start.26 = (f32[2,768]{1,0:T(2,128)S(1)}, f32[2,768]{1,0:T(2,128)S(1)}, u32[]{:S(2)}, u32[]{:S(2)}) collective-permute-start(f32[2,768]{1,0:T(2,128)S(1)} %add.20), channel_id=1, source_target_pairs={{0,2},{1,3},{2,0},{3,1},{4,6},{5,7},{6,4},{7,5},{8,10},{9,11},{10,... | collective-permute-start | bytes 18440 | tf_op jit(solution)/shard_map/ppermute | solution.py:420
  82.7 1.7 %attend_grads_kernel.1 = (bf16[4,96,768]{2,1,0:T(8,128)(2,1)S(1)}, bf16[4,96,768]{2,1,0:T(8,128)(2,1)S(1)}) custom-call(s32[13]{0:T(128)S(1)} %concatenate.6.ids, bf16[768,512]{1,0:T(8,128)(2,1)S(1)} %get-tuple-element.157.n1_turned, bf16[512,576]{1,0:T(8,128)(2,1)S(1)} %get-tuple-element.158.g_raw, bf16[256,768]{1,0:T(8,128)(2,1)S(1)} %get-tuple-element.144.gy, ...), custom_call_target="tpu_custom_call" | custom-call | flops 1 | bytes 1 | tf_op jit(solution)/shard_map/attend_grads_kernel/pallas_call | solution.py:30
  85.0 1.8 %collective-permute-start.33 = (bf16[256,768]{1,0:T(8,128)(2,1)S(1)}, bf16[256,768]{1,0:T(8,128)(2,1)S(1)}, u32[]{:S(2)}, u32[]{:S(2)}) collective-permute-start(bf16[256,768]{1,0:T(8,128)(2,1)S(1)} %pad_maximum_fusion.2), channel_id=1, source_target_pairs={{0,2},{1,3},{2,0},{3,1},{4,6},{5,7},{6,4},{7,5},{8,10},{9,11},{10,... | collective-permute-start | bytes 1179656 | tf_op jit(solution)/shard_map/ppermute | solution.py:420
  86.9 4.0 %collective-permute-start.24 = (bf16[96,864]{1,0:T(8,128)(2,1)S(1)}, bf16[96,864]{1,0:T(8,128)(2,1)S(1)}, u32[]{:S(2)}, u32[]{:S(2)}) collective-permute-start(bf16[96,864]{1,0:T(8,128)(2,1)S(1)} %get-tuple-element.165), channel_id=1, source_target_pairs={{0,24},{4,28},{8,16},{12,20},{16,8},{20,12},{24,0},{28,4},{1,25},{... | collective-permute-start | bytes 497672 | tf_op jit(solution)/shard_map/ppermute | solution.py:420
  91.6 4.6 %collective-permute-done.24.rest_2_ = bf16[96,864]{1,0:T(8,128)(2,1)S(1)} collective-permute-done((bf16[96,864]{1,0:T(8,128)(2,1)S(1)}, bf16[96,864]{1,0:T(8,128)(2,1)S(1)}, u32[]{:S(2)}, u32[]{:S(2)}) %collective-permute-start.24) | collective-permute-done | bytes 165920 | tf_op jit(solution)/shard_map/ppermute | solution.py:420
  96.2 1.9 %collective-permute-start.35 = (bf16[96,864]{1,0:T(8,128)(2,1)S(1)}, bf16[96,864]{1,0:T(8,128)(2,1)S(1)}, u32[]{:S(2)}, u32[]{:S(2)}) collective-permute-start(bf16[96,864]{1,0:T(8,128)(2,1)S(1)} %get-tuple-element.185), channel_id=1, source_target_pairs={{0,16},{4,20},{8,24},{12,28},{16,0},{20,4},{24,8},{28,12},{1,17},{... | collective-permute-start | bytes 497672 | tf_op jit(solution)/shard_map/ppermute | solution.py:420
  101.2 3.4 %collective-permute-start.31 = (bf16[104,768]{1,0:T(8,128)(2,1)S(1)}, bf16[104,768]{1,0:T(8,128)(2,1)S(1)}, u32[]{:S(2)}, u32[]{:S(2)}) collective-permute-start(bf16[104,768]{1,0:T(8,128)(2,1)S(1)} %get-tuple-element.174), channel_id=1, source_target_pairs={{0,16},{4,20},{8,24},{12,28},{16,0},{20,4},{24,8},{28,12},{1,17},{... | collective-permute-start | bytes 479240 | tf_op jit(solution)/shard_map/ppermute | solution.py:420
  108.3 7.8 %collective-permute-done.31.rest_1_ = bf16[104,768]{1,0:T(8,128)(2,1)S(1)} collective-permute-done((bf16[104,768]{1,0:T(8,128)(2,1)S(1)}, bf16[104,768]{1,0:T(8,128)(2,1)S(1)}, u32[]{:S(2)}, u32[]{:S(2)}) %collective-permute-start.31) | collective-permute-done | bytes 159776 | tf_op jit(solution)/shard_map/ppermute | solution.py:420
  (100 shorter events, 34.7 us)
Async XLA Ops:
  2.8 11.2 %collective-permute-start.1 = (bf16[96,768]{1,0:T(8,128)(2,1)S(1)}, bf16[96,768]{1,0:T(8,128)(2,1)S(1)}, u32[]{:S(2)}, u32[]{:S(2)}) collective-permute-start(bf16[96,768]{1,0:T(8,128)(2,1)S(1)} %pack_kernel.2.rest_0_), channel_id=1, source_target_pairs={{0,16},{4,20},{8,24},{12,28},{16,0},{20,4},{24,8},{28,12},{1,17},{... | collective-permute-start | bytes 442376 | tf_op jit(solution)/shard_map/ppermute | solution.py:420
  6.9 10.8 %collective-permute-start.5 = (bf16[128,768]{1,0:T(8,128)(2,1)S(1)}, bf16[128,768]{1,0:T(8,128)(2,1)S(1)}, u32[]{:S(2)}, u32[]{:S(2)}) collective-permute-start(bf16[128,768]{1,0:T(8,128)(2,1)S(1)} %copy-done), channel_id=1, source_target_pairs={{0,2},{1,3},{2,0},{3,1},{4,6},{5,7},{6,4},{7,5},{8,10},{9,11},{10,... | collective-permute-start | bytes 589832 | tf_op jit(solution)/shard_map/ppermute | solution.py:420
  8.9 8.8 %collective-permute-start.4 = (bf16[96,864]{1,0:T(8,128)(2,1)S(1)}, bf16[96,864]{1,0:T(8,128)(2,1)S(1)}, u32[]{:S(2)}, u32[]{:S(2)}) collective-permute-start(bf16[96,864]{1,0:T(8,128)(2,1)S(1)} %pack_kernel.3.rest_0_), channel_id=1, source_target_pairs={{0,4},{4,0},{8,12},{12,8},{16,20},{20,16},{24,28},{28,24},{1,5},{5... | collective-permute-start | bytes 497672 | tf_op jit(solution)/shard_map/ppermute | solution.py:420
  10.5 6.7 %collective-permute-start = (bf16[96,768]{1,0:T(8,128)(2,1)S(1)}, bf16[96,768]{1,0:T(8,128)(2,1)S(1)}, u32[]{:S(2)}, u32[]{:S(2)}) collective-permute-start(bf16[96,768]{1,0:T(8,128)(2,1)S(1)} %pack_kernel.2.rest_0_), channel_id=1, source_target_pairs={{0,8},{4,12},{8,0},{12,4},{16,24},{20,28},{24,16},{28,20},{1,9},{5... | collective-permute-start | bytes 442376 | tf_op jit(solution)/shard_map/ppermute | solution.py:420
  14.0 6.2 %collective-permute-start.2 = (bf16[96,768]{1,0:T(8,128)(2,1)S(1)}, bf16[96,768]{1,0:T(8,128)(2,1)S(1)}, u32[]{:S(2)}, u32[]{:S(2)}) collective-permute-start(bf16[96,768]{1,0:T(8,128)(2,1)S(1)} %collective-permute-done.1.rest_2_), channel_id=1, source_target_pairs={{0,8},{4,12},{8,0},{12,4},{16,24},{20,28},{24,16},{28,20},{1,9},{5... | collective-permute-start | bytes 442376 | tf_op jit(solution)/shard_map/ppermute | solution.py:420
  20.3 12.9 %collective-permute-start.6 = (bf16[3,96,768]{2,1,0:T(8,128)(2,1)S(1)}, bf16[3,96,768]{2,1,0:T(8,128)(2,1)S(1)}, u32[]{:S(2)}, u32[]{:S(2)}) collective-permute-start(bf16[3,96,768]{2,1,0:T(8,128)(2,1)S(1)} %pad_maximum_fusion.1), channel_id=1, source_target_pairs={{0,4},{4,0},{8,12},{12,8},{16,20},{20,16},{24,28},{28,24},{1,5},{5... | collective-permute-start | bytes 1327112 | tf_op jit(solution)/shard_map/ppermute | solution.py:420
  21.1 6.4 %collective-permute-start.8 = (bf16[128,768]{1,0:T(8,128)(2,1)S(1)}, bf16[128,768]{1,0:T(8,128)(2,1)S(1)}, u32[]{:S(2)}, u32[]{:S(2)}) collective-permute-start(bf16[128,768]{1,0:T(8,128)(2,1)S(1)} %collective-permute-done.5.t1), channel_id=1, source_target_pairs={{0,1},{1,0},{2,3},{3,2},{4,5},{5,4},{6,7},{7,6},{8,9},{9,8},{10,11... | collective-permute-start | bytes 589832 | tf_op jit(solution)/shard_map/ppermute | solution.py:420
  21.6 11.0 %collective-permute-start.10 = (bf16[96,864]{1,0:T(8,128)(2,1)S(1)}, bf16[96,864]{1,0:T(8,128)(2,1)S(1)}, u32[]{:S(2)}, u32[]{:S(2)}) collective-permute-start(bf16[96,864]{1,0:T(8,128)(2,1)S(1)} %pack_kernel.3.rest_0_), channel_id=1, source_target_pairs={{0,16},{4,20},{8,24},{12,28},{16,0},{20,4},{24,8},{28,12},{1,17},{... | collective-permute-start | bytes 497672 | tf_op jit(solution)/shard_map/ppermute | solution.py:420
  24.2 13.3 %collective-permute-start.9 = (bf16[96,864]{1,0:T(8,128)(2,1)S(1)}, bf16[96,864]{1,0:T(8,128)(2,1)S(1)}, u32[]{:S(2)}, u32[]{:S(2)}) collective-permute-start(bf16[96,864]{1,0:T(8,128)(2,1)S(1)} %pack_kernel.3.rest_0_), channel_id=1, source_target_pairs={{0,8},{4,12},{8,0},{12,4},{16,24},{20,28},{24,16},{28,20},{1,9},{5... | collective-permute-start | bytes 497672 | tf_op jit(solution)/shard_map/ppermute | solution.py:420
  26.0 11.6 %collective-permute-start.12 = (bf16[128,768]{1,0:T(8,128)(2,1)S(1)}, bf16[128,768]{1,0:T(8,128)(2,1)S(1)}, u32[]{:S(2)}, u32[]{:S(2)}) collective-permute-start(bf16[128,768]{1,0:T(8,128)(2,1)S(1)} %copy-done.1), channel_id=1, source_target_pairs={{0,2},{1,3},{2,0},{3,1},{4,6},{5,7},{6,4},{7,5},{8,10},{9,11},{10,... | collective-permute-start | bytes 589832 | tf_op jit(solution)/shard_map/ppermute | solution.py:420
  39.8 11.2 %collective-permute-start.14 = (bf16[256,768]{1,0:T(8,128)(2,1)S(1)}, bf16[256,768]{1,0:T(8,128)(2,1)S(1)}, u32[]{:S(2)}, u32[]{:S(2)}) collective-permute-start(bf16[256,768]{1,0:T(8,128)(2,1)S(1)} %add_convert_fusion.1.own), channel_id=1, source_target_pairs={{0,2},{1,3},{2,0},{3,1},{4,6},{5,7},{6,4},{7,5},{8,10},{9,11},{10,... | collective-permute-start | bytes 1179656 | tf_op jit(solution)/shard_map/ppermute | solution.py:420
  41.7 13.6 %collective-permute-start.18 = (bf16[3,96,864]{2,1,0:T(8,128)(2,1)S(1)}, bf16[3,96,864]{2,1,0:T(8,128)(2,1)S(1)}, u32[]{:S(2)}, u32[]{:S(2)}) collective-permute-start(bf16[3,96,864]{2,1,0:T(8,128)(2,1)S(1)} %pad_maximum_fusion), channel_id=1, source_target_pairs={{0,4},{4,0},{8,12},{12,8},{16,20},{20,16},{24,28},{28,24},{1,5},{5... | collective-permute-start | bytes 1493000 | tf_op jit(solution)/shard_map/ppermute | solution.py:420
  59.2 11.3 %collective-permute-start.20 = (bf16[256,768]{1,0:T(8,128)(2,1)S(1)}, bf16[256,768]{1,0:T(8,128)(2,1)S(1)}, u32[]{:S(2)}, u32[]{:S(2)}) collective-permute-start(bf16[256,768]{1,0:T(8,128)(2,1)S(1)} %add_convert_fusion.own), channel_id=1, source_target_pairs={{0,2},{1,3},{2,0},{3,1},{4,6},{5,7},{6,4},{7,5},{8,10},{9,11},{10,... | collective-permute-start | bytes 1179656 | tf_op jit(solution)/shard_map/ppermute | solution.py:420
  61.9 17.4 %collective-permute-start.22 = (bf16[4,96,864]{2,1,0:T(8,128)(2,1)S(1)}, bf16[4,96,864]{2,1,0:T(8,128)(2,1)S(1)}, u32[]{:S(2)}, u32[]{:S(2)}) collective-permute-start(bf16[4,96,864]{2,1,0:T(8,128)(2,1)S(1)} %get-tuple-element.155), channel_id=1, source_target_pairs={{0,4},{4,0},{8,12},{12,8},{16,20},{20,16},{24,28},{28,24},{1,5},{5... | collective-permute-start | bytes 1990664 | tf_op jit(solution)/shard_map/ppermute | solution.py:420
  71.2 13.6 %collective-permute-start.28 = (bf16[256,768]{1,0:T(8,128)(2,1)S(1)}, bf16[256,768]{1,0:T(8,128)(2,1)S(1)}, u32[]{:S(2)}, u32[]{:S(2)}) collective-permute-start(bf16[256,768]{1,0:T(8,128)(2,1)S(1)} %get-tuple-element.168), channel_id=1, source_target_pairs={{0,1},{1,0},{2,3},{3,2},{4,5},{5,4},{6,7},{7,6},{8,9},{9,8},{10,11... | collective-permute-start | bytes 1179656 | tf_op jit(solution)/shard_map/ppermute | solution.py:420
  84.4 15.3 %collective-permute-start.23 = (bf16[4,96,768]{2,1,0:T(8,128)(2,1)S(1)}, bf16[4,96,768]{2,1,0:T(8,128)(2,1)S(1)}, u32[]{:S(2)}, u32[]{:S(2)}) collective-permute-start(bf16[4,96,768]{2,1,0:T(8,128)(2,1)S(1)} %get-tuple-element.162), channel_id=1, source_target_pairs={{0,4},{4,0},{8,12},{12,8},{16,20},{20,16},{24,28},{28,24},{1,5},{5... | collective-permute-start | bytes 1769480 | tf_op jit(solution)/shard_map/ppermute | solution.py:420
  85.0 20.6 %collective-permute-start.33 = (bf16[256,768]{1,0:T(8,128)(2,1)S(1)}, bf16[256,768]{1,0:T(8,128)(2,1)S(1)}, u32[]{:S(2)}, u32[]{:S(2)}) collective-permute-start(bf16[256,768]{1,0:T(8,128)(2,1)S(1)} %pad_maximum_fusion.2), channel_id=1, source_target_pairs={{0,2},{1,3},{2,0},{3,1},{4,6},{5,7},{6,4},{7,5},{8,10},{9,11},{10,... | collective-permute-start | bytes 1179656 | tf_op jit(solution)/shard_map/ppermute | solution.py:420
  86.9 9.2 %collective-permute-start.24 = (bf16[96,864]{1,0:T(8,128)(2,1)S(1)}, bf16[96,864]{1,0:T(8,128)(2,1)S(1)}, u32[]{:S(2)}, u32[]{:S(2)}) collective-permute-start(bf16[96,864]{1,0:T(8,128)(2,1)S(1)} %get-tuple-element.165), channel_id=1, source_target_pairs={{0,24},{4,28},{8,16},{12,20},{16,8},{20,12},{24,0},{28,4},{1,25},{... | collective-permute-start | bytes 497672 | tf_op jit(solution)/shard_map/ppermute | solution.py:420
  90.9 13.7 %collective-permute-start.34 = (bf16[96,864]{1,0:T(8,128)(2,1)S(1)}, bf16[96,864]{1,0:T(8,128)(2,1)S(1)}, u32[]{:S(2)}, u32[]{:S(2)}) collective-permute-start(bf16[96,864]{1,0:T(8,128)(2,1)S(1)} %get-tuple-element.184), channel_id=1, source_target_pairs={{0,8},{4,12},{8,0},{12,4},{16,24},{20,28},{24,16},{28,20},{1,9},{5... | collective-permute-start | bytes 497672 | tf_op jit(solution)/shard_map/ppermute | solution.py:420
  90.9 8.8 %collective-permute-start.29 = (f32[2,768]{1,0:T(2,128)S(1)}, f32[2,768]{1,0:T(2,128)S(1)}, u32[]{:S(2)}, u32[]{:S(2)}) collective-permute-start(f32[2,768]{1,0:T(2,128)S(1)} %add.21.gains), channel_id=1, source_target_pairs={{0,4},{4,0},{8,12},{12,8},{16,20},{20,16},{24,28},{28,24},{1,5},{5... | collective-permute-start | bytes 18440 | tf_op jit(solution)/shard_map/ppermute | solution.py:420
  96.2 8.4 %collective-permute-start.35 = (bf16[96,864]{1,0:T(8,128)(2,1)S(1)}, bf16[96,864]{1,0:T(8,128)(2,1)S(1)}, u32[]{:S(2)}, u32[]{:S(2)}) collective-permute-start(bf16[96,864]{1,0:T(8,128)(2,1)S(1)} %get-tuple-element.185), channel_id=1, source_target_pairs={{0,16},{4,20},{8,24},{12,28},{16,0},{20,4},{24,8},{28,12},{1,17},{... | collective-permute-start | bytes 497672 | tf_op jit(solution)/shard_map/ppermute | solution.py:420
  99.9 8.4 %collective-permute-start.30 = (bf16[104,768]{1,0:T(8,128)(2,1)S(1)}, bf16[104,768]{1,0:T(8,128)(2,1)S(1)}, u32[]{:S(2)}, u32[]{:S(2)}) collective-permute-start(bf16[104,768]{1,0:T(8,128)(2,1)S(1)} %get-tuple-element.173), channel_id=1, source_target_pairs={{0,8},{4,12},{8,0},{12,4},{16,24},{20,28},{24,16},{28,20},{1,9},{5... | collective-permute-start | bytes 479240 | tf_op jit(solution)/shard_map/ppermute | solution.py:420
  101.2 14.8 %collective-permute-start.31 = (bf16[104,768]{1,0:T(8,128)(2,1)S(1)}, bf16[104,768]{1,0:T(8,128)(2,1)S(1)}, u32[]{:S(2)}, u32[]{:S(2)}) collective-permute-start(bf16[104,768]{1,0:T(8,128)(2,1)S(1)} %get-tuple-element.174), channel_id=1, source_target_pairs={{0,16},{4,20},{8,24},{12,28},{16,0},{20,4},{24,8},{28,12},{1,17},{... | collective-permute-start | bytes 479240 | tf_op jit(solution)/shard_map/ppermute | solution.py:420
  104.6 11.4 %collective-permute-start.32 = (bf16[104,768]{1,0:T(8,128)(2,1)S(1)}, bf16[104,768]{1,0:T(8,128)(2,1)S(1)}, u32[]{:S(2)}, u32[]{:S(2)}) collective-permute-start(bf16[104,768]{1,0:T(8,128)(2,1)S(1)} %get-tuple-element.175), channel_id=1, source_target_pairs={{0,24},{4,28},{8,16},{12,20},{16,8},{20,12},{24,0},{28,4},{1,25},{... | collective-permute-start | bytes 479240 | tf_op jit(solution)/shard_map/ppermute | solution.py:420
  (23 other events, 78.9 us)
